TPU v7x, 768 devices: a whole 4x8x12 slice. The times are simulated.
768 devices in a mesh: blk: 96 (over z_hi, x, y), grp: 8 (over z_lo, core).
Axes of the slice: x: 4, y: 8, z: 12 (z_hi: 3, z_lo: 4; z = z_hi * 4 + z_lo), core: 2. Of those that a mesh axis runs over, the one named last changes fastest.
Arguments:
- frequency_features: bfloat16 [98304, 1024], P(('blk', 'grp')), may hold values from -0.1875 to 0.1875
- sentence_features: bfloat16 [98304, 1024], P(('blk', 'grp')), may hold values from -0.1875 to 0.1875
- score_multiplier: float32 [1], replicated, may hold values from 4 to 20
- score_offset_term: float32 [1], replicated, may hold values from -4 to -1
Outputs:
- picture_derivatives: bfloat16 [98304, 1024], P(('blk', 'grp'))
- sentence_derivatives: bfloat16 [98304, 1024], P(('blk', 'grp'))
All inputs are finite; a program needn't handle non-finite values.
Results may differ from a plain program's by a relative error of at most 0.012.
Values may be sent and summed in bfloat16 or wider, within the bound.
No kernel may reach another device: no remote copies, remote signals or barrier semaphores. Data moves between devices by JAX's collectives and lax.ppermute only.
A program may use at most 32 MiB of HBM per device.

v0:
```python
import jax
import jax.numpy as jnp
from jax import lax
from jax.sharding import PartitionSpec as P


def passed_along(block, axis, distance):
    devices = range(lax.axis_size(axis))
    route = [((i - distance) % len(devices), i) for i in devices]
    return lax.ppermute(block, axis, route)


def body(frequency_features, sentence_features, score_multiplier, score_offset_term):
    row_count = frequency_features.shape[0]
    reciprocal_warmth = score_multiplier[0]
    tile_stride_amount = score_offset_term[0]
    local_block_index = lax.all_gather(sentence_features, "grp", axis=0, tiled=True)
    block_rows = local_block_index.shape[0]
    member = lax.axis_index("grp")
    columns = lax.broadcasted_iota(jnp.int32, (row_count, block_rows), 1)
    positions = lax.broadcasted_iota(jnp.int32, (row_count, block_rows), 0)
    diagonal = columns == member * row_count + positions

    def contrast(text_block, labels):
        pair_scores = lax.dot_general(
            frequency_features,
            text_block,
            (((1,), (1,)), ((), ())),
            preferred_element_type=jnp.float32,
        )
        pair_scores = pair_scores * reciprocal_warmth + tile_stride_amount
        slopes = (-labels * jax.nn.sigmoid(-labels * pair_scores)).astype(jnp.bfloat16)
        image_part = jnp.dot(slopes, text_block, preferred_element_type=jnp.float32)
        text_part = lax.dot_general(
            slopes, frequency_features, (((0,), (0,)), ((), ())), preferred_element_type=jnp.float32
        )
        return (image_part, text_part.astype(jnp.bfloat16))

    own_labels = jnp.where(diagonal, 1.0, -1.0).astype(jnp.float32)
    picture_count, own_part = contrast(local_block_index, own_labels)
    far_labels = jnp.float32(-1.0)
    sentence_count = own_part.astype(jnp.float32)
    text_block = passed_along(local_block_index, "blk", -1)
    image_part, text_part = contrast(text_block, far_labels)
    picture_count = picture_count + image_part
    returned = passed_along(text_part, "blk", 1)
    sentence_count = sentence_count + returned.astype(jnp.float32)
    sentence_lines = lax.psum_scatter(sentence_count, "grp", scatter_dimension=0, tiled=True)
    picture_derivatives = (reciprocal_warmth * picture_count).astype(jnp.bfloat16)
    sentence_derivatives = (reciprocal_warmth * sentence_lines).astype(jnp.bfloat16)
    return (picture_derivatives, sentence_derivatives)


def solution(mesh):
    in_specs = (P(("blk", "grp"), None), P(("blk", "grp"), None), P(), P())
    out_specs = (P(("blk", "grp"), None), P(("blk", "grp"), None))
    return jax.shard_map(body, mesh=mesh, in_specs=in_specs, out_specs=out_specs, check_vma=False)
```

profile of v0, /device:TPU:1, one launch (start us, length us, event | category | flops | bytes accessed | tf_op | source)
XLA Modules:
  0.0 434.3 jit_solution(7122215442897287057)
XLA Ops:
  7.2 0.0 copy-start
  7.2 0.0 all-gather.2.cloned.1.call-start
  7.2 0.7 all-gather.2.cloned.1.call-update
  7.9 0.0 reduce-scatter.2.cloned.1.call-start
  8.0 53.6 %all-gather.2.cloned.1.call-done = bf16[1024,1024]{1,0:T(8,128)(2,1)} async-done(((bf16[128,1024]{1,0:T(8,128)(2,1)}), bf16[1024,1024]{1,0:T(8,128)(2,1)}) %all-gather.2.cloned.1.call-update) | async-done | bytes 2097168 | tf_op jit(solution)/shard_map/all_gather | solution.py:17
  61.5 10.6 %collective-permute-start = (bf16[1024,1024]{1,0:T(8,128)(2,1)}, bf16[1024,1024]{1,0:T(8,128)(2,1)S(1)}, u32[]{:S(2)}, u32[]{:S(2)}) collective-permute-start(bf16[1024,1024]{1,0:T(8,128)(2,1)} %all-gather.2.cloned.1.call-done), channel_id=1, source_target_pairs={{8,0},{16,8},{24,16},{32,24},{40,32},{48,40},{56,48},{64,56},{72,6... | collective-permute-start | bytes 6291464 | tf_op jit(solution)/shard_map/ppermute | solution.py:10
  73.4 166.9 %collective-permute-done = bf16[1024,1024]{1,0:T(8,128)(2,1)S(1)} collective-permute-done((bf16[1024,1024]{1,0:T(8,128)(2,1)}, bf16[1024,1024]{1,0:T(8,128)(2,1)S(1)}, u32[]{:S(2)}, u32[]{:S(2)}) %collective-permute-start) | collective-permute-done | bytes 2097184 | tf_op jit(solution)/shard_map/ppermute | solution.py:10
  240.3 0.0 copy-start.2
  240.3 0.0 copy-done
  240.3 0.9 fusion.13
  241.2 0.4 copy-done.2
  241.6 0.7 convolution_convert_fusion
  242.3 1.9 collective-permute-start.1
  244.3 2.5 fusion.14
  246.8 125.5 %collective-permute-done.1 = bf16[1024,1024]{1,0:T(8,128)(2,1)} collective-permute-done((bf16[1024,1024]{1,0:T(8,128)(2,1)S(1)}, bf16[1024,1024]{1,0:T(8,128)(2,1)}, u32[]{:S(2)}, u32[]{:S(2)}) %collective-permute-start.1) | collective-permute-done | bytes 2097184 | tf_op jit(solution)/shard_map/ppermute | solution.py:10
  372.3 4.3 convert_add_fusion
  376.6 0.0 copy-start.1
  376.6 0.0 reduce-scatter.2.cloned.1.call-update
  376.6 1.6 copy-done.1
  378.2 0.0 copy-start.3
  378.2 0.4 fusion.16
  378.6 1.1 copy-done.3
  379.8 1.2 fusion.15
  380.9 44.7 %reduce-scatter.2.cloned.1.call-done = f32[128,1024]{1,0:T(8,128)} async-done(((f32[1024,1024]{1,0:T(8,128)}), f32[128,1024]{1,0:T(8,128)}) %reduce-scatter.2.cloned.1.call-update) | async-done | bytes 524304 | tf_op jit(solution)/shard_map/reduce_scatter | solution.py:48
  425.7 1.8 multiply_convert_fusion
  (1 shorter events, 0.0 us)
Async XLA Ops:
  7.2 233.1 %copy-start = (bf16[128,1024]{1,0:T(8,128)(2,1)S(1)}, bf16[128,1024]{1,0:T(8,128)(2,1)}, u32[]{:S(2)}) copy-start(bf16[128,1024]{1,0:T(8,128)(2,1)} %param.4) | copy-start | bytes 786436
  7.2 54.4 %all-gather.2.cloned.1.call-start = ((), (), s32[]{:S(2)}) async-start(), calls=%async_computation.1 | async-start | bytes 2359296 | tf_op jit(solution)/shard_map/all_gather | solution.py:17
  7.9 417.8 %reduce-scatter.2.cloned.1.call-start = ((), (), s32[]{:S(2)}) async-start(), calls=%async_computation.2 | async-start | bytes 4718592 | tf_op jit(solution)/shard_map/reduce_scatter | solution.py:48
  61.5 178.7 %collective-permute-start = (bf16[1024,1024]{1,0:T(8,128)(2,1)}, bf16[1024,1024]{1,0:T(8,128)(2,1)S(1)}, u32[]{:S(2)}, u32[]{:S(2)}) collective-permute-start(bf16[1024,1024]{1,0:T(8,128)(2,1)} %all-gather.2.cloned.1.call-done), channel_id=1, source_target_pairs={{8,0},{16,8},{24,16},{32,24},{40,32},{48,40},{56,48},{64,56},{72,6... | collective-permute-start | bytes 6291464 | tf_op jit(solution)/shard_map/ppermute | solution.py:10
  240.3 1.3 copy-start.2
  242.3 130.0 %collective-permute-start.1 = (bf16[1024,1024]{1,0:T(8,128)(2,1)S(1)}, bf16[1024,1024]{1,0:T(8,128)(2,1)}, u32[]{:S(2)}, u32[]{:S(2)}) collective-permute-start(bf16[1024,1024]{1,0:T(8,128)(2,1)S(1)} %convolution_convert_fusion), channel_id=1, source_target_pairs={{760,0},{0,8},{8,16},{16,24},{24,32},{32,40},{40,48},{48,56},{56,6... | collective-permute-start | bytes 6291464 | tf_op jit(solution)/shard_map/ppermute | solution.py:10
  376.6 1.6 copy-start.1
  378.2 1.6 copy-start.3
Sparse Core Ops, SparseCore 0:
  10.4 51.1 all-gather.1
  376.7 48.8 reduce-scatter.1
where the time goes:
time: 437 us; the launch traced here: 434 us
  waiting for transfers between devices  391 us (89%)
  between operations  15.4 us (4%)
  starting transfers between devices  12.6 us (3%)
  matrix products  10 us (2%)
    ppermute x2, waiting for transfers between devices, passed_along(): return lax.ppermute(block, axis, route)  292 us
    all_gather x1, waiting for transfers between devices, body(): lax.all_gather(sentence_features, 'grp', axis=0, tiled=True)  53.6 us
    reduce_scatter x1, waiting for transfers between devices, body(): lax.psum_scatter(sentence_count, 'grp', scatter_dimension=0, tiled=True)  44.7 us
    ppermute x2, starting transfers between devices, passed_along(): return lax.ppermute(block, axis, route)  12.5 us
  transfers between devices with their start and end apart: 4, of which 4 were waited for; matrix products, arithmetic and copies ran while one was open for 1% of the time, Pallas kernels for 0%

commit v1 on v0

v1 whole, which is shorter than its diff:
```python
import jax
import jax.numpy as jnp
from jax import lax
from jax.sharding import Mesh, PartitionSpec as P

CHIPS = 4
CORES = 2


def moved(array, axes, pairs):
    return lax.ppermute(array, axes, pairs)


def body(images, captions, multiplier, offset):
    scale = multiplier[0]
    bias = offset[0]
    rows = images.shape[0]
    blocks = lax.axis_size("blk")
    chip = lax.axis_index("zl")
    low = chip < 2
    inner = jnp.logical_or(chip == 1, chip == 2)

    own = jnp.where(low, captions, images)
    other = jnp.where(low, images, captions)
    both = jnp.concatenate([own, other])

    from_end = moved(both, "zl", [(0, 1), (3, 2)])
    from_inner = moved(both, "zl", [(1, 2), (2, 1)])
    from_far_end = moved(both, "zl", [(0, 2), (3, 1)])

    def neighbour(array, low_source, high_source):
        pairs = []
        for p in range(blocks):
            pairs.append((((p + 1) % blocks) * CHIPS + low_source, p * CHIPS + 1))
            pairs.append((((p - 1) % blocks) * CHIPS + high_source, p * CHIPS + 2))
        return moved(array, ("blk", "zl"), pairs)

    near = [
        neighbour(own, 1, 2),
        neighbour(own, 0, 3),
        neighbour(other, 2, 1),
        neighbour(other, 3, 0),
    ]

    left = jnp.concatenate([other, from_end[rows:], from_inner[:rows], from_far_end[:rows]])
    right = jnp.concatenate([own, from_end[:rows], from_inner[rows:], from_far_end[rows:]])
    next_right = jnp.concatenate(near)
    swap = [(0, 1), (1, 0)]
    right = jnp.concatenate([right, moved(right, "core", swap)])
    next_right = jnp.concatenate([next_right, moved(next_right, "core", swap)])

    def slopes_of(columns, paired):
        scores = lax.dot_general(
            left, columns, (((1,), (1,)), ((), ())), preferred_element_type=jnp.float32
        )
        scores = scores * scale + bias
        slopes = jax.nn.sigmoid(scores)
        if paired:
            row = lax.broadcasted_iota(jnp.int32, slopes.shape, 0)
            column = lax.broadcasted_iota(jnp.int32, slopes.shape, 1)
            slopes = jnp.where(row == column, -jax.nn.sigmoid(-scores), slopes)
        return slopes.astype(jnp.bfloat16)

    total = jnp.dot(slopes_of(right, True), right, preferred_element_type=jnp.float32)
    total = total + jnp.dot(slopes_of(next_right, False), next_right, preferred_element_type=jnp.float32)
    result = (scale * total).astype(jnp.bfloat16)

    to_end = moved(result[rows : 2 * rows], "zl", [(1, 0), (2, 3)])
    to_inner = moved(result[2 * rows : 3 * rows], "zl", [(1, 2), (2, 1)])
    to_far_end = moved(result[3 * rows :], "zl", [(1, 3), (2, 0)])
    own_result = jnp.where(inner, result[:rows], to_end)
    other_result = jnp.where(inner, to_inner, to_far_end)
    return (jnp.where(low, own_result, other_result), jnp.where(low, other_result, own_result))


def solution(mesh):
    fine = Mesh(mesh.devices.reshape(-1, CHIPS, CORES), ("blk", "zl", "core"))
    rows = P(("blk", "zl", "core"), None)
    return jax.shard_map(
        body, mesh=fine, in_specs=(rows, rows, P(), P()), out_specs=(rows, rows), check_vma=False
    )
```

time: 437 us -> 112 us (0.26)
  waiting for transfers between devices: 391 us -> 47.7 us
  starting transfers between devices: 12.6 us -> 41.2 us
  between operations: 15.4 us -> 2.16 us
    ppermute x2 -> x12, waiting for transfers between devices: 292 us -> 47.7 us  [moved(): return lax.ppermute(array, axes, pairs)]
    all_gather x1 -> x0, waiting for transfers between devices: 53.6 us -> none  [body(): lax.all_gather(sentence_features, 'grp', axis=0, tiled=True)]
    reduce_scatter x1 -> x0, waiting for transfers between devices: 44.7 us -> none  [body(): lax.psum_scatter(sentence_count, 'grp', scatter_dimension=0, tiled=True)]
    ppermute x2 -> x12, starting transfers between devices: 12.5 us -> 41.2 us  [moved(): return lax.ppermute(array, axes, pairs)]
    dot_general x6 -> x2, matrix products: 10 us -> 11.6 us  [the longest x1 6.11 us: body(): jnp.dot(slopes_of(next_right, False), next_right, preferred_element_type=...]
  transfers between devices with their start and end apart: 4 -> 12, of which waited for: 4 -> 5; matrix products, arithmetic and copies ran while one was open for 1% -> 9% of each run, Pallas kernels for 0% -> 0%
where the time goes in v1:
time: 112 us; the launch traced here: 110 us
  waiting for transfers between devices  47.7 us (43%)
  starting transfers between devices  41.2 us (37%)
  matrix products  11.6 us (10%)
  local copies, waits for them, and re-layouts  5.27 us (5%)
  other arithmetic  2.17 us (2%)
  between operations  2.16 us (2%)
    ppermute x12, waiting for transfers between devices, moved(): return lax.ppermute(array, axes, pairs)  47.7 us
    ppermute x12, starting transfers between devices, moved(): return lax.ppermute(array, axes, pairs)  41.2 us
    dot_general x1, matrix products, body(): jnp.dot(slopes_of(next_right, False), next_right, preferred_element_type=...  6.11 us
    dot_general x1, matrix products, body(): jnp.dot(slopes_of(right, True), right, preferred_element_type=jnp.float32)  5.48 us
    unnamed x6, local copies, waits for them, and re-layouts  2.89 us
  transfers between devices with their start and end apart: 12, of which 5 were waited for; matrix products, arithmetic and copies ran while one was open for 9% of the time, Pallas kernels for 0%

profile of v1, /device:TPU:1, one launch (start us, length us, event | category | flops | bytes accessed | tf_op | source)
XLA Modules:
  0.0 110.1 jit_solution(7150682947032637494)
XLA Ops:
  0.6 1.1 %constant_dynamic-update-slice_fusion.4 = (bf16[1024,1024]{1,0:T(8,128)(2,1)S(1)}, bf16[128,1024]{1,0:T(8,128)(2,1)S(1)}, bf16[128,1024]{1,0:T(8,128)(2,1)S(1)}) fusion(bf16[128,1024]{1,0:T(8,128)(2,1)} %param.5, bf16[128,1024]{1,0:T(8,128)(2,1)} %param.4, pred[]{:T(512)S(6)} %lt.3), kind=kLoop, calls=%fused_computation.22 | loop fusion | flops 262143 | bytes 1310721
  1.8 0.7 collective-permute-start.4
  2.5 22.5 %collective-permute-start.5 = (bf16[128,1024]{1,0:T(8,128)(2,1)S(1)}, bf16[128,1024]{1,0:T(8,128)(2,1)S(1)}, u32[]{:S(2)}, u32[]{:S(2)}) collective-permute-start(bf16[128,1024]{1,0:T(8,128)(2,1)S(1)} %get-tuple-element.3), channel_id=1, source_target_pairs={{8,2},{766,4},{16,10},{6,12},{24,18},{14,20},{32,26},{22,28},{40,3... | collective-permute-start | bytes 786440 | tf_op jit(solution)/shard_map/ppermute | solution.py:11
  25.0 0.7 collective-permute-start.6
  25.7 4.7 %collective-permute-start.7 = (bf16[128,1024]{1,0:T(8,128)(2,1)S(1)}, bf16[128,1024]{1,0:T(8,128)(2,1)S(1)}, u32[]{:S(2)}, u32[]{:S(2)}) collective-permute-start(bf16[128,1024]{1,0:T(8,128)(2,1)S(1)} %get-tuple-element.18), channel_id=1, source_target_pairs={{14,2},{760,4},{22,10},{0,12},{30,18},{8,20},{38,26},{16,28},{46,3... | collective-permute-start | bytes 786440 | tf_op jit(solution)/shard_map/ppermute | solution.py:11
  30.5 1.3 %collective-permute-start = (bf16[256,1024]{1,0:T(8,128)(2,1)S(1)}, bf16[256,1024]{1,0:T(8,128)(2,1)S(1)}, u32[]{:S(2)}, u32[]{:S(2)}) collective-permute-start(bf16[256,1024]{1,0:T(8,128)(2,1)S(1)} %pad_maximum_fusion.3), channel_id=1, source_target_pairs={{0,2},{6,4},{1,3},{7,5},{8,10},{14,12},{9,11},{15,13},{16,18},{22,... | collective-permute-start | bytes 1572872 | tf_op jit(solution)/shard_map/ppermute | solution.py:11
  33.1 1.3 %collective-permute-start.2 = (bf16[256,1024]{1,0:T(8,128)(2,1)S(1)}, bf16[256,1024]{1,0:T(8,128)(2,1)S(1)}, u32[]{:S(2)}, u32[]{:S(2)}) collective-permute-start(bf16[256,1024]{1,0:T(8,128)(2,1)S(1)} %pad_maximum_fusion.3), channel_id=1, source_target_pairs={{0,4},{6,2},{1,5},{7,3},{8,12},{14,10},{9,13},{15,11},{16,20},{22,... | collective-permute-start | bytes 1572872 | tf_op jit(solution)/shard_map/ppermute | solution.py:11
  34.4 5.7 %collective-permute-done.5 = bf16[128,1024]{1,0:T(8,128)(2,1)S(1)} collective-permute-done((bf16[128,1024]{1,0:T(8,128)(2,1)S(1)}, bf16[128,1024]{1,0:T(8,128)(2,1)S(1)}, u32[]{:S(2)}, u32[]{:S(2)}) %collective-permute-start.5) | collective-permute-done | bytes 262176 | tf_op jit(solution)/shard_map/ppermute | solution.py:11
  40.1 0.7 collective-permute-start.1
  40.9 0.1 pad_maximum_fusion.2
  40.9 2.4 %collective-permute-start.8 = (bf16[512,1024]{1,0:T(8,128)(2,1)S(1)}, bf16[512,1024]{1,0:T(8,128)(2,1)S(1)}, u32[]{:S(2)}, u32[]{:S(2)}) collective-permute-start(bf16[512,1024]{1,0:T(8,128)(2,1)S(1)} %pad_maximum_fusion.2), channel_id=1, source_target_pairs={{0,1},{1,0},{2,3},{3,2},{4,5},{5,4},{6,7},{7,6},{8,9},{9,8},{10,11... | collective-permute-start | bytes 3145736 | tf_op jit(solution)/shard_map/ppermute | solution.py:11
  43.3 0.7 constant_dynamic-update-slice_fusion.9
  44.1 0.7 constant_dynamic-update-slice_fusion.8
  44.8 4.2 %collective-permute-done = bf16[256,1024]{1,0:T(8,128)(2,1)S(1)} collective-permute-done((bf16[256,1024]{1,0:T(8,128)(2,1)S(1)}, bf16[256,1024]{1,0:T(8,128)(2,1)S(1)}, u32[]{:S(2)}, u32[]{:S(2)}) %collective-permute-start) | collective-permute-done | bytes 524320 | tf_op jit(solution)/shard_map/ppermute | solution.py:11
  49.0 0.1 fusion.11
  49.1 0.1 fusion.12
  49.1 11.1 %collective-permute-done.2 = bf16[256,1024]{1,0:T(8,128)(2,1)S(1)} collective-permute-done((bf16[256,1024]{1,0:T(8,128)(2,1)S(1)}, bf16[256,1024]{1,0:T(8,128)(2,1)S(1)}, u32[]{:S(2)}, u32[]{:S(2)}) %collective-permute-start.2) | collective-permute-done | bytes 524320 | tf_op jit(solution)/shard_map/ppermute | solution.py:11
  60.3 0.1 fusion.13
  60.4 0.1 pad_maximum_fusion.1
  60.4 3.6 %collective-permute-start.3 = (bf16[512,1024]{1,0:T(8,128)(2,1)S(1)}, bf16[512,1024]{1,0:T(8,128)(2,1)S(1)}, u32[]{:S(2)}, u32[]{:S(2)}) collective-permute-start(bf16[512,1024]{1,0:T(8,128)(2,1)S(1)} %pad_maximum_fusion.1), channel_id=1, source_target_pairs={{0,1},{1,0},{2,3},{3,2},{4,5},{5,4},{6,7},{7,6},{8,9},{9,8},{10,11... | collective-permute-start | bytes 3145736 | tf_op jit(solution)/shard_map/ppermute | solution.py:11
  64.1 0.7 constant_dynamic-update-slice_fusion.7
  64.8 0.7 constant_dynamic-update-slice_fusion.6
  65.5 1.1 constant_dynamic-update-slice_fusion.5
  66.6 6.1 %fusion.3 = f32[512,1024]{1,0:T(8,128)} fusion(bf16[1024,1024]{1,0:T(8,128)(2,1)} %constant_dynamic-update-slice_fusion.5, f32[]{:T(128)} %bitcast.9, f32[]{:T(128)} %bitcast.7, bf16[128,1024]{1,0:T(8,128)(2,1)S(1)} %get-tuple-element.17, bf16[128,1024]{1,0:T(8,128)(2,1)S(1)} %get-tuple-element.14, bf16[128,1024]{1,0:T(8,128)(2,1)S(1)} %get-tuple-element.11, ...), kind=kOutput, calls=%fused_computation.10 | convolution fusion | flops 2154823680 | bytes 5242888 | tf_op jit(solution)/shard_map/dot_general | solution.py:65
  72.7 1.1 constant_dynamic-update-slice_fusion
  73.8 5.5 %multiply_convert_fusion = bf16[512,1024]{1,0:T(8,128)(2,1)S(1)} fusion(f32[512,1024]{1,0:T(8,128)} %fusion.3, bf16[1024,1024]{1,0:T(8,128)(2,1)} %constant_dynamic-update-slice_fusion, f32[]{:T(128)} %bitcast.8, f32[]{:T(128)} %bitcast.6, bf16[128,1024]{1,0:T(8,128)(2,1)S(1)} %get-tuple-element.17, bf16[128,1024]{1,0:T(8,128)(2,1)S(1)} %get-tuple-element.14, ...), kind=kOutput, calls=%fused_computation | convolution fusion | flops 2159017984 | bytes 6291464 | tf_op jit(solution)/shard_map/dot_general | solution.py:64
  79.3 0.7 collective-permute-start.10
  80.0 1.3 %collective-permute-start.11 = (bf16[128,1024]{1,0:T(8,128)(2,1)S(1)}, bf16[128,1024]{1,0:T(8,128)(2,1)S(1)}, u32[]{:S(2)}, u32[]{:S(2)}) collective-permute-start(bf16[128,1024]{1,0:T(8,128)(2,1)S(1)} %get-tuple-element.7), channel_id=1, source_target_pairs={{2,6},{4,0},{3,7},{5,1},{10,14},{12,8},{11,15},{13,9},{18,22},{20,... | collective-permute-start | bytes 786440 | tf_op jit(solution)/shard_map/ppermute | solution.py:11
  81.3 1.3 %collective-permute-start.9 = (bf16[128,1024]{1,0:T(8,128)(2,1)S(1)}, bf16[128,1024]{1,0:T(8,128)(2,1)S(1)}, u32[]{:S(2)}, u32[]{:S(2)}) collective-permute-start(bf16[128,1024]{1,0:T(8,128)(2,1)S(1)} %get-tuple-element.6), channel_id=1, source_target_pairs={{2,0},{4,6},{3,1},{5,7},{10,8},{12,14},{11,9},{13,15},{18,16},{20,... | collective-permute-start | bytes 786440 | tf_op jit(solution)/shard_map/ppermute | solution.py:11
  82.6 25.0 %collective-permute-done.11 = bf16[128,1024]{1,0:T(8,128)(2,1)S(1)} collective-permute-done((bf16[128,1024]{1,0:T(8,128)(2,1)S(1)}, bf16[128,1024]{1,0:T(8,128)(2,1)S(1)}, u32[]{:S(2)}, u32[]{:S(2)}) %collective-permute-start.11) | collective-permute-done | bytes 262176 | tf_op jit(solution)/shard_map/ppermute | solution.py:11
  107.6 1.6 %collective-permute-done.9 = bf16[128,1024]{1,0:T(8,128)(2,1)S(1)} collective-permute-done((bf16[128,1024]{1,0:T(8,128)(2,1)S(1)}, bf16[128,1024]{1,0:T(8,128)(2,1)S(1)}, u32[]{:S(2)}, u32[]{:S(2)}) %collective-permute-start.9) | collective-permute-done | bytes 262176 | tf_op jit(solution)/shard_map/ppermute | solution.py:11
  109.2 0.8 broadcast_select_fusion.1
  (11 shorter events, 0.1 us)
Async XLA Ops:
  1.8 31.3 %collective-permute-start.4 = (bf16[128,1024]{1,0:T(8,128)(2,1)S(1)}, bf16[128,1024]{1,0:T(8,128)(2,1)S(1)}, u32[]{:S(2)}, u32[]{:S(2)}) collective-permute-start(bf16[128,1024]{1,0:T(8,128)(2,1)S(1)} %get-tuple-element.3), channel_id=1, source_target_pairs={{10,2},{764,4},{18,10},{4,12},{26,18},{12,20},{34,26},{20,28},{42,... | collective-permute-start | bytes 786440 | tf_op jit(solution)/shard_map/ppermute | solution.py:11
  2.5 37.7 %collective-permute-start.5 = (bf16[128,1024]{1,0:T(8,128)(2,1)S(1)}, bf16[128,1024]{1,0:T(8,128)(2,1)S(1)}, u32[]{:S(2)}, u32[]{:S(2)}) collective-permute-start(bf16[128,1024]{1,0:T(8,128)(2,1)S(1)} %get-tuple-element.3), channel_id=1, source_target_pairs={{8,2},{766,4},{16,10},{6,12},{24,18},{14,20},{32,26},{22,28},{40,3... | collective-permute-start | bytes 786440 | tf_op jit(solution)/shard_map/ppermute | solution.py:11
  25.0 15.8 %collective-permute-start.6 = (bf16[128,1024]{1,0:T(8,128)(2,1)S(1)}, bf16[128,1024]{1,0:T(8,128)(2,1)S(1)}, u32[]{:S(2)}, u32[]{:S(2)}) collective-permute-start(bf16[128,1024]{1,0:T(8,128)(2,1)S(1)} %get-tuple-element.18), channel_id=1, source_target_pairs={{12,2},{762,4},{20,10},{2,12},{28,18},{10,20},{36,26},{18,28},{44,... | collective-permute-start | bytes 786440 | tf_op jit(solution)/shard_map/ppermute | solution.py:11
  25.7 15.2 %collective-permute-start.7 = (bf16[128,1024]{1,0:T(8,128)(2,1)S(1)}, bf16[128,1024]{1,0:T(8,128)(2,1)S(1)}, u32[]{:S(2)}, u32[]{:S(2)}) collective-permute-start(bf16[128,1024]{1,0:T(8,128)(2,1)S(1)} %get-tuple-element.18), channel_id=1, source_target_pairs={{14,2},{760,4},{22,10},{0,12},{30,18},{8,20},{38,26},{16,28},{46,3... | collective-permute-start | bytes 786440 | tf_op jit(solution)/shard_map/ppermute | solution.py:11
  30.5 18.5 %collective-permute-start = (bf16[256,1024]{1,0:T(8,128)(2,1)S(1)}, bf16[256,1024]{1,0:T(8,128)(2,1)S(1)}, u32[]{:S(2)}, u32[]{:S(2)}) collective-permute-start(bf16[256,1024]{1,0:T(8,128)(2,1)S(1)} %pad_maximum_fusion.3), channel_id=1, source_target_pairs={{0,2},{6,4},{1,3},{7,5},{8,10},{14,12},{9,11},{15,13},{16,18},{22,... | collective-permute-start | bytes 1572872 | tf_op jit(solution)/shard_map/ppermute | solution.py:11
  33.1 27.2 %collective-permute-start.2 = (bf16[256,1024]{1,0:T(8,128)(2,1)S(1)}, bf16[256,1024]{1,0:T(8,128)(2,1)S(1)}, u32[]{:S(2)}, u32[]{:S(2)}) collective-permute-start(bf16[256,1024]{1,0:T(8,128)(2,1)S(1)} %pad_maximum_fusion.3), channel_id=1, source_target_pairs={{0,4},{6,2},{1,5},{7,3},{8,12},{14,10},{9,13},{15,11},{16,20},{22,... | collective-permute-start | bytes 1572872 | tf_op jit(solution)/shard_map/ppermute | solution.py:11
  40.1 8.9 %collective-permute-start.1 = (bf16[256,1024]{1,0:T(8,128)(2,1)S(1)}, bf16[256,1024]{1,0:T(8,128)(2,1)S(1)}, u32[]{:S(2)}, u32[]{:S(2)}) collective-permute-start(bf16[256,1024]{1,0:T(8,128)(2,1)S(1)} %pad_maximum_fusion.3), channel_id=1, source_target_pairs={{2,4},{4,2},{3,5},{5,3},{10,12},{12,10},{11,13},{13,11},{18,20},{2... | collective-permute-start | bytes 1572872 | tf_op jit(solution)/shard_map/ppermute | solution.py:11
  40.9 24.6 %collective-permute-start.8 = (bf16[512,1024]{1,0:T(8,128)(2,1)S(1)}, bf16[512,1024]{1,0:T(8,128)(2,1)S(1)}, u32[]{:S(2)}, u32[]{:S(2)}) collective-permute-start(bf16[512,1024]{1,0:T(8,128)(2,1)S(1)} %pad_maximum_fusion.2), channel_id=1, source_target_pairs={{0,1},{1,0},{2,3},{3,2},{4,5},{5,4},{6,7},{7,6},{8,9},{9,8},{10,11... | collective-permute-start | bytes 3145736 | tf_op jit(solution)/shard_map/ppermute | solution.py:11
  60.3 6.3 %copy-start = (bf16[1024,1024]{1,0:T(8,128)(2,1)}, bf16[1024,1024]{1,0:T(8,128)(2,1)S(1)}, u32[]{:S(2)}) copy-start(bf16[1024,1024]{1,0:T(8,128)(2,1)S(1)} %get-tuple-element.16) | copy-start | bytes 6291460
  60.4 12.3 %collective-permute-start.3 = (bf16[512,1024]{1,0:T(8,128)(2,1)S(1)}, bf16[512,1024]{1,0:T(8,128)(2,1)S(1)}, u32[]{:S(2)}, u32[]{:S(2)}) collective-permute-start(bf16[512,1024]{1,0:T(8,128)(2,1)S(1)} %pad_maximum_fusion.1), channel_id=1, source_target_pairs={{0,1},{1,0},{2,3},{3,2},{4,5},{5,4},{6,7},{7,6},{8,9},{9,8},{10,11... | collective-permute-start | bytes 3145736 | tf_op jit(solution)/shard_map/ppermute | solution.py:11
  79.3 3.3 %collective-permute-start.10 = (bf16[128,1024]{1,0:T(8,128)(2,1)S(1)}, bf16[128,1024]{1,0:T(8,128)(2,1)S(1)}, u32[]{:S(2)}, u32[]{:S(2)}) collective-permute-start(bf16[128,1024]{1,0:T(8,128)(2,1)S(1)} %get-tuple-element.8), channel_id=1, source_target_pairs={{2,4},{4,2},{3,5},{5,3},{10,12},{12,10},{11,13},{13,11},{18,20},{2... | collective-permute-start | bytes 786440 | tf_op jit(solution)/shard_map/ppermute | solution.py:11
  80.0 27.6 %collective-permute-start.11 = (bf16[128,1024]{1,0:T(8,128)(2,1)S(1)}, bf16[128,1024]{1,0:T(8,128)(2,1)S(1)}, u32[]{:S(2)}, u32[]{:S(2)}) collective-permute-start(bf16[128,1024]{1,0:T(8,128)(2,1)S(1)} %get-tuple-element.7), channel_id=1, source_target_pairs={{2,6},{4,0},{3,7},{5,1},{10,14},{12,8},{11,15},{13,9},{18,22},{20,... | collective-permute-start | bytes 786440 | tf_op jit(solution)/shard_map/ppermute | solution.py:11
  81.3 27.9 %collective-permute-start.9 = (bf16[128,1024]{1,0:T(8,128)(2,1)S(1)}, bf16[128,1024]{1,0:T(8,128)(2,1)S(1)}, u32[]{:S(2)}, u32[]{:S(2)}) collective-permute-start(bf16[128,1024]{1,0:T(8,128)(2,1)S(1)} %get-tuple-element.6), channel_id=1, source_target_pairs={{2,0},{4,6},{3,1},{5,7},{10,8},{12,14},{11,9},{13,15},{18,16},{20,... | collective-permute-start | bytes 786440 | tf_op jit(solution)/shard_map/ppermute | solution.py:11

commit v2 on v1

v2 whole, which is shorter than its diff:
```python
import functools
import math

import jax
import jax.numpy as jnp
from jax import lax
from jax.experimental import pallas as pl
from jax.experimental.pallas import tpu as pltpu
from jax.sharding import Mesh, PartitionSpec as P

CHIPS = 4
CORES = 2
LIMIT = 16 * 1024 * 1024


def in_vmem(kernel, shapes, *operands, flops=0, scalars=0, scratch=()):
    moved_bytes = sum(math.prod(s.shape) * s.dtype.itemsize for s in shapes)
    return pl.pallas_call(
        kernel,
        out_shape=shapes,
        in_specs=[pl.BlockSpec(memory_space=pltpu.SMEM)] * scalars
        + [pl.BlockSpec(memory_space=pltpu.VMEM)] * (len(operands) - scalars),
        out_specs=[pl.BlockSpec(memory_space=pltpu.VMEM)] * len(shapes),
        scratch_shapes=[pltpu.VMEM(s.shape, s.dtype) for s in scratch],
        compiler_params=pltpu.CompilerParams(vmem_limit_bytes=LIMIT),
        cost_estimate=pl.CostEstimate(flops=flops, bytes_accessed=moved_bytes, transcendentals=0),
    )(*operands)


def pack_kernel(rows, own, other, own_far, xe, xo, y0, af, to_near, to_last, w1, left, first):
    gathered(to_near, [(xe, 0, rows), (xo, 1, rows)])
    gathered(to_last, [(other, 0, rows), (y0, 0, rows)])
    gathered(w1, [(xe, 0, rows), (xo, 1, rows), (y0, 0, rows)])
    gathered(left, [(other, 0, rows), (xe, 1, rows), (xo, 0, rows), (af, 0, rows)])
    gathered(first, [(own, 0, rows), (own_far, 0, rows)])


def slopes_of(scores, scale, bias, diagonal=None):
    scores = scores * scale + bias
    if diagonal is not None:
        scores = jnp.where(diagonal, -scores, scores)
    slopes = 1.0 / (1.0 + jnp.exp(-scores))
    if diagonal is not None:
        slopes = jnp.where(diagonal, -slopes, slopes)
    return slopes.astype(jnp.bfloat16)


def across(a, b):
    return lax.dot_general(a, b, (((1,), (1,)), ((), ())), preferred_element_type=jnp.float32)


def gathered(buffer, pieces):
    row = 0
    for ref, part, rows in pieces:
        buffer[row : row + rows, :] = ref[part * rows : (part + 1) * rows, :]
        row += rows


def pairs_of(rows, *triples):
    return [(ref, part, rows) for near, far, part in triples for ref in (near, far)]


def accumulated(left, columns, total, scale, bias, matches=()):
    rows = left.shape[0]
    wide = 256
    for j in range(columns.shape[0] // wide):
        chunk = columns[j * wide : (j + 1) * wide, :]
        scores = across(left, chunk)
        diagonal = None
        starts = [row for row, number in matches if number == j]
        if starts:
            row = lax.broadcasted_iota(jnp.int32, scores.shape, 0)
            column = lax.broadcasted_iota(jnp.int32, scores.shape, 1)
            diagonal = jnp.logical_and(column == row - starts[0], column < wide // 2)
        term = jnp.dot(slopes_of(scores, scale, bias, diagonal), chunk, preferred_element_type=jnp.float32)
        total = term if total is None else total + term
    return total


def early_kernel(scale, bias, left, first, w1, w1_far, acc, columns):
    rows = first.shape[0] // 2
    gathered(columns, [(first, 0, 2 * rows)])
    gathered(columns.at[2 * rows :, :], pairs_of(rows, (w1, w1_far, 0), (w1, w1_far, 1), (w1, w1_far, 2)))
    acc[...] = accumulated(left[...], columns, None, scale[0], bias[0], [(i * rows, i) for i in range(3)])


def middle_kernel(scale, bias, left, y1, y1_far, acc, out, columns):
    rows = y1.shape[0] // 2
    gathered(columns, pairs_of(rows, (y1, y1_far, 0), (y1, y1_far, 1)))
    out[...] = accumulated(left[...], columns, acc[...], scale[0], bias[0])


def late_kernel(parts, scale, bias, left, acc, last, last_far, out0, out1, columns):
    rows = out0.shape[0]
    gathered(columns, pairs_of(rows, (last, last_far, 0), (last, last_far, 1)))
    for part, out in zip(parts, (out0, out1)):
        here = slice(part * rows, (part + 1) * rows)
        total = accumulated(
            left[here, :], columns, acc[here, :], scale[0], bias[0], [(0, 0)] if part == CHIPS - 1 else []
        )
        out[...] = (scale[0] * total).astype(out.dtype)


def body(images, captions, scale, bias):
    rows, width = images.shape
    blocks = lax.axis_size("blk")
    chip = lax.axis_index("zl")
    low = chip < 2
    inner = jnp.logical_or(chip == 1, chip == 2)

    def line(array, pairs):
        return lax.ppermute(array, "zl", pairs)

    def swapped(array):
        return lax.ppermute(array, "core", [(0, 1), (1, 0)])

    def neighbour(array, chips):
        pairs = []
        for p in range(blocks):
            for k in chips:
                q = p + 1 if k % 2 else p - 1
                pairs.append(((q % blocks) * CHIPS + k, p * CHIPS + k))
        return lax.ppermute(array, ("blk", "zl"), pairs)

    f32 = functools.partial(jax.ShapeDtypeStruct, dtype=jnp.float32)
    b16 = functools.partial(jax.ShapeDtypeStruct, dtype=jnp.bfloat16)
    unit = 4 * rows * rows * width

    to_inner = [(0, 1), (3, 2)]
    between = [(1, 2), (2, 1)]
    to_far = [(0, 2), (3, 1)]

    own = jnp.where(low, captions, images)
    other = jnp.where(low, images, captions)
    both = jnp.concatenate([own, other])

    y0 = neighbour(jnp.where(inner, own, other), range(CHIPS))
    xe = line(both, to_inner)
    xo = line(both, between)
    own_far = swapped(own)
    af = line(own, to_far)

    to_near, to_last, w1, left, first = in_vmem(
        functools.partial(pack_kernel, rows),
        [b16((n * rows, width)) for n in (2, 2, 3, 4, 2)],
        own, other, own_far, xe, xo, y0, af,
    )
    y1 = neighbour(to_near, (1, 2))
    last = line(to_last, to_far)
    w1_far = swapped(w1)
    (acc,) = in_vmem(
        early_kernel, [f32((4 * rows, width))], scale, bias, left, first, w1, w1_far,
        flops=32 * unit, scalars=2, scratch=[b16((8 * rows, width))],
    )
    y1, acc = lax.optimization_barrier((y1, acc))
    y1_far = swapped(y1)
    (acc,) = in_vmem(
        middle_kernel, [f32((4 * rows, width))], scale, bias, left, y1, y1_far, acc,
        flops=16 * unit, scalars=2, scratch=[b16((4 * rows, width))],
    )
    last_far = swapped(last)
    oe, of = in_vmem(
        functools.partial(late_kernel, (1, 3)), [b16((rows, width))] * 2, scale, bias, left, acc, last, last_far,
        flops=8 * unit, scalars=2, scratch=[b16((4 * rows, width))],
    )
    om, oo = in_vmem(
        functools.partial(late_kernel, (0, 2)), [b16((rows, width))] * 2, scale, bias, left, acc, last, last_far,
        flops=8 * unit, scalars=2, scratch=[b16((4 * rows, width))],
    )

    to_end = line(oe, [(1, 0), (2, 3)])
    to_far_end = line(of, [(1, 3), (2, 0)])
    to_other = line(oo, between)
    own_result = jnp.where(inner, om, to_end)
    other_result = jnp.where(inner, to_other, to_far_end)
    return (jnp.where(low, own_result, other_result), jnp.where(low, other_result, own_result))


def solution(mesh):
    fine = Mesh(mesh.devices.reshape(-1, CHIPS, CORES), ("blk", "zl", "core"))
    rows = P(("blk", "zl", "core"), None)
    return jax.shard_map(
        body, mesh=fine, in_specs=(rows, rows, P(), P()), out_specs=(rows, rows), check_vma=False
    )
```

time: 112 us -> 97.5 us (0.87); the launches traced: 110 us -> 97 us
  matrix products: 11.6 us -> 0 us
  starting transfers between devices: 41.2 us -> 30.9 us
  Pallas kernels: 0 us -> 7.75 us
  waiting for transfers between devices: 47.7 us -> 54.3 us
  local copies, waits for them, and re-layouts: 5.27 us -> 0 us
    dot_general x2 -> x0, matrix products: 11.6 us -> none  [the longest x1 6.11 us: body(): jnp.dot(slopes_of(next_right, False), next_right, preferred_element_type=...]
    ppermute x12 -> x13, starting transfers between devices: 41.2 us -> 30.9 us  [the longest x4 16.8 us: swapped(): return lax.ppermute(array, 'core', [(0, 1), (1, 0)])]
    pallas_call x0 -> x5, Pallas kernels: none -> 7.75 us  [in_vmem(): pl.pallas_call(kernel, out_shape=shapes, in_specs=[pl.BlockSpec(memory_sp...]
    ppermute x12 -> x13, waiting for transfers between devices: 47.7 us -> 54.3 us  [the longest x2 27.6 us: neighbour(): return lax.ppermute(array, ('blk', 'zl'), pairs)]
    unnamed x6 -> x0, local copies, waits for them, and re-layouts: 2.89 us -> none
    concatenate x2 -> x0, local copies, waits for them, and re-layouts: 2.15 us -> none  [the longest x1 1.09 us: body(): next_right = jnp.concatenate([next_right, moved(next_right, 'core', swap)])]
    unnamed x1 -> x0, other arithmetic: 1.14 us -> none
  transfers between devices with their start and end apart: 12 -> 13, of which waited for: 5 -> 4; matrix products, arithmetic and copies ran while one was open for 9% -> 0% of each run, Pallas kernels for 0% -> 6%
where the time goes in v2:
time: 97.5 us; the launch traced here: 97 us
  waiting for transfers between devices  54.3 us (56%)
  starting transfers between devices  30.9 us (32%)
  Pallas kernels  7.75 us (8%)
  between operations  2.13 us (2%)
  other arithmetic  1.97 us (2%)
    ppermute x2, waiting for transfers between devices, neighbour(): return lax.ppermute(array, ('blk', 'zl'), pairs)  27.6 us
    ppermute x7, waiting for transfers between devices, line(): return lax.ppermute(array, 'zl', pairs)  26.7 us
    ppermute x4, starting transfers between devices, swapped(): return lax.ppermute(array, 'core', [(0, 1), (1, 0)])  16.8 us
    ppermute x7, starting transfers between devices, line(): return lax.ppermute(array, 'zl', pairs)  11.4 us
    pallas_call x5, Pallas kernels, in_vmem(): pl.pallas_call(kernel, out_shape=shapes, in_specs=[pl.BlockSpec(memory_sp...  7.75 us
    ppermute x2, starting transfers between devices, neighbour(): return lax.ppermute(array, ('blk', 'zl'), pairs)  2.61 us
  transfers between devices with their start and end apart: 13, of which 4 were waited for; matrix products, arithmetic and copies ran while one was open for 0% of the time, Pallas kernels for 6%

profile of v2, /device:TPU:1, one launch (start us, length us, event | category | flops | bytes accessed | tf_op | source)
XLA Modules:
  0.0 97.0 jit_solution(6065936573857795945)
XLA Ops:
  0.6 1.1 %broadcast_select_fusion.2 = (bf16[128,1024]{1,0:T(8,128)(2,1)S(1)}, bf16[128,1024]{1,0:T(8,128)(2,1)S(1)}, bf16[128,1024]{1,0:T(8,128)(2,1)S(1)}) fusion(pred[]{:T(512)S(6)} %or.3, bf16[128,1024]{1,0:T(8,128)(2,1)} %param.4, bf16[128,1024]{1,0:T(8,128)(2,1)} %param.5, pred[]{:T(512)S(6)} %lt.3), kind=kLoop, calls=%fused_computation.3 | loop fusion | flops 393216 | bytes 1310722 | tf_op jit(solution)/shard_map/jit(_where)/select_n | solution.py:137
  1.8 4.9 %collective-permute-start.1 = (bf16[256,1024]{1,0:T(8,128)(2,1)S(1)}, bf16[256,1024]{1,0:T(8,128)(2,1)S(1)}, u32[]{:S(2)}, u32[]{:S(2)}) collective-permute-start(bf16[256,1024]{1,0:T(8,128)(2,1)S(1)} %pad_maximum_fusion), channel_id=1, source_target_pairs={{0,2},{6,4},{1,3},{7,5},{8,10},{14,12},{9,11},{15,13},{16,18},{22,... | collective-permute-start | bytes 1572872 | tf_op jit(solution)/shard_map/ppermute | solution.py:112
  6.6 0.7 collective-permute-start.2
  7.3 8.9 %collective-permute-start = (bf16[128,1024]{1,0:T(8,128)(2,1)S(1)}, bf16[128,1024]{1,0:T(8,128)(2,1)S(1)}, u32[]{:S(2)}, u32[]{:S(2)}) collective-permute-start(bf16[128,1024]{1,0:T(8,128)(2,1)S(1)} %get-tuple-element.26.own), channel_id=1, source_target_pairs={{0,1},{1,0},{2,3},{3,2},{4,5},{5,4},{6,7},{7,6},{8,9},{9,8},{10,11... | collective-permute-start | bytes 786440 | tf_op jit(solution)/shard_map/ppermute | solution.py:115
  16.2 1.3 %collective-permute-start.4 = (bf16[128,1024]{1,0:T(8,128)(2,1)S(1)}, bf16[128,1024]{1,0:T(8,128)(2,1)S(1)}, u32[]{:S(2)}, u32[]{:S(2)}) collective-permute-start(bf16[128,1024]{1,0:T(8,128)(2,1)S(1)} %get-tuple-element.26.own), channel_id=1, source_target_pairs={{0,4},{6,2},{1,5},{7,3},{8,12},{14,10},{9,13},{15,11},{16,20},{22,... | collective-permute-start | bytes 786440 | tf_op jit(solution)/shard_map/ppermute | solution.py:112
  17.6 1.9 %collective-permute-start.3 = (bf16[128,1024]{1,0:T(8,128)(2,1)S(1)}, bf16[128,1024]{1,0:T(8,128)(2,1)S(1)}, u32[]{:S(2)}, u32[]{:S(2)}) collective-permute-start(bf16[128,1024]{1,0:T(8,128)(2,1)S(1)} %get-tuple-element.24), channel_id=1, source_target_pairs={{760,0},{10,2},{764,4},{14,6},{0,8},{18,10},{4,12},{22,14},{8,16},... | collective-permute-start | bytes 786440 | tf_op jit(solution)/shard_map/ppermute | solution.py:123
  19.5 0.0 collective-permute-done.own_far
  19.5 4.3 %collective-permute-done.4.af = bf16[128,1024]{1,0:T(8,128)(2,1)S(1)} collective-permute-done((bf16[128,1024]{1,0:T(8,128)(2,1)S(1)}, bf16[128,1024]{1,0:T(8,128)(2,1)S(1)}, u32[]{:S(2)}, u32[]{:S(2)}) %collective-permute-start.4) | collective-permute-done | bytes 262176 | tf_op jit(solution)/shard_map/ppermute | solution.py:112
  23.8 27.6 %collective-permute-done.3.y0 = bf16[128,1024]{1,0:T(8,128)(2,1)S(1)} collective-permute-done((bf16[128,1024]{1,0:T(8,128)(2,1)S(1)}, bf16[128,1024]{1,0:T(8,128)(2,1)S(1)}, u32[]{:S(2)}, u32[]{:S(2)}) %collective-permute-start.3) | collective-permute-done | bytes 262176 | tf_op jit(solution)/shard_map/ppermute | solution.py:123
  51.3 0.0 collective-permute-done.1.xe
  51.3 0.0 collective-permute-done.2.xo
  51.3 0.2 shard_map.59
  51.6 3.5 %collective-permute-start.6 = (bf16[384,1024]{1,0:T(8,128)(2,1)S(1)}, bf16[384,1024]{1,0:T(8,128)(2,1)S(1)}, u32[]{:S(2)}, u32[]{:S(2)}) collective-permute-start(bf16[384,1024]{1,0:T(8,128)(2,1)S(1)} %get-tuple-element.16.w1), channel_id=1, source_target_pairs={{0,1},{1,0},{2,3},{3,2},{4,5},{5,4},{6,7},{7,6},{8,9},{9,8},{10,11... | collective-permute-start | bytes 2359304 | tf_op jit(solution)/shard_map/ppermute | solution.py:115
  55.1 0.7 collective-permute-start.5
  55.8 1.3 %collective-permute-start.8 = (bf16[256,1024]{1,0:T(8,128)(2,1)S(1)}, bf16[256,1024]{1,0:T(8,128)(2,1)S(1)}, u32[]{:S(2)}, u32[]{:S(2)}) collective-permute-start(bf16[256,1024]{1,0:T(8,128)(2,1)S(1)} %get-tuple-element.19), channel_id=1, source_target_pairs={{0,4},{6,2},{1,5},{7,3},{8,12},{14,10},{9,13},{15,11},{16,20},{22,... | collective-permute-start | bytes 1572872 | tf_op jit(solution)/shard_map/ppermute | solution.py:112
  58.4 0.0 collective-permute-done.6.w1_far
  58.4 3.1 %shard_map.60.acc = f32[512,1024]{1,0:T(8,128)S(1)} custom-call(f32[1]{0:T(128)S(6)} %copy.6.scale, f32[1]{0:T(128)S(6)} %copy.7.bias, bf16[512,1024]{1,0:T(8,128)(2,1)S(1)} %get-tuple-element.13.left, bf16[256,1024]{1,0:T(8,128)(2,1)S(1)} %get-tuple-element.15.first, bf16[384,1024]{1,0:T(8,128)(2,1)S(1)} %get-tuple-element.16.w1, ...), custom_call_target="tpu_custom_call" | custom-call | flops 2147483648 | bytes 2097152 | tf_op jit(solution)/shard_map/pallas_call | solution.py:18
  61.6 0.0 collective-permute-done.5.y1
  61.6 1.9 %collective-permute-start.7 = (bf16[256,1024]{1,0:T(8,128)(2,1)S(1)}, bf16[256,1024]{1,0:T(8,128)(2,1)S(1)}, u32[]{:S(2)}, u32[]{:S(2)}) collective-permute-start(bf16[256,1024]{1,0:T(8,128)(2,1)S(1)} %collective-permute-done.5.y1), channel_id=1, source_target_pairs={{0,1},{1,0},{2,3},{3,2},{4,5},{5,4},{6,7},{7,6},{8,9},{9,8},{10,11... | collective-permute-start | bytes 1572872 | tf_op jit(solution)/shard_map/ppermute | solution.py:115
  63.5 5.1 %collective-permute-done.8.last = bf16[256,1024]{1,0:T(8,128)(2,1)S(1)} collective-permute-done((bf16[256,1024]{1,0:T(8,128)(2,1)S(1)}, bf16[256,1024]{1,0:T(8,128)(2,1)S(1)}, u32[]{:S(2)}, u32[]{:S(2)}) %collective-permute-start.8) | collective-permute-done | bytes 524320 | tf_op jit(solution)/shard_map/ppermute | solution.py:112
  68.6 2.5 %collective-permute-start.9 = (bf16[256,1024]{1,0:T(8,128)(2,1)S(1)}, bf16[256,1024]{1,0:T(8,128)(2,1)S(1)}, u32[]{:S(2)}, u32[]{:S(2)}) collective-permute-start(bf16[256,1024]{1,0:T(8,128)(2,1)S(1)} %collective-permute-done.8.last), channel_id=1, source_target_pairs={{0,1},{1,0},{2,3},{3,2},{4,5},{5,4},{6,7},{7,6},{8,9},{9,8},{10,11... | collective-permute-start | bytes 1572872 | tf_op jit(solution)/shard_map/ppermute | solution.py:115
  71.1 0.0 collective-permute-done.7.y1_far
  71.1 1.8 %shard_map.61.acc = f32[512,1024]{1,0:T(8,128)S(1)} custom-call(f32[1]{0:T(128)S(6)} %copy.6.scale, f32[1]{0:T(128)S(6)} %copy.7.bias, bf16[512,1024]{1,0:T(8,128)(2,1)S(1)} %get-tuple-element.13.left, bf16[256,1024]{1,0:T(8,128)(2,1)S(1)} %collective-permute-done.5.y1, bf16[256,1024]{1,0:T(8,128)(2,1)S(1)} %collective-permute-done.7.y1_far, ...), custom_call_target="tpu_custom_call" | custom-call | flops 1073741824 | bytes 2097152 | tf_op jit(solution)/shard_map/pallas_call | solution.py:18
  73.0 0.0 collective-permute-done.9.last_far
  73.0 1.3 %shard_map.63 = (bf16[128,1024]{1,0:T(8,128)(2,1)S(1)}, bf16[128,1024]{1,0:T(8,128)(2,1)S(1)}) custom-call(f32[1]{0:T(128)S(6)} %copy.6.scale, f32[1]{0:T(128)S(6)} %copy.7.bias, bf16[512,1024]{1,0:T(8,128)(2,1)S(1)} %get-tuple-element.13.left, f32[512,1024]{1,0:T(8,128)S(1)} %shard_map.61.acc, bf16[256,1024]{1,0:T(8,128)(2,1)S(1)} %collective-permute-done.8.last, ...), custom_call_target="tpu_custom_call" | custom-call | flops 536870912 | bytes 524288 | tf_op jit(solution)/shard_map/pallas_call | solution.py:18
  74.3 1.3 %collective-permute-start.10 = (bf16[128,1024]{1,0:T(8,128)(2,1)S(1)}, bf16[128,1024]{1,0:T(8,128)(2,1)S(1)}, u32[]{:S(2)}, u32[]{:S(2)}) collective-permute-start(bf16[128,1024]{1,0:T(8,128)(2,1)S(1)} %get-tuple-element.21), channel_id=1, source_target_pairs={{2,0},{4,6},{3,1},{5,7},{10,8},{12,14},{11,9},{13,15},{18,16},{20,... | collective-permute-start | bytes 786440 | tf_op jit(solution)/shard_map/ppermute | solution.py:112
  75.6 1.3 %collective-permute-start.12 = (bf16[128,1024]{1,0:T(8,128)(2,1)S(1)}, bf16[128,1024]{1,0:T(8,128)(2,1)S(1)}, u32[]{:S(2)}, u32[]{:S(2)}) collective-permute-start(bf16[128,1024]{1,0:T(8,128)(2,1)S(1)} %get-tuple-element.23), channel_id=1, source_target_pairs={{2,6},{4,0},{3,7},{5,1},{10,14},{12,8},{11,15},{13,9},{18,22},{20,... | collective-permute-start | bytes 786440 | tf_op jit(solution)/shard_map/ppermute | solution.py:112
  76.9 1.3 %shard_map.62 = (bf16[128,1024]{1,0:T(8,128)(2,1)S(1)}, bf16[128,1024]{1,0:T(8,128)(2,1)S(1)}) custom-call(f32[1]{0:T(128)S(6)} %copy.6.scale, f32[1]{0:T(128)S(6)} %copy.7.bias, bf16[512,1024]{1,0:T(8,128)(2,1)S(1)} %get-tuple-element.13.left, f32[512,1024]{1,0:T(8,128)S(1)} %shard_map.61.acc, bf16[256,1024]{1,0:T(8,128)(2,1)S(1)} %collective-permute-done.8.last, ...), custom_call_target="tpu_custom_call" | custom-call | flops 536870912 | bytes 524288 | tf_op jit(solution)/shard_map/pallas_call | solution.py:18
  78.2 0.7 collective-permute-start.11
  78.8 17.3 %collective-permute-done.10 = bf16[128,1024]{1,0:T(8,128)(2,1)S(1)} collective-permute-done((bf16[128,1024]{1,0:T(8,128)(2,1)S(1)}, bf16[128,1024]{1,0:T(8,128)(2,1)S(1)}, u32[]{:S(2)}, u32[]{:S(2)}) %collective-permute-start.10) | collective-permute-done | bytes 262176 | tf_op jit(solution)/shard_map/ppermute | solution.py:112
  96.2 0.0 collective-permute-done.12
  96.2 0.8 broadcast_select_fusion.3
  (2 shorter events, 0.0 us)
Async XLA Ops:
  1.8 49.6 %collective-permute-start.1 = (bf16[256,1024]{1,0:T(8,128)(2,1)S(1)}, bf16[256,1024]{1,0:T(8,128)(2,1)S(1)}, u32[]{:S(2)}, u32[]{:S(2)}) collective-permute-start(bf16[256,1024]{1,0:T(8,128)(2,1)S(1)} %pad_maximum_fusion), channel_id=1, source_target_pairs={{0,2},{6,4},{1,3},{7,5},{8,10},{14,12},{9,11},{15,13},{16,18},{22,... | collective-permute-start | bytes 1572872 | tf_op jit(solution)/shard_map/ppermute | solution.py:112
  6.6 44.7 %collective-permute-start.2 = (bf16[256,1024]{1,0:T(8,128)(2,1)S(1)}, bf16[256,1024]{1,0:T(8,128)(2,1)S(1)}, u32[]{:S(2)}, u32[]{:S(2)}) collective-permute-start(bf16[256,1024]{1,0:T(8,128)(2,1)S(1)} %pad_maximum_fusion), channel_id=1, source_target_pairs={{2,4},{4,2},{3,5},{5,3},{10,12},{12,10},{11,13},{13,11},{18,20},{2... | collective-permute-start | bytes 1572872 | tf_op jit(solution)/shard_map/ppermute | solution.py:112
  7.3 12.1 %collective-permute-start = (bf16[128,1024]{1,0:T(8,128)(2,1)S(1)}, bf16[128,1024]{1,0:T(8,128)(2,1)S(1)}, u32[]{:S(2)}, u32[]{:S(2)}) collective-permute-start(bf16[128,1024]{1,0:T(8,128)(2,1)S(1)} %get-tuple-element.26.own), channel_id=1, source_target_pairs={{0,1},{1,0},{2,3},{3,2},{4,5},{5,4},{6,7},{7,6},{8,9},{9,8},{10,11... | collective-permute-start | bytes 786440 | tf_op jit(solution)/shard_map/ppermute | solution.py:115
  16.2 7.5 %collective-permute-start.4 = (bf16[128,1024]{1,0:T(8,128)(2,1)S(1)}, bf16[128,1024]{1,0:T(8,128)(2,1)S(1)}, u32[]{:S(2)}, u32[]{:S(2)}) collective-permute-start(bf16[128,1024]{1,0:T(8,128)(2,1)S(1)} %get-tuple-element.26.own), channel_id=1, source_target_pairs={{0,4},{6,2},{1,5},{7,3},{8,12},{14,10},{9,13},{15,11},{16,20},{22,... | collective-permute-start | bytes 786440 | tf_op jit(solution)/shard_map/ppermute | solution.py:112
  17.6 33.8 %collective-permute-start.3 = (bf16[128,1024]{1,0:T(8,128)(2,1)S(1)}, bf16[128,1024]{1,0:T(8,128)(2,1)S(1)}, u32[]{:S(2)}, u32[]{:S(2)}) collective-permute-start(bf16[128,1024]{1,0:T(8,128)(2,1)S(1)} %get-tuple-element.24), channel_id=1, source_target_pairs={{760,0},{10,2},{764,4},{14,6},{0,8},{18,10},{4,12},{22,14},{8,16},... | collective-permute-start | bytes 786440 | tf_op jit(solution)/shard_map/ppermute | solution.py:123
  51.6 6.9 %collective-permute-start.6 = (bf16[384,1024]{1,0:T(8,128)(2,1)S(1)}, bf16[384,1024]{1,0:T(8,128)(2,1)S(1)}, u32[]{:S(2)}, u32[]{:S(2)}) collective-permute-start(bf16[384,1024]{1,0:T(8,128)(2,1)S(1)} %get-tuple-element.16.w1), channel_id=1, source_target_pairs={{0,1},{1,0},{2,3},{3,2},{4,5},{5,4},{6,7},{7,6},{8,9},{9,8},{10,11... | collective-permute-start | bytes 2359304 | tf_op jit(solution)/shard_map/ppermute | solution.py:115
  55.1 6.5 %collective-permute-start.5 = (bf16[256,1024]{1,0:T(8,128)(2,1)S(1)}, bf16[256,1024]{1,0:T(8,128)(2,1)S(1)}, u32[]{:S(2)}, u32[]{:S(2)}) collective-permute-start(bf16[256,1024]{1,0:T(8,128)(2,1)S(1)} %get-tuple-element.14), channel_id=1, source_target_pairs={{10,2},{764,4},{18,10},{4,12},{26,18},{12,20},{34,26},{20,28},{42,... | collective-permute-start | bytes 1572872 | tf_op jit(solution)/shard_map/ppermute | solution.py:123
  55.8 12.8 %collective-permute-start.8 = (bf16[256,1024]{1,0:T(8,128)(2,1)S(1)}, bf16[256,1024]{1,0:T(8,128)(2,1)S(1)}, u32[]{:S(2)}, u32[]{:S(2)}) collective-permute-start(bf16[256,1024]{1,0:T(8,128)(2,1)S(1)} %get-tuple-element.19), channel_id=1, source_target_pairs={{0,4},{6,2},{1,5},{7,3},{8,12},{14,10},{9,13},{15,11},{16,20},{22,... | collective-permute-start | bytes 1572872 | tf_op jit(solution)/shard_map/ppermute | solution.py:112
  61.6 9.6 %collective-permute-start.7 = (bf16[256,1024]{1,0:T(8,128)(2,1)S(1)}, bf16[256,1024]{1,0:T(8,128)(2,1)S(1)}, u32[]{:S(2)}, u32[]{:S(2)}) collective-permute-start(bf16[256,1024]{1,0:T(8,128)(2,1)S(1)} %collective-permute-done.5.y1), channel_id=1, source_target_pairs={{0,1},{1,0},{2,3},{3,2},{4,5},{5,4},{6,7},{7,6},{8,9},{9,8},{10,11... | collective-permute-start | bytes 1572872 | tf_op jit(solution)/shard_map/ppermute | solution.py:115
  68.6 4.4 %collective-permute-start.9 = (bf16[256,1024]{1,0:T(8,128)(2,1)S(1)}, bf16[256,1024]{1,0:T(8,128)(2,1)S(1)}, u32[]{:S(2)}, u32[]{:S(2)}) collective-permute-start(bf16[256,1024]{1,0:T(8,128)(2,1)S(1)} %collective-permute-done.8.last), channel_id=1, source_target_pairs={{0,1},{1,0},{2,3},{3,2},{4,5},{5,4},{6,7},{7,6},{8,9},{9,8},{10,11... | collective-permute-start | bytes 1572872 | tf_op jit(solution)/shard_map/ppermute | solution.py:115
  74.3 21.9 %collective-permute-start.10 = (bf16[128,1024]{1,0:T(8,128)(2,1)S(1)}, bf16[128,1024]{1,0:T(8,128)(2,1)S(1)}, u32[]{:S(2)}, u32[]{:S(2)}) collective-permute-start(bf16[128,1024]{1,0:T(8,128)(2,1)S(1)} %get-tuple-element.21), channel_id=1, source_target_pairs={{2,0},{4,6},{3,1},{5,7},{10,8},{12,14},{11,9},{13,15},{18,16},{20,... | collective-permute-start | bytes 786440 | tf_op jit(solution)/shard_map/ppermute | solution.py:112
  75.6 20.6 %collective-permute-start.12 = (bf16[128,1024]{1,0:T(8,128)(2,1)S(1)}, bf16[128,1024]{1,0:T(8,128)(2,1)S(1)}, u32[]{:S(2)}, u32[]{:S(2)}) collective-permute-start(bf16[128,1024]{1,0:T(8,128)(2,1)S(1)} %get-tuple-element.23), channel_id=1, source_target_pairs={{2,6},{4,0},{3,7},{5,1},{10,14},{12,8},{11,15},{13,9},{18,22},{20,... | collective-permute-start | bytes 786440 | tf_op jit(solution)/shard_map/ppermute | solution.py:112
  78.2 18.0 %collective-permute-start.11 = (bf16[128,1024]{1,0:T(8,128)(2,1)S(1)}, bf16[128,1024]{1,0:T(8,128)(2,1)S(1)}, u32[]{:S(2)}, u32[]{:S(2)}) collective-permute-start(bf16[128,1024]{1,0:T(8,128)(2,1)S(1)} %get-tuple-element.22), channel_id=1, source_target_pairs={{2,4},{4,2},{3,5},{5,3},{10,12},{12,10},{11,13},{13,11},{18,20},{2... | collective-permute-start | bytes 786440 | tf_op jit(solution)/shard_map/ppermute | solution.py:112

commit v3 on v2

v3 whole, which is shorter than its diff:
```python
import functools
import math

import jax
import jax.numpy as jnp
from jax import lax
from jax.experimental import pallas as pl
from jax.experimental.pallas import tpu as pltpu
from jax.sharding import Mesh, PartitionSpec as P

CHIPS = 4
CORES = 2
GROUPS = 3
LIMIT = 12 * 1024 * 1024


def in_vmem(kernel, shapes, *operands, flops=0, scalars=0, scratch=()):
    moved_bytes = sum(math.prod(s.shape) * s.dtype.itemsize for s in shapes)
    return pl.pallas_call(
        kernel,
        out_shape=shapes,
        in_specs=[pl.BlockSpec(memory_space=pltpu.SMEM)] * scalars
        + [pl.BlockSpec(memory_space=pltpu.VMEM)] * (len(operands) - scalars),
        out_specs=[pl.BlockSpec(memory_space=pltpu.VMEM)] * len(shapes),
        scratch_shapes=[pltpu.VMEM(s.shape, s.dtype) for s in scratch],
        compiler_params=pltpu.CompilerParams(vmem_limit_bytes=LIMIT),
        cost_estimate=pl.CostEstimate(flops=flops, bytes_accessed=moved_bytes, transcendentals=0),
    )(*operands)


def pack_kernel(rows, own, other, xe, xo, y0, to_near, to_last, w1):
    gathered(to_near, [(xe, 0, rows), (xo, 1, rows)])
    gathered(to_last, [(other, 0, rows), (y0, 0, rows)])
    gathered(w1, [(own, 0, rows), (xe, 0, rows), (xo, 1, rows)])


def slopes_of(scores, scale, bias, diagonal=None):
    scores = scores * scale + bias
    if diagonal is not None:
        scores = jnp.where(diagonal, -scores, scores)
    slopes = 1.0 / (1.0 + jnp.exp(-scores))
    if diagonal is not None:
        slopes = jnp.where(diagonal, -slopes, slopes)
    return slopes.astype(jnp.bfloat16)


def across(a, b):
    return lax.dot_general(a, b, (((1,), (1,)), ((), ())), preferred_element_type=jnp.float32)


def at_inner():
    chip = lax.axis_index("zl")
    return jnp.logical_or(chip == 1, chip == 2)


def at_border(group):
    chip, place = lax.axis_index("zl"), lax.rem(lax.axis_index("blk"), group)
    return jnp.logical_or(
        jnp.logical_and(place == group - 1, chip == 2), jnp.logical_and(place == 0, chip == 1)
    )


def gathered(buffer, pieces):
    row = 0
    for ref, part, rows in pieces:
        buffer[row : row + rows, :] = ref[part * rows : (part + 1) * rows, :]
        row += rows


def pairs_of(rows, *triples):
    return [(ref, part, rows) for near, far, part in triples for ref in (near, far)]


def accumulated(left, columns, total, scale, bias, matches=()):
    rows = left.shape[0]
    wide = 256
    for j in range(columns.shape[0] // wide):
        chunk = columns[j * wide : (j + 1) * wide, :]
        scores = across(left, chunk)
        diagonal = None
        starts = [row for row, number in matches if number == j]
        if starts:
            row = lax.broadcasted_iota(jnp.int32, scores.shape, 0)
            column = lax.broadcasted_iota(jnp.int32, scores.shape, 1)
            diagonal = jnp.logical_and(column == row - starts[0], column < wide // 2)
        term = jnp.dot(slopes_of(scores, scale, bias, diagonal), chunk, preferred_element_type=jnp.float32)
        total = term if total is None else total + term
    return total


def early_kernel(scale, bias, am, xe, xo, af, w1, w1_far, left, acc, columns):
    @pl.when(at_inner())
    def _():
        rows = am.shape[0]
        gathered(left, [(am, 0, rows), (xe, 1, rows), (xo, 0, rows), (af, 0, rows)])
        gathered(columns, pairs_of(rows, *((w1, w1_far, i) for i in range(3))))
        acc[...] = accumulated(left[...], columns, None, scale[0], bias[0], [(i * rows, i) for i in range(3)])


def second_pack_kernel(group, y1, last, y0, ka, kb, w2):
    rows = y0.shape[0]
    gathered(w2, [(y1, 0, 2 * rows), (last, 0, 2 * rows), (y0, 0, rows)])

    @pl.when(at_border(group))
    def _():
        gathered(w2.at[3 * rows :, :], [(kb, 0, rows), (ka, 0, rows)])


def late_kernel(parts, scale, bias, left, acc, w2, w2_far, out0, out1, columns):
    @pl.when(at_inner())
    def _():
        rows = out0.shape[0]
        gathered(columns, pairs_of(rows, *((w2, w2_far, i) for i in range(5))))
        for part, out in zip(parts, (out0, out1)):
            here = slice(part * rows, (part + 1) * rows)
            matches = [(0, 2)] if part == CHIPS - 1 else []
            total = accumulated(left[here, :], columns, acc[here, :], scale[0], bias[0], matches)
            out[...] = (scale[0] * total).astype(out.dtype)


def body(images, captions, scale, bias):
    rows, width = images.shape
    blocks = lax.axis_size("blk")
    chip = lax.axis_index("zl")
    low = chip < 2
    inner = jnp.logical_or(chip == 1, chip == 2)

    def line(array, pairs):
        return lax.ppermute(array, "zl", pairs)

    group = blocks // GROUPS
    def swapped(array):
        pairs = [(chip * CORES + core, chip * CORES + 1 - core) for chip in (1, 2) for core in (0, 1)]
        return lax.ppermute(array, ("zl", "core"), pairs)

    def swapped_at_border(array):
        pairs = []
        for p in range(0, blocks, group):
            for place in (p * CHIPS + 1, (p + group - 1) * CHIPS + 2):
                pairs += [(place * CORES, place * CORES + 1), (place * CORES + 1, place * CORES)]
        return lax.ppermute(array, ("blk", "zl", "core"), pairs)

    def neighbour(array):
        pairs = []
        for p in range(blocks):
            pairs.append((((p + 1) % blocks) * CHIPS + 2, p * CHIPS + 2))
            pairs.append((((p - 1) % blocks) * CHIPS + 1, p * CHIPS + 1))
        return lax.ppermute(array, ("blk", "zl"), pairs)

    def neighbour_in_group(array):
        pairs = []
        for p in range(blocks):
            start = p - p % group
            for k in range(CHIPS):
                q = start + (p - start + (-1 if k % 2 else 1)) % group
                pairs.append((q * CHIPS + k, p * CHIPS + k))
        return lax.ppermute(array, ("blk", "zl"), pairs)

    def across_groups(array, low_source, high_source):
        pairs = []
        for p in range(0, blocks, group):
            q = p + group - 1
            pairs.append((((q + group) % blocks) * CHIPS + low_source, q * CHIPS + 2))
            pairs.append((((p - group) % blocks) * CHIPS + high_source, p * CHIPS + 1))
        return lax.ppermute(array, ("blk", "zl"), pairs)

    f32 = functools.partial(jax.ShapeDtypeStruct, dtype=jnp.float32)
    b16 = functools.partial(jax.ShapeDtypeStruct, dtype=jnp.bfloat16)
    unit = 4 * rows * rows * width

    to_inner = [(0, 1), (3, 2)]
    between = [(1, 2), (2, 1)]
    to_far = [(0, 2), (3, 1)]

    own = jnp.where(low, images, captions)
    other = jnp.where(low, captions, images)
    both = jnp.concatenate([own, other])
    xe = line(both, to_inner)
    xo = line(both, between)
    af = line(own, to_far)
    y0 = neighbour_in_group(jnp.where(inner, own, other))

    to_near, to_last, w1 = in_vmem(
        functools.partial(pack_kernel, rows), [b16((n * rows, width)) for n in (2, 2, 3)], own, other, xe, xo, y0
    )
    af, y0, w1, to_near, to_last = lax.optimization_barrier((af, y0, w1, to_near, to_last))
    y1 = neighbour(to_near)
    ka = across_groups(y0, 2, 1)
    kb = across_groups(y0, 0, 3)
    last = line(to_last, to_far)
    w1_far = swapped(w1)
    left, acc = in_vmem(
        early_kernel, [b16((4 * rows, width)), f32((4 * rows, width))],
        scale, bias, other, xe, xo, af, w1, w1_far,
        flops=24 * unit, scalars=2, scratch=[b16((6 * rows, width))],
    )
    y1, last, ka, kb, acc = lax.optimization_barrier((y1, last, ka, kb, acc))
    (w2,) = in_vmem(
        functools.partial(second_pack_kernel, group), [b16((5 * rows, width))], y1, last, y0, ka, kb
    )
    w2_far = swapped(w2)
    oe, of = in_vmem(
        functools.partial(late_kernel, (1, 3)), [b16((rows, width))] * 2, scale, bias, left, acc, w2, w2_far,
        flops=20 * unit, scalars=2, scratch=[b16((10 * rows, width))],
    )
    om, oo = in_vmem(
        functools.partial(late_kernel, (0, 2)), [b16((rows, width))] * 2, scale, bias, left, acc, w2, w2_far,
        flops=20 * unit, scalars=2, scratch=[b16((10 * rows, width))],
    )

    to_end = line(oe, [(1, 0), (2, 3)])
    to_far_end = line(of, [(1, 3), (2, 0)])
    to_other = line(oo, between)
    own_result = jnp.where(inner, om, to_end)
    other_result = jnp.where(inner, to_other, to_far_end)
    return (jnp.where(low, other_result, own_result), jnp.where(low, own_result, other_result))


def solution(mesh):
    fine = Mesh(mesh.devices.reshape(-1, CHIPS, CORES), ("blk", "zl", "core"))
    rows = P(("blk", "zl", "core"), None)
    return jax.shard_map(
        body, mesh=fine, in_specs=(rows, rows, P(), P()), out_specs=(rows, rows), check_vma=False
    )
```

time: 97.5 us -> 93.4 us (0.958)
  the two profiles are of different devices: /device:TPU:1 before, /device:TPU:64 now
where the time goes in v3:
time: 93.4 us; the launch traced here: 93 us
  starting transfers between devices  45.8 us (49%)
  waiting for transfers between devices  34.2 us (37%)
  Pallas kernels  8.93 us (10%)
  between operations  2.12 us (2%)
  other arithmetic  1.97 us (2%)
    ppermute x7, starting transfers between devices, line(): return lax.ppermute(array, 'zl', pairs)  22.8 us
    ppermute x2, starting transfers between devices, across_groups(): return lax.ppermute(array, ('blk', 'zl'), pairs)  12.2 us
    ppermute x7, waiting for transfers between devices, line(): return lax.ppermute(array, 'zl', pairs)  10.5 us
    ppermute x2, waiting for transfers between devices, across_groups(): return lax.ppermute(array, ('blk', 'zl'), pairs)  9.42 us
    pallas_call x5, Pallas kernels, in_vmem(): pl.pallas_call(kernel, out_shape=shapes, in_specs=[pl.BlockSpec(memory_sp...  8.93 us
    ppermute x1, waiting for transfers between devices, neighbour_in_group(): return lax.ppermute(array, ('blk', 'zl'), pairs)  8.8 us
    ppermute x2, starting transfers between devices, swapped(): return lax.ppermute(array, ('zl', 'core'), pairs)  3.84 us
    ppermute x1, starting transfers between devices, neighbour_in_group(): return lax.ppermute(array, ('blk', 'zl'), pairs)  3.48 us
  transfers between devices with their start and end apart: 13, of which 7 were waited for; matrix products, arithmetic and copies ran while one was open for 0% of the time, Pallas kernels for 6%

profile of v3, /device:TPU:64, one launch (start us, length us, event | category | flops | bytes accessed | tf_op | source)
XLA Modules:
  0.0 93.0 jit_solution(8533491401437133189)
XLA Ops:
  0.6 1.1 %broadcast_select_fusion.2 = (bf16[128,1024]{1,0:T(8,128)(2,1)S(1)}, bf16[128,1024]{1,0:T(8,128)(2,1)S(1)}, bf16[128,1024]{1,0:T(8,128)(2,1)S(1)}) fusion(pred[]{:T(512)S(6)} %or.3, bf16[128,1024]{1,0:T(8,128)(2,1)} %param.4, bf16[128,1024]{1,0:T(8,128)(2,1)} %param.5, pred[]{:T(512)S(6)} %lt.3), kind=kLoop, calls=%fused_computation.3 | loop fusion | flops 393216 | bytes 1310722 | tf_op jit(solution)/shard_map/jit(_where)/select_n | solution.py:181
  1.8 1.3 %collective-permute-start = (bf16[256,1024]{1,0:T(8,128)(2,1)S(1)}, bf16[256,1024]{1,0:T(8,128)(2,1)S(1)}, u32[]{:S(2)}, u32[]{:S(2)}) collective-permute-start(bf16[256,1024]{1,0:T(8,128)(2,1)S(1)} %pad_maximum_fusion), channel_id=1, source_target_pairs={{0,2},{6,4},{1,3},{7,5},{8,10},{14,12},{9,11},{15,13},{16,18},{22,... | collective-permute-start | bytes 1572872 | tf_op jit(solution)/shard_map/ppermute | solution.py:129
  3.1 4.3 %collective-permute-start.1 = (bf16[256,1024]{1,0:T(8,128)(2,1)S(1)}, bf16[256,1024]{1,0:T(8,128)(2,1)S(1)}, u32[]{:S(2)}, u32[]{:S(2)}) collective-permute-start(bf16[256,1024]{1,0:T(8,128)(2,1)S(1)} %pad_maximum_fusion), channel_id=1, source_target_pairs={{2,4},{4,2},{3,5},{5,3},{10,12},{12,10},{11,13},{13,11},{18,20},{2... | collective-permute-start | bytes 1572872 | tf_op jit(solution)/shard_map/ppermute | solution.py:129
  7.4 3.5 %collective-permute-start.3 = (bf16[128,1024]{1,0:T(8,128)(2,1)S(1)}, bf16[128,1024]{1,0:T(8,128)(2,1)S(1)}, u32[]{:S(2)}, u32[]{:S(2)}) collective-permute-start(bf16[128,1024]{1,0:T(8,128)(2,1)S(1)} %get-tuple-element.40), channel_id=1, source_target_pairs={{8,0},{250,2},{12,4},{254,6},{16,8},{2,10},{20,12},{6,14},{24,16},... | collective-permute-start | bytes 786440 | tf_op jit(solution)/shard_map/ppermute | solution.py:157
  10.9 1.3 %collective-permute-start.2 = (bf16[128,1024]{1,0:T(8,128)(2,1)S(1)}, bf16[128,1024]{1,0:T(8,128)(2,1)S(1)}, u32[]{:S(2)}, u32[]{:S(2)}) collective-permute-start(bf16[128,1024]{1,0:T(8,128)(2,1)S(1)} %get-tuple-element.41.own), channel_id=1, source_target_pairs={{0,4},{6,2},{1,5},{7,3},{8,12},{14,10},{9,13},{15,11},{16,20},{22,... | collective-permute-start | bytes 786440 | tf_op jit(solution)/shard_map/ppermute | solution.py:129
  12.2 8.8 %collective-permute-done.3.y0 = bf16[128,1024]{1,0:T(8,128)(2,1)S(1)} collective-permute-done((bf16[128,1024]{1,0:T(8,128)(2,1)S(1)}, bf16[128,1024]{1,0:T(8,128)(2,1)S(1)}, u32[]{:S(2)}, u32[]{:S(2)}) %collective-permute-start.3) | collective-permute-done | bytes 262176 | tf_op jit(solution)/shard_map/ppermute | solution.py:157
  21.0 0.0 collective-permute-done.xe
  21.0 3.9 %collective-permute-done.1.xo = bf16[256,1024]{1,0:T(8,128)(2,1)S(1)} collective-permute-done((bf16[256,1024]{1,0:T(8,128)(2,1)S(1)}, bf16[256,1024]{1,0:T(8,128)(2,1)S(1)}, u32[]{:S(2)}, u32[]{:S(2)}) %collective-permute-start.1) | collective-permute-done | bytes 524320 | tf_op jit(solution)/shard_map/ppermute | solution.py:129
  24.9 0.1 shard_map.59
  25.0 0.0 collective-permute-done.2.af
  25.0 1.9 %collective-permute-start.4 = (bf16[384,1024]{1,0:T(8,128)(2,1)S(1)}, bf16[384,1024]{1,0:T(8,128)(2,1)S(1)}, u32[]{:S(2)}, u32[]{:S(2)}) collective-permute-start(bf16[384,1024]{1,0:T(8,128)(2,1)S(1)} %get-tuple-element.25.w1), channel_id=1, source_target_pairs={{2,3},{3,2},{4,5},{5,4},{10,11},{11,10},{12,13},{13,12},{18,19},{1... | collective-permute-start | bytes 2359304 | tf_op jit(solution)/shard_map/ppermute | solution.py:134
  26.9 3.5 %collective-permute-start.5 = (bf16[256,1024]{1,0:T(8,128)(2,1)S(1)}, bf16[256,1024]{1,0:T(8,128)(2,1)S(1)}, u32[]{:S(2)}, u32[]{:S(2)}) collective-permute-start(bf16[256,1024]{1,0:T(8,128)(2,1)S(1)} %get-tuple-element.27), channel_id=1, source_target_pairs={{12,4},{762,2},{20,12},{2,10},{28,20},{10,18},{36,28},{18,26},{44,... | collective-permute-start | bytes 1572872 | tf_op jit(solution)/shard_map/ppermute | solution.py:148
  30.4 1.3 %collective-permute-start.6 = (bf16[256,1024]{1,0:T(8,128)(2,1)S(1)}, bf16[256,1024]{1,0:T(8,128)(2,1)S(1)}, u32[]{:S(2)}, u32[]{:S(2)}) collective-permute-start(bf16[256,1024]{1,0:T(8,128)(2,1)S(1)} %get-tuple-element.28), channel_id=1, source_target_pairs={{0,4},{6,2},{1,5},{7,3},{8,12},{14,10},{9,13},{15,11},{16,20},{22,... | collective-permute-start | bytes 1572872 | tf_op jit(solution)/shard_map/ppermute | solution.py:129
  31.7 10.9 %collective-permute-start.7 = (bf16[128,1024]{1,0:T(8,128)(2,1)S(1)}, bf16[128,1024]{1,0:T(8,128)(2,1)S(1)}, u32[]{:S(2)}, u32[]{:S(2)}) collective-permute-start(bf16[128,1024]{1,0:T(8,128)(2,1)S(1)} %collective-permute-done.3.y0), channel_id=1, source_target_pairs={{508,252},{514,2},{764,508},{2,258},{252,764},{258,514},{509,253},... | collective-permute-start | bytes 786440 | tf_op jit(solution)/shard_map/ppermute | solution.py:165
  42.7 1.3 %collective-permute-start.8 = (bf16[128,1024]{1,0:T(8,128)(2,1)S(1)}, bf16[128,1024]{1,0:T(8,128)(2,1)S(1)}, u32[]{:S(2)}, u32[]{:S(2)}) collective-permute-start(bf16[128,1024]{1,0:T(8,128)(2,1)S(1)} %collective-permute-done.3.y0), channel_id=1, source_target_pairs={{504,252},{518,2},{760,508},{6,258},{248,764},{262,514},{505,253},... | collective-permute-start | bytes 786440 | tf_op jit(solution)/shard_map/ppermute | solution.py:165
  45.3 0.0 collective-permute-done.4.w1_far
  45.3 2.5 %shard_map.60 = (bf16[512,1024]{1,0:T(8,128)(2,1)S(1)}, f32[512,1024]{1,0:T(8,128)S(1)}) custom-call(f32[1]{0:T(128)S(6)} %copy.6.scale, f32[1]{0:T(128)S(6)} %copy.7.bias, bf16[128,1024]{1,0:T(8,128)(2,1)S(1)} %get-tuple-element.42.other.am, bf16[256,1024]{1,0:T(8,128)(2,1)S(1)} %collective-permute-done.xe, ...), custom_call_target="tpu_custom_call" | custom-call | flops 1610612736 | bytes 3145728 | tf_op jit(solution)/shard_map/pallas_call | solution.py:19
  47.7 3.9 %collective-permute-done.7.ka = bf16[128,1024]{1,0:T(8,128)(2,1)S(1)} collective-permute-done((bf16[128,1024]{1,0:T(8,128)(2,1)S(1)}, bf16[128,1024]{1,0:T(8,128)(2,1)S(1)}, u32[]{:S(2)}, u32[]{:S(2)}) %collective-permute-start.7) | collective-permute-done | bytes 262176 | tf_op jit(solution)/shard_map/ppermute | solution.py:165
  51.6 5.5 %collective-permute-done.8.kb = bf16[128,1024]{1,0:T(8,128)(2,1)S(1)} collective-permute-done((bf16[128,1024]{1,0:T(8,128)(2,1)S(1)}, bf16[128,1024]{1,0:T(8,128)(2,1)S(1)}, u32[]{:S(2)}, u32[]{:S(2)}) %collective-permute-start.8) | collective-permute-done | bytes 262176 | tf_op jit(solution)/shard_map/ppermute | solution.py:165
  57.2 2.4 %collective-permute-done.5.y1 = bf16[256,1024]{1,0:T(8,128)(2,1)S(1)} collective-permute-done((bf16[256,1024]{1,0:T(8,128)(2,1)S(1)}, bf16[256,1024]{1,0:T(8,128)(2,1)S(1)}, u32[]{:S(2)}, u32[]{:S(2)}) %collective-permute-start.5) | collective-permute-done | bytes 524320 | tf_op jit(solution)/shard_map/ppermute | solution.py:148
  59.6 0.0 collective-permute-done.6.last
  59.6 0.1 shard_map.61.w2
  59.7 1.9 %collective-permute-start.9 = (bf16[640,1024]{1,0:T(8,128)(2,1)S(1)}, bf16[640,1024]{1,0:T(8,128)(2,1)S(1)}, u32[]{:S(2)}, u32[]{:S(2)}) collective-permute-start(bf16[640,1024]{1,0:T(8,128)(2,1)S(1)} %shard_map.61.w2), channel_id=1, source_target_pairs={{2,3},{3,2},{4,5},{5,4},{10,11},{11,10},{12,13},{13,12},{18,19},{1... | collective-permute-start | bytes 3932168 | tf_op jit(solution)/shard_map/ppermute | solution.py:134
  61.7 3.0 %collective-permute-done.9.w2_far = bf16[640,1024]{1,0:T(8,128)(2,1)S(1)} collective-permute-done((bf16[640,1024]{1,0:T(8,128)(2,1)S(1)}, bf16[640,1024]{1,0:T(8,128)(2,1)S(1)}, u32[]{:S(2)}, u32[]{:S(2)}) %collective-permute-start.9) | collective-permute-done | bytes 1310752 | tf_op jit(solution)/shard_map/ppermute | solution.py:134
  64.7 3.1 %shard_map.63 = (bf16[128,1024]{1,0:T(8,128)(2,1)S(1)}, bf16[128,1024]{1,0:T(8,128)(2,1)S(1)}) custom-call(f32[1]{0:T(128)S(6)} %copy.6.scale, f32[1]{0:T(128)S(6)} %copy.7.bias, bf16[512,1024]{1,0:T(8,128)(2,1)S(1)} %get-tuple-element.26.left, f32[512,1024]{1,0:T(8,128)S(1)} %get-tuple-element.31.acc, bf16[640,1024]{1,0:T(8,128)(2,1)S(1)} %shard_map.61.w2, ...), custom_call_target="tpu_custom_call" | custom-call | flops 1342177280 | bytes 524288 | tf_op jit(solution)/shard_map/pallas_call | solution.py:19
  67.8 1.3 %collective-permute-start.11 = (bf16[128,1024]{1,0:T(8,128)(2,1)S(1)}, bf16[128,1024]{1,0:T(8,128)(2,1)S(1)}, u32[]{:S(2)}, u32[]{:S(2)}) collective-permute-start(bf16[128,1024]{1,0:T(8,128)(2,1)S(1)} %get-tuple-element.37), channel_id=1, source_target_pairs={{2,6},{4,0},{3,7},{5,1},{10,14},{12,8},{11,15},{13,9},{18,22},{20,... | collective-permute-start | bytes 786440 | tf_op jit(solution)/shard_map/ppermute | solution.py:129
  69.1 2.9 %collective-permute-start.12 = (bf16[128,1024]{1,0:T(8,128)(2,1)S(1)}, bf16[128,1024]{1,0:T(8,128)(2,1)S(1)}, u32[]{:S(2)}, u32[]{:S(2)}) collective-permute-start(bf16[128,1024]{1,0:T(8,128)(2,1)S(1)} %get-tuple-element.39), channel_id=1, source_target_pairs={{2,0},{4,6},{3,1},{5,7},{10,8},{12,14},{11,9},{13,15},{18,16},{20,... | collective-permute-start | bytes 786440 | tf_op jit(solution)/shard_map/ppermute | solution.py:129
  71.9 3.1 %shard_map.62 = (bf16[128,1024]{1,0:T(8,128)(2,1)S(1)}, bf16[128,1024]{1,0:T(8,128)(2,1)S(1)}) custom-call(f32[1]{0:T(128)S(6)} %copy.6.scale, f32[1]{0:T(128)S(6)} %copy.7.bias, bf16[512,1024]{1,0:T(8,128)(2,1)S(1)} %get-tuple-element.26.left, f32[512,1024]{1,0:T(8,128)S(1)} %get-tuple-element.31.acc, bf16[640,1024]{1,0:T(8,128)(2,1)S(1)} %shard_map.61.w2, ...), custom_call_target="tpu_custom_call" | custom-call | flops 1342177280 | bytes 524288 | tf_op jit(solution)/shard_map/pallas_call | solution.py:19
  75.1 10.5 %collective-permute-start.10 = (bf16[128,1024]{1,0:T(8,128)(2,1)S(1)}, bf16[128,1024]{1,0:T(8,128)(2,1)S(1)}, u32[]{:S(2)}, u32[]{:S(2)}) collective-permute-start(bf16[128,1024]{1,0:T(8,128)(2,1)S(1)} %get-tuple-element.36), channel_id=1, source_target_pairs={{2,4},{4,2},{3,5},{5,3},{10,12},{12,10},{11,13},{13,11},{18,20},{2... | collective-permute-start | bytes 786440 | tf_op jit(solution)/shard_map/ppermute | solution.py:129
  85.6 0.0 collective-permute-done.11
  85.6 6.6 %collective-permute-done.10 = bf16[128,1024]{1,0:T(8,128)(2,1)S(1)} collective-permute-done((bf16[128,1024]{1,0:T(8,128)(2,1)S(1)}, bf16[128,1024]{1,0:T(8,128)(2,1)S(1)}, u32[]{:S(2)}, u32[]{:S(2)}) %collective-permute-start.10) | collective-permute-done | bytes 262176 | tf_op jit(solution)/shard_map/ppermute | solution.py:129
  92.2 0.8 broadcast_select_fusion.3
  (2 shorter events, 0.0 us)
Async XLA Ops:
  1.8 19.2 %collective-permute-start = (bf16[256,1024]{1,0:T(8,128)(2,1)S(1)}, bf16[256,1024]{1,0:T(8,128)(2,1)S(1)}, u32[]{:S(2)}, u32[]{:S(2)}) collective-permute-start(bf16[256,1024]{1,0:T(8,128)(2,1)S(1)} %pad_maximum_fusion), channel_id=1, source_target_pairs={{0,2},{6,4},{1,3},{7,5},{8,10},{14,12},{9,11},{15,13},{16,18},{22,... | collective-permute-start | bytes 1572872 | tf_op jit(solution)/shard_map/ppermute | solution.py:129
  3.1 21.8 %collective-permute-start.1 = (bf16[256,1024]{1,0:T(8,128)(2,1)S(1)}, bf16[256,1024]{1,0:T(8,128)(2,1)S(1)}, u32[]{:S(2)}, u32[]{:S(2)}) collective-permute-start(bf16[256,1024]{1,0:T(8,128)(2,1)S(1)} %pad_maximum_fusion), channel_id=1, source_target_pairs={{2,4},{4,2},{3,5},{5,3},{10,12},{12,10},{11,13},{13,11},{18,20},{2... | collective-permute-start | bytes 1572872 | tf_op jit(solution)/shard_map/ppermute | solution.py:129
  7.4 13.6 %collective-permute-start.3 = (bf16[128,1024]{1,0:T(8,128)(2,1)S(1)}, bf16[128,1024]{1,0:T(8,128)(2,1)S(1)}, u32[]{:S(2)}, u32[]{:S(2)}) collective-permute-start(bf16[128,1024]{1,0:T(8,128)(2,1)S(1)} %get-tuple-element.40), channel_id=1, source_target_pairs={{8,0},{250,2},{12,4},{254,6},{16,8},{2,10},{20,12},{6,14},{24,16},... | collective-permute-start | bytes 786440 | tf_op jit(solution)/shard_map/ppermute | solution.py:157
  10.9 14.2 %collective-permute-start.2 = (bf16[128,1024]{1,0:T(8,128)(2,1)S(1)}, bf16[128,1024]{1,0:T(8,128)(2,1)S(1)}, u32[]{:S(2)}, u32[]{:S(2)}) collective-permute-start(bf16[128,1024]{1,0:T(8,128)(2,1)S(1)} %get-tuple-element.41.own), channel_id=1, source_target_pairs={{0,4},{6,2},{1,5},{7,3},{8,12},{14,10},{9,13},{15,11},{16,20},{22,... | collective-permute-start | bytes 786440 | tf_op jit(solution)/shard_map/ppermute | solution.py:129
  25.0 20.2 %collective-permute-start.4 = (bf16[384,1024]{1,0:T(8,128)(2,1)S(1)}, bf16[384,1024]{1,0:T(8,128)(2,1)S(1)}, u32[]{:S(2)}, u32[]{:S(2)}) collective-permute-start(bf16[384,1024]{1,0:T(8,128)(2,1)S(1)} %get-tuple-element.25.w1), channel_id=1, source_target_pairs={{2,3},{3,2},{4,5},{5,4},{10,11},{11,10},{12,13},{13,12},{18,19},{1... | collective-permute-start | bytes 2359304 | tf_op jit(solution)/shard_map/ppermute | solution.py:134
  26.9 32.6 %collective-permute-start.5 = (bf16[256,1024]{1,0:T(8,128)(2,1)S(1)}, bf16[256,1024]{1,0:T(8,128)(2,1)S(1)}, u32[]{:S(2)}, u32[]{:S(2)}) collective-permute-start(bf16[256,1024]{1,0:T(8,128)(2,1)S(1)} %get-tuple-element.27), channel_id=1, source_target_pairs={{12,4},{762,2},{20,12},{2,10},{28,20},{10,18},{36,28},{18,26},{44,... | collective-permute-start | bytes 1572872 | tf_op jit(solution)/shard_map/ppermute | solution.py:148
  30.4 29.2 %collective-permute-start.6 = (bf16[256,1024]{1,0:T(8,128)(2,1)S(1)}, bf16[256,1024]{1,0:T(8,128)(2,1)S(1)}, u32[]{:S(2)}, u32[]{:S(2)}) collective-permute-start(bf16[256,1024]{1,0:T(8,128)(2,1)S(1)} %get-tuple-element.28), channel_id=1, source_target_pairs={{0,4},{6,2},{1,5},{7,3},{8,12},{14,10},{9,13},{15,11},{16,20},{22,... | collective-permute-start | bytes 1572872 | tf_op jit(solution)/shard_map/ppermute | solution.py:129
  31.7 19.9 %collective-permute-start.7 = (bf16[128,1024]{1,0:T(8,128)(2,1)S(1)}, bf16[128,1024]{1,0:T(8,128)(2,1)S(1)}, u32[]{:S(2)}, u32[]{:S(2)}) collective-permute-start(bf16[128,1024]{1,0:T(8,128)(2,1)S(1)} %collective-permute-done.3.y0), channel_id=1, source_target_pairs={{508,252},{514,2},{764,508},{2,258},{252,764},{258,514},{509,253},... | collective-permute-start | bytes 786440 | tf_op jit(solution)/shard_map/ppermute | solution.py:165
  42.7 14.5 %collective-permute-start.8 = (bf16[128,1024]{1,0:T(8,128)(2,1)S(1)}, bf16[128,1024]{1,0:T(8,128)(2,1)S(1)}, u32[]{:S(2)}, u32[]{:S(2)}) collective-permute-start(bf16[128,1024]{1,0:T(8,128)(2,1)S(1)} %collective-permute-done.3.y0), channel_id=1, source_target_pairs={{504,252},{518,2},{760,508},{6,258},{248,764},{262,514},{505,253},... | collective-permute-start | bytes 786440 | tf_op jit(solution)/shard_map/ppermute | solution.py:165
  59.7 4.9 %collective-permute-start.9 = (bf16[640,1024]{1,0:T(8,128)(2,1)S(1)}, bf16[640,1024]{1,0:T(8,128)(2,1)S(1)}, u32[]{:S(2)}, u32[]{:S(2)}) collective-permute-start(bf16[640,1024]{1,0:T(8,128)(2,1)S(1)} %shard_map.61.w2), channel_id=1, source_target_pairs={{2,3},{3,2},{4,5},{5,4},{10,11},{11,10},{12,13},{13,12},{18,19},{1... | collective-permute-start | bytes 3932168 | tf_op jit(solution)/shard_map/ppermute | solution.py:134
  67.8 17.8 %collective-permute-start.11 = (bf16[128,1024]{1,0:T(8,128)(2,1)S(1)}, bf16[128,1024]{1,0:T(8,128)(2,1)S(1)}, u32[]{:S(2)}, u32[]{:S(2)}) collective-permute-start(bf16[128,1024]{1,0:T(8,128)(2,1)S(1)} %get-tuple-element.37), channel_id=1, source_target_pairs={{2,6},{4,0},{3,7},{5,1},{10,14},{12,8},{11,15},{13,9},{18,22},{20,... | collective-permute-start | bytes 786440 | tf_op jit(solution)/shard_map/ppermute | solution.py:129
  69.1 16.5 %collective-permute-start.12 = (bf16[128,1024]{1,0:T(8,128)(2,1)S(1)}, bf16[128,1024]{1,0:T(8,128)(2,1)S(1)}, u32[]{:S(2)}, u32[]{:S(2)}) collective-permute-start(bf16[128,1024]{1,0:T(8,128)(2,1)S(1)} %get-tuple-element.39), channel_id=1, source_target_pairs={{2,0},{4,6},{3,1},{5,7},{10,8},{12,14},{11,9},{13,15},{18,16},{20,... | collective-permute-start | bytes 786440 | tf_op jit(solution)/shard_map/ppermute | solution.py:129
  75.1 17.1 %collective-permute-start.10 = (bf16[128,1024]{1,0:T(8,128)(2,1)S(1)}, bf16[128,1024]{1,0:T(8,128)(2,1)S(1)}, u32[]{:S(2)}, u32[]{:S(2)}) collective-permute-start(bf16[128,1024]{1,0:T(8,128)(2,1)S(1)} %get-tuple-element.36), channel_id=1, source_target_pairs={{2,4},{4,2},{3,5},{5,3},{10,12},{12,10},{11,13},{13,11},{18,20},{2... | collective-permute-start | bytes 786440 | tf_op jit(solution)/shard_map/ppermute | solution.py:129

commit v4 on v3

--- a/solution.py
+++ b/solution.py
@@ -28,10 +28,9 @@
     )(*operands)
 
 
-def pack_kernel(rows, own, other, xe, xo, y0, to_near, to_last, w1):
+def pack_kernel(rows, other, xe, xo, y0, to_near, to_last):
     gathered(to_near, [(xe, 0, rows), (xo, 1, rows)])
     gathered(to_last, [(other, 0, rows), (y0, 0, rows)])
-    gathered(w1, [(own, 0, rows), (xe, 0, rows), (xo, 1, rows)])
 
 
 def slopes_of(scores, scale, bias, diagonal=None):
@@ -57,6 +56,14 @@
     chip, place = lax.axis_index("zl"), lax.rem(lax.axis_index("blk"), group)
     return jnp.logical_or(
         jnp.logical_and(place == group - 1, chip == 2), jnp.logical_and(place == 0, chip == 1)
+    )
+
+
+def at_late(group):
+    chip, block, blocks = lax.axis_index("zl"), lax.axis_index("blk"), lax.axis_size("blk")
+    upper = jnp.logical_and(lax.rem(block, group) == 0, block > 0)
+    return jnp.logical_or(
+        jnp.logical_and(block == blocks - 1, chip == 2), jnp.logical_and(upper, chip == 1)
     )
 
 
@@ -88,22 +95,26 @@
     return total
 
 
-def early_kernel(scale, bias, am, xe, xo, af, w1, w1_far, left, acc, columns):
+def early_kernel(scale, bias, am, xe, xo, af, own, own_far, w1, w1_far, left, acc, columns):
     @pl.when(at_inner())
     def _():
         rows = am.shape[0]
         gathered(left, [(am, 0, rows), (xe, 1, rows), (xo, 0, rows), (af, 0, rows)])
-        gathered(columns, pairs_of(rows, *((w1, w1_far, i) for i in range(3))))
+        gathered(columns, pairs_of(rows, (own, own_far, 0), (w1, w1_far, 0), (w1, w1_far, 1)))
         acc[...] = accumulated(left[...], columns, None, scale[0], bias[0], [(i * rows, i) for i in range(3)])
 
 
-def second_pack_kernel(group, y1, last, y0, ka, kb, w2):
+def second_pack_kernel(group, y1, y2, last, y0, ka, kb, w2):
     rows = y0.shape[0]
     gathered(w2, [(y1, 0, 2 * rows), (last, 0, 2 * rows), (y0, 0, rows)])
 
     @pl.when(at_border(group))
     def _():
         gathered(w2.at[3 * rows :, :], [(kb, 0, rows), (ka, 0, rows)])
+
+    @pl.when(at_late(group))
+    def _():
+        gathered(w2, [(y2, 0, 2 * rows)])
 
 
 def late_kernel(parts, scale, bias, left, acc, w2, w2_far, out0, out1, columns):
@@ -140,11 +151,13 @@
                 pairs += [(place * CORES, place * CORES + 1), (place * CORES + 1, place * CORES)]
         return lax.ppermute(array, ("blk", "zl", "core"), pairs)
 
-    def neighbour(array):
+    def neighbour(array, late):
         pairs = []
         for p in range(blocks):
-            pairs.append((((p + 1) % blocks) * CHIPS + 2, p * CHIPS + 2))
-            pairs.append((((p - 1) % blocks) * CHIPS + 1, p * CHIPS + 1))
+            if (p == blocks - 1) == late:
+                pairs.append((((p + 1) % blocks) * CHIPS + 2, p * CHIPS + 2))
+            if (p % group == 0 and p > 0) == late:
+                pairs.append((((p - 1) % blocks) * CHIPS + 1, p * CHIPS + 1))
         return lax.ppermute(array, ("blk", "zl"), pairs)
 
     def neighbour_in_group(array):
@@ -180,23 +193,26 @@
     af = line(own, to_far)
     y0 = neighbour_in_group(jnp.where(inner, own, other))
 
-    to_near, to_last, w1 = in_vmem(
-        functools.partial(pack_kernel, rows), [b16((n * rows, width)) for n in (2, 2, 3)], own, other, xe, xo, y0
-    )
-    af, y0, w1, to_near, to_last = lax.optimization_barrier((af, y0, w1, to_near, to_last))
-    y1 = neighbour(to_near)
+    own_far = swapped(own)
+    to_near, to_last = in_vmem(
+        functools.partial(pack_kernel, rows), [b16((2 * rows, width))] * 2, other, xe, xo, y0
+    )
+    af, own_far, y0, to_near, to_last = lax.optimization_barrier((af, own_far, y0, to_near, to_last))
+    y1 = neighbour(to_near, False)
+    last = line(to_last, to_far)
+    kb = across_groups(y0, 0, 3)
     ka = across_groups(y0, 2, 1)
-    kb = across_groups(y0, 0, 3)
-    last = line(to_last, to_far)
-    w1_far = swapped(w1)
+    y2 = neighbour(to_near, True)
+    w1_far = swapped(to_near)
     left, acc = in_vmem(
         early_kernel, [b16((4 * rows, width)), f32((4 * rows, width))],
-        scale, bias, other, xe, xo, af, w1, w1_far,
+        scale, bias, other, xe, xo, af, own, own_far, to_near, w1_far,
         flops=24 * unit, scalars=2, scratch=[b16((6 * rows, width))],
     )
-    y1, last, ka, kb, acc = lax.optimization_barrier((y1, last, ka, kb, acc))
+    y1, last, kb, ka, acc = lax.optimization_barrier((y1, last, kb, ka, acc))
+    y1, last, kb, ka, y2 = lax.optimization_barrier((y1, last, kb, ka, y2))
     (w2,) = in_vmem(
-        functools.partial(second_pack_kernel, group), [b16((5 * rows, width))], y1, last, y0, ka, kb
+        functools.partial(second_pack_kernel, group), [b16((5 * rows, width))], y1, y2, last, y0, ka, kb
     )
     w2_far = swapped(w2)
     oe, of = in_vmem(

time: 93.4 us -> 91.2 us (0.976)
  starting transfers between devices: 45.8 us -> 38.9 us
  waiting for transfers between devices: 34.2 us -> 38.8 us
    ppermute x7, starting transfers between devices: 22.8 us -> 12.7 us  [line(): return lax.ppermute(array, 'zl', pairs)]
    ppermute x1 -> x2, waiting for transfers between devices: 2.44 us -> 7.63 us  [neighbour(): return lax.ppermute(array, ('blk', 'zl'), pairs)]
    ppermute x1, waiting for transfers between devices: 8.8 us -> 6.87 us  [neighbour_in_group(): return lax.ppermute(array, ('blk', 'zl'), pairs)]
    ppermute x2 -> x3, starting transfers between devices: 3.84 us -> 5.76 us  [swapped(): return lax.ppermute(array, ('zl', 'core'), pairs)]
    ppermute x7, waiting for transfers between devices: 10.5 us -> 12.2 us  [line(): return lax.ppermute(array, 'zl', pairs)]
    ppermute x1 -> x2, starting transfers between devices: 3.48 us -> 4.18 us  [neighbour(): return lax.ppermute(array, ('blk', 'zl'), pairs)]
    ppermute x2 -> x3, waiting for transfers between devices: 3 us -> 3.01 us  [swapped(): return lax.ppermute(array, ('zl', 'core'), pairs)]
  transfers between devices with their start and end apart: 13 -> 15, of which waited for: 7 -> 7; matrix products, arithmetic and copies ran while one was open for 0% -> 0% of each run, Pallas kernels for 6% -> 6%
where the time goes in v4:
time: 91.2 us; the launch traced here: 90.7 us
  starting transfers between devices  38.9 us (43%)
  waiting for transfers between devices  38.8 us (43%)
  Pallas kernels  8.88 us (10%)
  between operations  2.14 us (2%)
  other arithmetic  1.97 us (2%)
    ppermute x2, starting transfers between devices, across_groups(): return lax.ppermute(array, ('blk', 'zl'), pairs)  12.8 us
    ppermute x7, starting transfers between devices, line(): return lax.ppermute(array, 'zl', pairs)  12.7 us
    ppermute x7, waiting for transfers between devices, line(): return lax.ppermute(array, 'zl', pairs)  12.2 us
    ppermute x2, waiting for transfers between devices, across_groups(): return lax.ppermute(array, ('blk', 'zl'), pairs)  9.03 us
    pallas_call x5, Pallas kernels, in_vmem(): pl.pallas_call(kernel, out_shape=shapes, in_specs=[pl.BlockSpec(memory_sp...  8.88 us
    ppermute x2, waiting for transfers between devices, neighbour(): return lax.ppermute(array, ('blk', 'zl'), pairs)  7.63 us
    ppermute x1, waiting for transfers between devices, neighbour_in_group(): return lax.ppermute(array, ('blk', 'zl'), pairs)  6.87 us
    ppermute x3, starting transfers between devices, swapped(): return lax.ppermute(array, ('zl', 'core'), pairs)  5.76 us
  transfers between devices with their start and end apart: 15, of which 7 were waited for; matrix products, arithmetic and copies ran while one was open for 0% of the time, Pallas kernels for 6%

profile of v4, /device:TPU:64, one launch (start us, length us, event | category | flops | bytes accessed | tf_op | source)
XLA Modules:
  0.0 90.7 jit_solution(11605904018575667517)
XLA Ops:
  0.6 1.1 %broadcast_select_fusion.2 = (bf16[128,1024]{1,0:T(8,128)(2,1)S(1)}, bf16[128,1024]{1,0:T(8,128)(2,1)S(1)}, bf16[128,1024]{1,0:T(8,128)(2,1)S(1)}) fusion(pred[]{:T(512)S(6)} %or.3, bf16[128,1024]{1,0:T(8,128)(2,1)} %param.4, bf16[128,1024]{1,0:T(8,128)(2,1)} %param.5, pred[]{:T(512)S(6)} %lt.3), kind=kLoop, calls=%fused_computation.3 | loop fusion | flops 393216 | bytes 1310722 | tf_op jit(solution)/shard_map/jit(_where)/select_n | solution.py:194
  1.8 1.3 %collective-permute-start = (bf16[256,1024]{1,0:T(8,128)(2,1)S(1)}, bf16[256,1024]{1,0:T(8,128)(2,1)S(1)}, u32[]{:S(2)}, u32[]{:S(2)}) collective-permute-start(bf16[256,1024]{1,0:T(8,128)(2,1)S(1)} %pad_maximum_fusion), channel_id=1, source_target_pairs={{0,2},{6,4},{1,3},{7,5},{8,10},{14,12},{9,11},{15,13},{16,18},{22,... | collective-permute-start | bytes 1572872 | tf_op jit(solution)/shard_map/ppermute | solution.py:140
  3.1 4.3 %collective-permute-start.1 = (bf16[256,1024]{1,0:T(8,128)(2,1)S(1)}, bf16[256,1024]{1,0:T(8,128)(2,1)S(1)}, u32[]{:S(2)}, u32[]{:S(2)}) collective-permute-start(bf16[256,1024]{1,0:T(8,128)(2,1)S(1)} %pad_maximum_fusion), channel_id=1, source_target_pairs={{2,4},{4,2},{3,5},{5,3},{10,12},{12,10},{11,13},{13,11},{18,20},{2... | collective-permute-start | bytes 1572872 | tf_op jit(solution)/shard_map/ppermute | solution.py:140
  7.4 3.5 %collective-permute-start.4 = (bf16[128,1024]{1,0:T(8,128)(2,1)S(1)}, bf16[128,1024]{1,0:T(8,128)(2,1)S(1)}, u32[]{:S(2)}, u32[]{:S(2)}) collective-permute-start(bf16[128,1024]{1,0:T(8,128)(2,1)S(1)} %get-tuple-element.48), channel_id=1, source_target_pairs={{8,0},{250,2},{12,4},{254,6},{16,8},{2,10},{20,12},{6,14},{24,16},... | collective-permute-start | bytes 786440 | tf_op jit(solution)/shard_map/ppermute | solution.py:170
  10.9 1.3 %collective-permute-start.2 = (bf16[128,1024]{1,0:T(8,128)(2,1)S(1)}, bf16[128,1024]{1,0:T(8,128)(2,1)S(1)}, u32[]{:S(2)}, u32[]{:S(2)}) collective-permute-start(bf16[128,1024]{1,0:T(8,128)(2,1)S(1)} %get-tuple-element.49.own), channel_id=1, source_target_pairs={{0,4},{6,2},{1,5},{7,3},{8,12},{14,10},{9,13},{15,11},{16,20},{22,... | collective-permute-start | bytes 786440 | tf_op jit(solution)/shard_map/ppermute | solution.py:140
  12.2 1.9 %collective-permute-start.3 = (bf16[128,1024]{1,0:T(8,128)(2,1)S(1)}, bf16[128,1024]{1,0:T(8,128)(2,1)S(1)}, u32[]{:S(2)}, u32[]{:S(2)}) collective-permute-start(bf16[128,1024]{1,0:T(8,128)(2,1)S(1)} %get-tuple-element.49.own), channel_id=1, source_target_pairs={{2,3},{3,2},{4,5},{5,4},{10,11},{11,10},{12,13},{13,12},{18,19},{1... | collective-permute-start | bytes 786440 | tf_op jit(solution)/shard_map/ppermute | solution.py:145
  14.1 6.9 %collective-permute-done.4.y0 = bf16[128,1024]{1,0:T(8,128)(2,1)S(1)} collective-permute-done((bf16[128,1024]{1,0:T(8,128)(2,1)S(1)}, bf16[128,1024]{1,0:T(8,128)(2,1)S(1)}, u32[]{:S(2)}, u32[]{:S(2)}) %collective-permute-start.4) | collective-permute-done | bytes 262176 | tf_op jit(solution)/shard_map/ppermute | solution.py:170
  21.0 0.0 collective-permute-done.xe
  21.0 3.9 %collective-permute-done.1.xo = bf16[256,1024]{1,0:T(8,128)(2,1)S(1)} collective-permute-done((bf16[256,1024]{1,0:T(8,128)(2,1)S(1)}, bf16[256,1024]{1,0:T(8,128)(2,1)S(1)}, u32[]{:S(2)}, u32[]{:S(2)}) %collective-permute-start.1) | collective-permute-done | bytes 524320 | tf_op jit(solution)/shard_map/ppermute | solution.py:140
  24.9 0.1 shard_map.59
  25.0 0.0 collective-permute-done.3.own_far
  25.0 1.9 %collective-permute-start.5 = (bf16[256,1024]{1,0:T(8,128)(2,1)S(1)}, bf16[256,1024]{1,0:T(8,128)(2,1)S(1)}, u32[]{:S(2)}, u32[]{:S(2)}) collective-permute-start(bf16[256,1024]{1,0:T(8,128)(2,1)S(1)} %get-tuple-element.29.w1), channel_id=1, source_target_pairs={{2,3},{3,2},{4,5},{5,4},{10,11},{11,10},{12,13},{13,12},{18,19},{1... | collective-permute-start | bytes 1572872 | tf_op jit(solution)/shard_map/ppermute | solution.py:145
  26.9 3.5 %collective-permute-start.6 = (bf16[256,1024]{1,0:T(8,128)(2,1)S(1)}, bf16[256,1024]{1,0:T(8,128)(2,1)S(1)}, u32[]{:S(2)}, u32[]{:S(2)}) collective-permute-start(bf16[256,1024]{1,0:T(8,128)(2,1)S(1)} %get-tuple-element.29.w1), channel_id=1, source_target_pairs={{12,4},{762,2},{20,12},{2,10},{28,20},{10,18},{36,28},{18,26},{44,... | collective-permute-start | bytes 1572872 | tf_op jit(solution)/shard_map/ppermute | solution.py:161
  30.4 1.3 %collective-permute-start.7 = (bf16[256,1024]{1,0:T(8,128)(2,1)S(1)}, bf16[256,1024]{1,0:T(8,128)(2,1)S(1)}, u32[]{:S(2)}, u32[]{:S(2)}) collective-permute-start(bf16[256,1024]{1,0:T(8,128)(2,1)S(1)} %get-tuple-element.31), channel_id=1, source_target_pairs={{0,4},{6,2},{1,5},{7,3},{8,12},{14,10},{9,13},{15,11},{16,20},{22,... | collective-permute-start | bytes 1572872 | tf_op jit(solution)/shard_map/ppermute | solution.py:140
  31.7 0.7 collective-permute-start.10
  32.4 1.3 %collective-permute-start.8 = (bf16[128,1024]{1,0:T(8,128)(2,1)S(1)}, bf16[128,1024]{1,0:T(8,128)(2,1)S(1)}, u32[]{:S(2)}, u32[]{:S(2)}) collective-permute-start(bf16[128,1024]{1,0:T(8,128)(2,1)S(1)} %collective-permute-done.4.y0), channel_id=1, source_target_pairs={{504,252},{518,2},{760,508},{6,258},{248,764},{262,514},{505,253},... | collective-permute-start | bytes 786440 | tf_op jit(solution)/shard_map/ppermute | solution.py:178
  33.7 0.0 collective-permute-done.5.w1_far
  33.7 11.5 %collective-permute-start.9 = (bf16[128,1024]{1,0:T(8,128)(2,1)S(1)}, bf16[128,1024]{1,0:T(8,128)(2,1)S(1)}, u32[]{:S(2)}, u32[]{:S(2)}) collective-permute-start(bf16[128,1024]{1,0:T(8,128)(2,1)S(1)} %collective-permute-done.4.y0), channel_id=1, source_target_pairs={{508,252},{514,2},{764,508},{2,258},{252,764},{258,514},{509,253},... | collective-permute-start | bytes 786440 | tf_op jit(solution)/shard_map/ppermute | solution.py:178
  46.6 2.5 %shard_map.60 = (bf16[512,1024]{1,0:T(8,128)(2,1)S(1)}, f32[512,1024]{1,0:T(8,128)S(1)}) custom-call(f32[1]{0:T(128)S(6)} %copy.6.scale, f32[1]{0:T(128)S(6)} %copy.7.bias, bf16[128,1024]{1,0:T(8,128)(2,1)S(1)} %get-tuple-element.50.other.am, bf16[256,1024]{1,0:T(8,128)(2,1)S(1)} %collective-permute-done.xe, ...), custom_call_target="tpu_custom_call" | custom-call | flops 1610612736 | bytes 3145728 | tf_op jit(solution)/shard_map/pallas_call | solution.py:19
  49.0 9.0 %collective-permute-done.8.kb = bf16[128,1024]{1,0:T(8,128)(2,1)S(1)} collective-permute-done((bf16[128,1024]{1,0:T(8,128)(2,1)S(1)}, bf16[128,1024]{1,0:T(8,128)(2,1)S(1)}, u32[]{:S(2)}, u32[]{:S(2)}) %collective-permute-start.8) | collective-permute-done | bytes 262176 | tf_op jit(solution)/shard_map/ppermute | solution.py:178
  58.1 7.6 %collective-permute-done.6.y1 = bf16[256,1024]{1,0:T(8,128)(2,1)S(1)} collective-permute-done((bf16[256,1024]{1,0:T(8,128)(2,1)S(1)}, bf16[256,1024]{1,0:T(8,128)(2,1)S(1)}, u32[]{:S(2)}, u32[]{:S(2)}) %collective-permute-start.6) | collective-permute-done | bytes 524320 | tf_op jit(solution)/shard_map/ppermute | solution.py:161
  65.7 0.1 shard_map.61.w2
  65.8 1.9 %collective-permute-start.11 = (bf16[640,1024]{1,0:T(8,128)(2,1)S(1)}, bf16[640,1024]{1,0:T(8,128)(2,1)S(1)}, u32[]{:S(2)}, u32[]{:S(2)}) collective-permute-start(bf16[640,1024]{1,0:T(8,128)(2,1)S(1)} %shard_map.61.w2), channel_id=1, source_target_pairs={{2,3},{3,2},{4,5},{5,4},{10,11},{11,10},{12,13},{13,12},{18,19},{1... | collective-permute-start | bytes 3932168 | tf_op jit(solution)/shard_map/ppermute | solution.py:145
  67.7 3.0 %collective-permute-done.11.w2_far = bf16[640,1024]{1,0:T(8,128)(2,1)S(1)} collective-permute-done((bf16[640,1024]{1,0:T(8,128)(2,1)S(1)}, bf16[640,1024]{1,0:T(8,128)(2,1)S(1)}, u32[]{:S(2)}, u32[]{:S(2)}) %collective-permute-start.11) | collective-permute-done | bytes 1310752 | tf_op jit(solution)/shard_map/ppermute | solution.py:145
  70.7 3.1 %shard_map.63 = (bf16[128,1024]{1,0:T(8,128)(2,1)S(1)}, bf16[128,1024]{1,0:T(8,128)(2,1)S(1)}) custom-call(f32[1]{0:T(128)S(6)} %copy.6.scale, f32[1]{0:T(128)S(6)} %copy.7.bias, bf16[512,1024]{1,0:T(8,128)(2,1)S(1)} %get-tuple-element.30.left, f32[512,1024]{1,0:T(8,128)S(1)} %get-tuple-element.34.acc, bf16[640,1024]{1,0:T(8,128)(2,1)S(1)} %shard_map.61.w2, ...), custom_call_target="tpu_custom_call" | custom-call | flops 1342177280 | bytes 524288 | tf_op jit(solution)/shard_map/pallas_call | solution.py:19
  73.9 1.3 %collective-permute-start.13 = (bf16[128,1024]{1,0:T(8,128)(2,1)S(1)}, bf16[128,1024]{1,0:T(8,128)(2,1)S(1)}, u32[]{:S(2)}, u32[]{:S(2)}) collective-permute-start(bf16[128,1024]{1,0:T(8,128)(2,1)S(1)} %get-tuple-element.45), channel_id=1, source_target_pairs={{2,6},{4,0},{3,7},{5,1},{10,14},{12,8},{11,15},{13,9},{18,22},{20,... | collective-permute-start | bytes 786440 | tf_op jit(solution)/shard_map/ppermute | solution.py:140
  75.2 1.3 %collective-permute-start.14 = (bf16[128,1024]{1,0:T(8,128)(2,1)S(1)}, bf16[128,1024]{1,0:T(8,128)(2,1)S(1)}, u32[]{:S(2)}, u32[]{:S(2)}) collective-permute-start(bf16[128,1024]{1,0:T(8,128)(2,1)S(1)} %get-tuple-element.47), channel_id=1, source_target_pairs={{2,0},{4,6},{3,1},{5,7},{10,8},{12,14},{11,9},{13,15},{18,16},{20,... | collective-permute-start | bytes 786440 | tf_op jit(solution)/shard_map/ppermute | solution.py:140
  76.5 3.1 %shard_map.62 = (bf16[128,1024]{1,0:T(8,128)(2,1)S(1)}, bf16[128,1024]{1,0:T(8,128)(2,1)S(1)}) custom-call(f32[1]{0:T(128)S(6)} %copy.6.scale, f32[1]{0:T(128)S(6)} %copy.7.bias, bf16[512,1024]{1,0:T(8,128)(2,1)S(1)} %get-tuple-element.30.left, f32[512,1024]{1,0:T(8,128)S(1)} %get-tuple-element.34.acc, bf16[640,1024]{1,0:T(8,128)(2,1)S(1)} %shard_map.61.w2, ...), custom_call_target="tpu_custom_call" | custom-call | flops 1342177280 | bytes 524288 | tf_op jit(solution)/shard_map/pallas_call | solution.py:19
  79.6 1.9 %collective-permute-start.12 = (bf16[128,1024]{1,0:T(8,128)(2,1)S(1)}, bf16[128,1024]{1,0:T(8,128)(2,1)S(1)}, u32[]{:S(2)}, u32[]{:S(2)}) collective-permute-start(bf16[128,1024]{1,0:T(8,128)(2,1)S(1)} %get-tuple-element.44), channel_id=1, source_target_pairs={{2,4},{4,2},{3,5},{5,3},{10,12},{12,10},{11,13},{13,11},{18,20},{2... | collective-permute-start | bytes 786440 | tf_op jit(solution)/shard_map/ppermute | solution.py:140
  81.6 1.7 %collective-permute-done.14 = bf16[128,1024]{1,0:T(8,128)(2,1)S(1)} collective-permute-done((bf16[128,1024]{1,0:T(8,128)(2,1)S(1)}, bf16[128,1024]{1,0:T(8,128)(2,1)S(1)}, u32[]{:S(2)}, u32[]{:S(2)}) %collective-permute-start.14) | collective-permute-done | bytes 262176 | tf_op jit(solution)/shard_map/ppermute | solution.py:140
  83.3 6.6 %collective-permute-done.12 = bf16[128,1024]{1,0:T(8,128)(2,1)S(1)} collective-permute-done((bf16[128,1024]{1,0:T(8,128)(2,1)S(1)}, bf16[128,1024]{1,0:T(8,128)(2,1)S(1)}, u32[]{:S(2)}, u32[]{:S(2)}) %collective-permute-start.12) | collective-permute-done | bytes 262176 | tf_op jit(solution)/shard_map/ppermute | solution.py:140
  89.9 0.8 broadcast_select_fusion.3
  (6 shorter events, 0.0 us)
Async XLA Ops:
  1.8 19.2 %collective-permute-start = (bf16[256,1024]{1,0:T(8,128)(2,1)S(1)}, bf16[256,1024]{1,0:T(8,128)(2,1)S(1)}, u32[]{:S(2)}, u32[]{:S(2)}) collective-permute-start(bf16[256,1024]{1,0:T(8,128)(2,1)S(1)} %pad_maximum_fusion), channel_id=1, source_target_pairs={{0,2},{6,4},{1,3},{7,5},{8,10},{14,12},{9,11},{15,13},{16,18},{22,... | collective-permute-start | bytes 1572872 | tf_op jit(solution)/shard_map/ppermute | solution.py:140
  3.1 21.8 %collective-permute-start.1 = (bf16[256,1024]{1,0:T(8,128)(2,1)S(1)}, bf16[256,1024]{1,0:T(8,128)(2,1)S(1)}, u32[]{:S(2)}, u32[]{:S(2)}) collective-permute-start(bf16[256,1024]{1,0:T(8,128)(2,1)S(1)} %pad_maximum_fusion), channel_id=1, source_target_pairs={{2,4},{4,2},{3,5},{5,3},{10,12},{12,10},{11,13},{13,11},{18,20},{2... | collective-permute-start | bytes 1572872 | tf_op jit(solution)/shard_map/ppermute | solution.py:140
  7.4 13.6 %collective-permute-start.4 = (bf16[128,1024]{1,0:T(8,128)(2,1)S(1)}, bf16[128,1024]{1,0:T(8,128)(2,1)S(1)}, u32[]{:S(2)}, u32[]{:S(2)}) collective-permute-start(bf16[128,1024]{1,0:T(8,128)(2,1)S(1)} %get-tuple-element.48), channel_id=1, source_target_pairs={{8,0},{250,2},{12,4},{254,6},{16,8},{2,10},{20,12},{6,14},{24,16},... | collective-permute-start | bytes 786440 | tf_op jit(solution)/shard_map/ppermute | solution.py:170
  10.9 14.1 %collective-permute-start.2 = (bf16[128,1024]{1,0:T(8,128)(2,1)S(1)}, bf16[128,1024]{1,0:T(8,128)(2,1)S(1)}, u32[]{:S(2)}, u32[]{:S(2)}) collective-permute-start(bf16[128,1024]{1,0:T(8,128)(2,1)S(1)} %get-tuple-element.49.own), channel_id=1, source_target_pairs={{0,4},{6,2},{1,5},{7,3},{8,12},{14,10},{9,13},{15,11},{16,20},{22,... | collective-permute-start | bytes 786440 | tf_op jit(solution)/shard_map/ppermute | solution.py:140
  12.2 12.8 %collective-permute-start.3 = (bf16[128,1024]{1,0:T(8,128)(2,1)S(1)}, bf16[128,1024]{1,0:T(8,128)(2,1)S(1)}, u32[]{:S(2)}, u32[]{:S(2)}) collective-permute-start(bf16[128,1024]{1,0:T(8,128)(2,1)S(1)} %get-tuple-element.49.own), channel_id=1, source_target_pairs={{2,3},{3,2},{4,5},{5,4},{10,11},{11,10},{12,13},{13,12},{18,19},{1... | collective-permute-start | bytes 786440 | tf_op jit(solution)/shard_map/ppermute | solution.py:145
  25.0 8.7 %collective-permute-start.5 = (bf16[256,1024]{1,0:T(8,128)(2,1)S(1)}, bf16[256,1024]{1,0:T(8,128)(2,1)S(1)}, u32[]{:S(2)}, u32[]{:S(2)}) collective-permute-start(bf16[256,1024]{1,0:T(8,128)(2,1)S(1)} %get-tuple-element.29.w1), channel_id=1, source_target_pairs={{2,3},{3,2},{4,5},{5,4},{10,11},{11,10},{12,13},{13,12},{18,19},{1... | collective-permute-start | bytes 1572872 | tf_op jit(solution)/shard_map/ppermute | solution.py:145
  26.9 38.8 %collective-permute-start.6 = (bf16[256,1024]{1,0:T(8,128)(2,1)S(1)}, bf16[256,1024]{1,0:T(8,128)(2,1)S(1)}, u32[]{:S(2)}, u32[]{:S(2)}) collective-permute-start(bf16[256,1024]{1,0:T(8,128)(2,1)S(1)} %get-tuple-element.29.w1), channel_id=1, source_target_pairs={{12,4},{762,2},{20,12},{2,10},{28,20},{10,18},{36,28},{18,26},{44,... | collective-permute-start | bytes 1572872 | tf_op jit(solution)/shard_map/ppermute | solution.py:161
  30.4 35.3 %collective-permute-start.7 = (bf16[256,1024]{1,0:T(8,128)(2,1)S(1)}, bf16[256,1024]{1,0:T(8,128)(2,1)S(1)}, u32[]{:S(2)}, u32[]{:S(2)}) collective-permute-start(bf16[256,1024]{1,0:T(8,128)(2,1)S(1)} %get-tuple-element.31), channel_id=1, source_target_pairs={{0,4},{6,2},{1,5},{7,3},{8,12},{14,10},{9,13},{15,11},{16,20},{22,... | collective-permute-start | bytes 1572872 | tf_op jit(solution)/shard_map/ppermute | solution.py:140
  31.7 34.0 %collective-permute-start.10 = (bf16[256,1024]{1,0:T(8,128)(2,1)S(1)}, bf16[256,1024]{1,0:T(8,128)(2,1)S(1)}, u32[]{:S(2)}, u32[]{:S(2)}) collective-permute-start(bf16[256,1024]{1,0:T(8,128)(2,1)S(1)} %get-tuple-element.29.w1), channel_id=1, source_target_pairs={{250,258},{506,514},{4,764},{251,259},{507,515},{5,765}} | collective-permute-start | bytes 1572872 | tf_op jit(solution)/shard_map/ppermute | solution.py:161
  32.4 25.6 %collective-permute-start.8 = (bf16[128,1024]{1,0:T(8,128)(2,1)S(1)}, bf16[128,1024]{1,0:T(8,128)(2,1)S(1)}, u32[]{:S(2)}, u32[]{:S(2)}) collective-permute-start(bf16[128,1024]{1,0:T(8,128)(2,1)S(1)} %collective-permute-done.4.y0), channel_id=1, source_target_pairs={{504,252},{518,2},{760,508},{6,258},{248,764},{262,514},{505,253},... | collective-permute-start | bytes 786440 | tf_op jit(solution)/shard_map/ppermute | solution.py:178
  33.7 24.3 %collective-permute-start.9 = (bf16[128,1024]{1,0:T(8,128)(2,1)S(1)}, bf16[128,1024]{1,0:T(8,128)(2,1)S(1)}, u32[]{:S(2)}, u32[]{:S(2)}) collective-permute-start(bf16[128,1024]{1,0:T(8,128)(2,1)S(1)} %collective-permute-done.4.y0), channel_id=1, source_target_pairs={{508,252},{514,2},{764,508},{2,258},{252,764},{258,514},{509,253},... | collective-permute-start | bytes 786440 | tf_op jit(solution)/shard_map/ppermute | solution.py:178
  65.8 4.9 %collective-permute-start.11 = (bf16[640,1024]{1,0:T(8,128)(2,1)S(1)}, bf16[640,1024]{1,0:T(8,128)(2,1)S(1)}, u32[]{:S(2)}, u32[]{:S(2)}) collective-permute-start(bf16[640,1024]{1,0:T(8,128)(2,1)S(1)} %shard_map.61.w2), channel_id=1, source_target_pairs={{2,3},{3,2},{4,5},{5,4},{10,11},{11,10},{12,13},{13,12},{18,19},{1... | collective-permute-start | bytes 3932168 | tf_op jit(solution)/shard_map/ppermute | solution.py:145
  73.9 7.7 %collective-permute-start.13 = (bf16[128,1024]{1,0:T(8,128)(2,1)S(1)}, bf16[128,1024]{1,0:T(8,128)(2,1)S(1)}, u32[]{:S(2)}, u32[]{:S(2)}) collective-permute-start(bf16[128,1024]{1,0:T(8,128)(2,1)S(1)} %get-tuple-element.45), channel_id=1, source_target_pairs={{2,6},{4,0},{3,7},{5,1},{10,14},{12,8},{11,15},{13,9},{18,22},{20,... | collective-permute-start | bytes 786440 | tf_op jit(solution)/shard_map/ppermute | solution.py:140
  75.2 8.1 %collective-permute-start.14 = (bf16[128,1024]{1,0:T(8,128)(2,1)S(1)}, bf16[128,1024]{1,0:T(8,128)(2,1)S(1)}, u32[]{:S(2)}, u32[]{:S(2)}) collective-permute-start(bf16[128,1024]{1,0:T(8,128)(2,1)S(1)} %get-tuple-element.47), channel_id=1, source_target_pairs={{2,0},{4,6},{3,1},{5,7},{10,8},{12,14},{11,9},{13,15},{18,16},{20,... | collective-permute-start | bytes 786440 | tf_op jit(solution)/shard_map/ppermute | solution.py:140
  79.6 10.2 %collective-permute-start.12 = (bf16[128,1024]{1,0:T(8,128)(2,1)S(1)}, bf16[128,1024]{1,0:T(8,128)(2,1)S(1)}, u32[]{:S(2)}, u32[]{:S(2)}) collective-permute-start(bf16[128,1024]{1,0:T(8,128)(2,1)S(1)} %get-tuple-element.44), channel_id=1, source_target_pairs={{2,4},{4,2},{3,5},{5,3},{10,12},{12,10},{11,13},{13,11},{18,20},{2... | collective-permute-start | bytes 786440 | tf_op jit(solution)/shard_map/ppermute | solution.py:140

commit v5 on v4

--- a/solution.py
+++ b/solution.py
@@ -117,16 +117,17 @@
         gathered(w2, [(y2, 0, 2 * rows)])
 
 
-def late_kernel(parts, scale, bias, left, acc, w2, w2_far, out0, out1, columns):
+def late_kernel(start, scale, bias, left, acc, w2, w2_far, *outs_and_columns):
     @pl.when(at_inner())
     def _():
-        rows = out0.shape[0]
+        *outs, columns = outs_and_columns
+        rows = outs[0].shape[0]
         gathered(columns, pairs_of(rows, *((w2, w2_far, i) for i in range(5))))
-        for part, out in zip(parts, (out0, out1)):
-            here = slice(part * rows, (part + 1) * rows)
-            matches = [(0, 2)] if part == CHIPS - 1 else []
-            total = accumulated(left[here, :], columns, acc[here, :], scale[0], bias[0], matches)
-            out[...] = (scale[0] * total).astype(out.dtype)
+        here = slice(start * rows, (start + len(outs)) * rows)
+        matches = [(0, 2)] if start == CHIPS - 1 else []
+        total = scale[0] * accumulated(left[here, :], columns, acc[here, :], scale[0], bias[0], matches)
+        for i, out in enumerate(outs):
+            out[...] = total[i * rows : (i + 1) * rows, :].astype(out.dtype)
 
 
 def body(images, captions, scale, bias):
@@ -215,17 +216,21 @@
         functools.partial(second_pack_kernel, group), [b16((5 * rows, width))], y1, y2, last, y0, ka, kb
     )
     w2_far = swapped(w2)
-    oe, of = in_vmem(
-        functools.partial(late_kernel, (1, 3)), [b16((rows, width))] * 2, scale, bias, left, acc, w2, w2_far,
+    (of,) = in_vmem(
+        functools.partial(late_kernel, 3), [b16((rows, width))] * 1, scale, bias, left, acc, w2, w2_far,
+        flops=10 * unit, scalars=2, scratch=[b16((10 * rows, width))],
+    )
+    oe, oo = in_vmem(
+        functools.partial(late_kernel, 1), [b16((rows, width))] * 2, scale, bias, left, acc, w2, w2_far,
         flops=20 * unit, scalars=2, scratch=[b16((10 * rows, width))],
     )
-    om, oo = in_vmem(
-        functools.partial(late_kernel, (0, 2)), [b16((rows, width))] * 2, scale, bias, left, acc, w2, w2_far,
-        flops=20 * unit, scalars=2, scratch=[b16((10 * rows, width))],
-    )
-
+    (om,) = in_vmem(
+        functools.partial(late_kernel, 0), [b16((rows, width))] * 1, scale, bias, left, acc, w2, w2_far,
+        flops=10 * unit, scalars=2, scratch=[b16((10 * rows, width))],
+    )
+
+    to_far_end = line(of, [(1, 3), (2, 0)])
     to_end = line(oe, [(1, 0), (2, 3)])
-    to_far_end = line(of, [(1, 3), (2, 0)])
     to_other = line(oo, between)
     own_result = jnp.where(inner, om, to_end)
     other_result = jnp.where(inner, to_other, to_far_end)

time: 91.2 us -> 89.8 us (0.985)
  the two profiles are of different devices: /device:TPU:64 before, /device:TPU:1 now
where the time goes in v5:
time: 89.8 us; the launch traced here: 89.3 us
  waiting for transfers between devices  50.7 us (56%)
  starting transfers between devices  34.3 us (38%)
  between operations  2.18 us (2%)
  other arithmetic  1.97 us (2%)
    ppermute x7, waiting for transfers between devices, line(): return lax.ppermute(array, 'zl', pairs)  50.7 us
    ppermute x7, starting transfers between devices, line(): return lax.ppermute(array, 'zl', pairs)  22.1 us
    ppermute x1, starting transfers between devices, neighbour_in_group(): return lax.ppermute(array, ('blk', 'zl'), pairs)  7.29 us
    ppermute x3, starting transfers between devices, swapped(): return lax.ppermute(array, ('zl', 'core'), pairs)  2.11 us
  transfers between devices with their start and end apart: 15, of which 4 were waited for; matrix products, arithmetic and copies ran while one was open for 0% of the time, Pallas kernels for 0%

profile of v5, /device:TPU:1, one launch (start us, length us, event | category | flops | bytes accessed | tf_op | source)
XLA Modules:
  0.0 89.3 jit_solution(12110887410912505460)
XLA Ops:
  0.6 1.1 %broadcast_select_fusion.2 = (bf16[128,1024]{1,0:T(8,128)(2,1)S(1)}, bf16[128,1024]{1,0:T(8,128)(2,1)S(1)}, bf16[128,1024]{1,0:T(8,128)(2,1)S(1)}) fusion(pred[]{:T(512)S(6)} %or.3, bf16[128,1024]{1,0:T(8,128)(2,1)} %param.4, bf16[128,1024]{1,0:T(8,128)(2,1)} %param.5, pred[]{:T(512)S(6)} %lt.3), kind=kLoop, calls=%fused_computation.3 | loop fusion | flops 393216 | bytes 1310722 | tf_op jit(solution)/shard_map/jit(_where)/select_n | solution.py:195
  1.8 4.9 %collective-permute-start = (bf16[256,1024]{1,0:T(8,128)(2,1)S(1)}, bf16[256,1024]{1,0:T(8,128)(2,1)S(1)}, u32[]{:S(2)}, u32[]{:S(2)}) collective-permute-start(bf16[256,1024]{1,0:T(8,128)(2,1)S(1)} %pad_maximum_fusion), channel_id=1, source_target_pairs={{0,2},{6,4},{1,3},{7,5},{8,10},{14,12},{9,11},{15,13},{16,18},{22,... | collective-permute-start | bytes 1572872 | tf_op jit(solution)/shard_map/ppermute | solution.py:141
  6.6 0.7 collective-permute-start.1
  7.3 7.3 %collective-permute-start.4 = (bf16[128,1024]{1,0:T(8,128)(2,1)S(1)}, bf16[128,1024]{1,0:T(8,128)(2,1)S(1)}, u32[]{:S(2)}, u32[]{:S(2)}) collective-permute-start(bf16[128,1024]{1,0:T(8,128)(2,1)S(1)} %get-tuple-element.44), channel_id=1, source_target_pairs={{8,0},{250,2},{12,4},{254,6},{16,8},{2,10},{20,12},{6,14},{24,16},... | collective-permute-start | bytes 786440 | tf_op jit(solution)/shard_map/ppermute | solution.py:171
  14.6 4.3 %collective-permute-start.2 = (bf16[128,1024]{1,0:T(8,128)(2,1)S(1)}, bf16[128,1024]{1,0:T(8,128)(2,1)S(1)}, u32[]{:S(2)}, u32[]{:S(2)}) collective-permute-start(bf16[128,1024]{1,0:T(8,128)(2,1)S(1)} %get-tuple-element.45.own), channel_id=1, source_target_pairs={{0,4},{6,2},{1,5},{7,3},{8,12},{14,10},{9,13},{15,11},{16,20},{22,... | collective-permute-start | bytes 786440 | tf_op jit(solution)/shard_map/ppermute | solution.py:141
  19.0 0.7 collective-permute-start.3
  19.6 0.0 collective-permute-done.4.y0
  19.7 0.0 collective-permute-done.xe
  19.7 0.0 collective-permute-done.1.xo
  19.7 0.1 shard_map.59
  19.8 4.8 %collective-permute-done.2.af = bf16[128,1024]{1,0:T(8,128)(2,1)S(1)} collective-permute-done((bf16[128,1024]{1,0:T(8,128)(2,1)S(1)}, bf16[128,1024]{1,0:T(8,128)(2,1)S(1)}, u32[]{:S(2)}, u32[]{:S(2)}) %collective-permute-start.2) | collective-permute-done | bytes 262176 | tf_op jit(solution)/shard_map/ppermute | solution.py:141
  24.5 0.0 collective-permute-done.3.own_far
  24.5 0.7 collective-permute-start.5
  25.2 0.7 collective-permute-start.6
  25.9 9.0 %collective-permute-start.7 = (bf16[256,1024]{1,0:T(8,128)(2,1)S(1)}, bf16[256,1024]{1,0:T(8,128)(2,1)S(1)}, u32[]{:S(2)}, u32[]{:S(2)}) collective-permute-start(bf16[256,1024]{1,0:T(8,128)(2,1)S(1)} %get-tuple-element.29), channel_id=1, source_target_pairs={{0,4},{6,2},{1,5},{7,3},{8,12},{14,10},{9,13},{15,11},{16,20},{22,... | collective-permute-start | bytes 1572872 | tf_op jit(solution)/shard_map/ppermute | solution.py:141
  34.9 0.7 collective-permute-start.10
  35.6 0.7 collective-permute-start.8
  36.3 0.0 collective-permute-done.5.w1_far
  36.3 0.7 collective-permute-start.9
  38.3 0.0 collective-permute-done.8.kb
  38.3 0.0 collective-permute-done.9.ka
  38.3 0.0 collective-permute-done.6.y1
  38.3 7.9 %collective-permute-done.7.last = bf16[256,1024]{1,0:T(8,128)(2,1)S(1)} collective-permute-done((bf16[256,1024]{1,0:T(8,128)(2,1)S(1)}, bf16[256,1024]{1,0:T(8,128)(2,1)S(1)}, u32[]{:S(2)}, u32[]{:S(2)}) %collective-permute-start.7) | collective-permute-done | bytes 524320 | tf_op jit(solution)/shard_map/ppermute | solution.py:141
  46.2 0.0 collective-permute-done.10.y2
  46.2 0.1 shard_map.61.w2
  46.3 0.7 collective-permute-start.11
  47.1 1.3 %collective-permute-start.13 = (bf16[128,1024]{1,0:T(8,128)(2,1)S(1)}, bf16[128,1024]{1,0:T(8,128)(2,1)S(1)}, u32[]{:S(2)}, u32[]{:S(2)}) collective-permute-start(bf16[128,1024]{1,0:T(8,128)(2,1)S(1)} %shard_map.63), channel_id=1, source_target_pairs={{2,6},{4,0},{3,7},{5,1},{10,14},{12,8},{11,15},{13,9},{18,22},{20,... | collective-permute-start | bytes 786440 | tf_op jit(solution)/shard_map/ppermute | solution.py:141
  48.4 0.7 collective-permute-start.12
  49.1 1.3 %collective-permute-start.14 = (bf16[128,1024]{1,0:T(8,128)(2,1)S(1)}, bf16[128,1024]{1,0:T(8,128)(2,1)S(1)}, u32[]{:S(2)}, u32[]{:S(2)}) collective-permute-start(bf16[128,1024]{1,0:T(8,128)(2,1)S(1)} %get-tuple-element.43), channel_id=1, source_target_pairs={{2,0},{4,6},{3,1},{5,7},{10,8},{12,14},{11,9},{13,15},{18,16},{20,... | collective-permute-start | bytes 786440 | tf_op jit(solution)/shard_map/ppermute | solution.py:141
  50.4 29.1 %collective-permute-done.13 = bf16[128,1024]{1,0:T(8,128)(2,1)S(1)} collective-permute-done((bf16[128,1024]{1,0:T(8,128)(2,1)S(1)}, bf16[128,1024]{1,0:T(8,128)(2,1)S(1)}, u32[]{:S(2)}, u32[]{:S(2)}) %collective-permute-start.13) | collective-permute-done | bytes 262176 | tf_op jit(solution)/shard_map/ppermute | solution.py:141
  79.6 8.9 %collective-permute-done.14 = bf16[128,1024]{1,0:T(8,128)(2,1)S(1)} collective-permute-done((bf16[128,1024]{1,0:T(8,128)(2,1)S(1)}, bf16[128,1024]{1,0:T(8,128)(2,1)S(1)}, u32[]{:S(2)}, u32[]{:S(2)}) %collective-permute-start.14) | collective-permute-done | bytes 262176 | tf_op jit(solution)/shard_map/ppermute | solution.py:141
  88.5 0.8 broadcast_select_fusion.3
  (7 shorter events, 0.1 us)
Async XLA Ops:
  1.8 17.9 %collective-permute-start = (bf16[256,1024]{1,0:T(8,128)(2,1)S(1)}, bf16[256,1024]{1,0:T(8,128)(2,1)S(1)}, u32[]{:S(2)}, u32[]{:S(2)}) collective-permute-start(bf16[256,1024]{1,0:T(8,128)(2,1)S(1)} %pad_maximum_fusion), channel_id=1, source_target_pairs={{0,2},{6,4},{1,3},{7,5},{8,10},{14,12},{9,11},{15,13},{16,18},{22,... | collective-permute-start | bytes 1572872 | tf_op jit(solution)/shard_map/ppermute | solution.py:141
  6.6 13.0 %collective-permute-start.1 = (bf16[256,1024]{1,0:T(8,128)(2,1)S(1)}, bf16[256,1024]{1,0:T(8,128)(2,1)S(1)}, u32[]{:S(2)}, u32[]{:S(2)}) collective-permute-start(bf16[256,1024]{1,0:T(8,128)(2,1)S(1)} %pad_maximum_fusion), channel_id=1, source_target_pairs={{2,4},{4,2},{3,5},{5,3},{10,12},{12,10},{11,13},{13,11},{18,20},{2... | collective-permute-start | bytes 1572872 | tf_op jit(solution)/shard_map/ppermute | solution.py:141
  7.3 12.3 %collective-permute-start.4 = (bf16[128,1024]{1,0:T(8,128)(2,1)S(1)}, bf16[128,1024]{1,0:T(8,128)(2,1)S(1)}, u32[]{:S(2)}, u32[]{:S(2)}) collective-permute-start(bf16[128,1024]{1,0:T(8,128)(2,1)S(1)} %get-tuple-element.44), channel_id=1, source_target_pairs={{8,0},{250,2},{12,4},{254,6},{16,8},{2,10},{20,12},{6,14},{24,16},... | collective-permute-start | bytes 786440 | tf_op jit(solution)/shard_map/ppermute | solution.py:171
  14.6 9.9 %collective-permute-start.2 = (bf16[128,1024]{1,0:T(8,128)(2,1)S(1)}, bf16[128,1024]{1,0:T(8,128)(2,1)S(1)}, u32[]{:S(2)}, u32[]{:S(2)}) collective-permute-start(bf16[128,1024]{1,0:T(8,128)(2,1)S(1)} %get-tuple-element.45.own), channel_id=1, source_target_pairs={{0,4},{6,2},{1,5},{7,3},{8,12},{14,10},{9,13},{15,11},{16,20},{22,... | collective-permute-start | bytes 786440 | tf_op jit(solution)/shard_map/ppermute | solution.py:141
  19.0 5.6 %collective-permute-start.3 = (bf16[128,1024]{1,0:T(8,128)(2,1)S(1)}, bf16[128,1024]{1,0:T(8,128)(2,1)S(1)}, u32[]{:S(2)}, u32[]{:S(2)}) collective-permute-start(bf16[128,1024]{1,0:T(8,128)(2,1)S(1)} %get-tuple-element.45.own), channel_id=1, source_target_pairs={{2,3},{3,2},{4,5},{5,4},{10,11},{11,10},{12,13},{13,12},{18,19},{1... | collective-permute-start | bytes 786440 | tf_op jit(solution)/shard_map/ppermute | solution.py:146
  24.5 11.8 %collective-permute-start.5 = (bf16[256,1024]{1,0:T(8,128)(2,1)S(1)}, bf16[256,1024]{1,0:T(8,128)(2,1)S(1)}, u32[]{:S(2)}, u32[]{:S(2)}) collective-permute-start(bf16[256,1024]{1,0:T(8,128)(2,1)S(1)} %get-tuple-element.27.w1), channel_id=1, source_target_pairs={{2,3},{3,2},{4,5},{5,4},{10,11},{11,10},{12,13},{13,12},{18,19},{1... | collective-permute-start | bytes 1572872 | tf_op jit(solution)/shard_map/ppermute | solution.py:146
  25.2 13.1 %collective-permute-start.6 = (bf16[256,1024]{1,0:T(8,128)(2,1)S(1)}, bf16[256,1024]{1,0:T(8,128)(2,1)S(1)}, u32[]{:S(2)}, u32[]{:S(2)}) collective-permute-start(bf16[256,1024]{1,0:T(8,128)(2,1)S(1)} %get-tuple-element.27.w1), channel_id=1, source_target_pairs={{12,4},{762,2},{20,12},{2,10},{28,20},{10,18},{36,28},{18,26},{44,... | collective-permute-start | bytes 1572872 | tf_op jit(solution)/shard_map/ppermute | solution.py:162
  25.9 20.3 %collective-permute-start.7 = (bf16[256,1024]{1,0:T(8,128)(2,1)S(1)}, bf16[256,1024]{1,0:T(8,128)(2,1)S(1)}, u32[]{:S(2)}, u32[]{:S(2)}) collective-permute-start(bf16[256,1024]{1,0:T(8,128)(2,1)S(1)} %get-tuple-element.29), channel_id=1, source_target_pairs={{0,4},{6,2},{1,5},{7,3},{8,12},{14,10},{9,13},{15,11},{16,20},{22,... | collective-permute-start | bytes 1572872 | tf_op jit(solution)/shard_map/ppermute | solution.py:141
  34.9 11.3 %collective-permute-start.10 = (bf16[256,1024]{1,0:T(8,128)(2,1)S(1)}, bf16[256,1024]{1,0:T(8,128)(2,1)S(1)}, u32[]{:S(2)}, u32[]{:S(2)}) collective-permute-start(bf16[256,1024]{1,0:T(8,128)(2,1)S(1)} %get-tuple-element.27.w1), channel_id=1, source_target_pairs={{250,258},{506,514},{4,764},{251,259},{507,515},{5,765}} | collective-permute-start | bytes 1572872 | tf_op jit(solution)/shard_map/ppermute | solution.py:162
  35.6 2.7 %collective-permute-start.8 = (bf16[128,1024]{1,0:T(8,128)(2,1)S(1)}, bf16[128,1024]{1,0:T(8,128)(2,1)S(1)}, u32[]{:S(2)}, u32[]{:S(2)}) collective-permute-start(bf16[128,1024]{1,0:T(8,128)(2,1)S(1)} %collective-permute-done.4.y0), channel_id=1, source_target_pairs={{504,252},{518,2},{760,508},{6,258},{248,764},{262,514},{505,253},... | collective-permute-start | bytes 786440 | tf_op jit(solution)/shard_map/ppermute | solution.py:179
  36.3 2.0 %collective-permute-start.9 = (bf16[128,1024]{1,0:T(8,128)(2,1)S(1)}, bf16[128,1024]{1,0:T(8,128)(2,1)S(1)}, u32[]{:S(2)}, u32[]{:S(2)}) collective-permute-start(bf16[128,1024]{1,0:T(8,128)(2,1)S(1)} %collective-permute-done.4.y0), channel_id=1, source_target_pairs={{508,252},{514,2},{764,508},{2,258},{252,764},{258,514},{509,253},... | collective-permute-start | bytes 786440 | tf_op jit(solution)/shard_map/ppermute | solution.py:179
  46.3 0.8 collective-permute-start.11
  47.1 32.5 %collective-permute-start.13 = (bf16[128,1024]{1,0:T(8,128)(2,1)S(1)}, bf16[128,1024]{1,0:T(8,128)(2,1)S(1)}, u32[]{:S(2)}, u32[]{:S(2)}) collective-permute-start(bf16[128,1024]{1,0:T(8,128)(2,1)S(1)} %shard_map.63), channel_id=1, source_target_pairs={{2,6},{4,0},{3,7},{5,1},{10,14},{12,8},{11,15},{13,9},{18,22},{20,... | collective-permute-start | bytes 786440 | tf_op jit(solution)/shard_map/ppermute | solution.py:141
  48.4 31.1 %collective-permute-start.12 = (bf16[128,1024]{1,0:T(8,128)(2,1)S(1)}, bf16[128,1024]{1,0:T(8,128)(2,1)S(1)}, u32[]{:S(2)}, u32[]{:S(2)}) collective-permute-start(bf16[128,1024]{1,0:T(8,128)(2,1)S(1)} %get-tuple-element.42), channel_id=1, source_target_pairs={{2,4},{4,2},{3,5},{5,3},{10,12},{12,10},{11,13},{13,11},{18,20},{2... | collective-permute-start | bytes 786440 | tf_op jit(solution)/shard_map/ppermute | solution.py:141
  49.1 39.4 %collective-permute-start.14 = (bf16[128,1024]{1,0:T(8,128)(2,1)S(1)}, bf16[128,1024]{1,0:T(8,128)(2,1)S(1)}, u32[]{:S(2)}, u32[]{:S(2)}) collective-permute-start(bf16[128,1024]{1,0:T(8,128)(2,1)S(1)} %get-tuple-element.43), channel_id=1, source_target_pairs={{2,0},{4,6},{3,1},{5,7},{10,8},{12,14},{11,9},{13,15},{18,16},{20,... | collective-permute-start | bytes 786440 | tf_op jit(solution)/shard_map/ppermute | solution.py:141

commit v6 on v5

--- a/solution.py
+++ b/solution.py
@@ -28,9 +28,15 @@
     )(*operands)
 
 
-def pack_kernel(rows, other, xe, xo, y0, to_near, to_last):
+def pack_kernel(group, other, xe, xo, af, y0, to_near, to_last, to_group):
+    rows = other.shape[0]
     gathered(to_near, [(xe, 0, rows), (xo, 1, rows)])
     gathered(to_last, [(other, 0, rows), (y0, 0, rows)])
+    to_group[...] = to_near[...]
+
+    @pl.when(sends_down(group))
+    def _():
+        gathered(to_group, [(af, 0, rows), (other, 0, rows)])
 
 
 def slopes_of(scores, scale, bias, diagonal=None):
@@ -59,11 +65,11 @@
     )
 
 
-def at_late(group):
+def sends_down(group):
     chip, block, blocks = lax.axis_index("zl"), lax.axis_index("blk"), lax.axis_size("blk")
-    upper = jnp.logical_and(lax.rem(block, group) == 0, block > 0)
+    lower = jnp.logical_and(lax.rem(block, group) == 0, block > 0)
     return jnp.logical_or(
-        jnp.logical_and(block == blocks - 1, chip == 2), jnp.logical_and(upper, chip == 1)
+        jnp.logical_and(block == blocks - 1, chip == 2), jnp.logical_and(lower, chip == 1)
     )
 
 
@@ -110,11 +116,8 @@
 
     @pl.when(at_border(group))
     def _():
+        gathered(w2, [(y2, 0, 2 * rows)])
         gathered(w2.at[3 * rows :, :], [(kb, 0, rows), (ka, 0, rows)])
-
-    @pl.when(at_late(group))
-    def _():
-        gathered(w2, [(y2, 0, 2 * rows)])
 
 
 def late_kernel(start, scale, bias, left, acc, w2, w2_far, *outs_and_columns):
@@ -152,13 +155,21 @@
                 pairs += [(place * CORES, place * CORES + 1), (place * CORES + 1, place * CORES)]
         return lax.ppermute(array, ("blk", "zl", "core"), pairs)
 
-    def neighbour(array, late):
+    def neighbour(array):
         pairs = []
         for p in range(blocks):
-            if (p == blocks - 1) == late:
-                pairs.append((((p + 1) % blocks) * CHIPS + 2, p * CHIPS + 2))
-            if (p % group == 0 and p > 0) == late:
-                pairs.append((((p - 1) % blocks) * CHIPS + 1, p * CHIPS + 1))
+            if (p + 1) % group:
+                pairs.append(((p + 1) * CHIPS + 2, p * CHIPS + 2))
+            if p % group:
+                pairs.append(((p - 1) * CHIPS + 1, p * CHIPS + 1))
+        return lax.ppermute(array, ("blk", "zl"), pairs)
+
+    def between_groups(array):
+        pairs = []
+        for p in range(group - 1, blocks, group):
+            q = (p + 1) % blocks
+            pairs.append((q * CHIPS + (1 if q else 2), p * CHIPS + 2))
+            pairs.append((p * CHIPS + (1 if q else 2), q * CHIPS + 1))
         return lax.ppermute(array, ("blk", "zl"), pairs)
 
     def neighbour_in_group(array):
@@ -195,15 +206,17 @@
     y0 = neighbour_in_group(jnp.where(inner, own, other))
 
     own_far = swapped(own)
-    to_near, to_last = in_vmem(
-        functools.partial(pack_kernel, rows), [b16((2 * rows, width))] * 2, other, xe, xo, y0
-    )
-    af, own_far, y0, to_near, to_last = lax.optimization_barrier((af, own_far, y0, to_near, to_last))
-    y1 = neighbour(to_near, False)
+    to_near, to_last, to_group = in_vmem(
+        functools.partial(pack_kernel, group), [b16((2 * rows, width))] * 3, other, xe, xo, af, y0
+    )
+    af, own_far, y0, to_near, to_last, to_group = lax.optimization_barrier(
+        (af, own_far, y0, to_near, to_last, to_group)
+    )
+    y1 = neighbour(to_near)
     last = line(to_last, to_far)
     kb = across_groups(y0, 0, 3)
     ka = across_groups(y0, 2, 1)
-    y2 = neighbour(to_near, True)
+    y2 = between_groups(to_group)
     w1_far = swapped(to_near)
     left, acc = in_vmem(
         early_kernel, [b16((4 * rows, width)), f32((4 * rows, width))],
@@ -232,6 +245,8 @@
     to_far_end = line(of, [(1, 3), (2, 0)])
     to_end = line(oe, [(1, 0), (2, 3)])
     to_other = line(oo, between)
+    to_end, to_far_end = lax.optimization_barrier((to_end, to_far_end))
+    to_end, to_other = lax.optimization_barrier((to_end, to_other))
     own_result = jnp.where(inner, om, to_end)
     other_result = jnp.where(inner, to_other, to_far_end)
     return (jnp.where(low, other_result, own_result), jnp.where(low, own_result, other_result))

time: 89.8 us -> 88.6 us (0.987)
  waiting for transfers between devices: 50.7 us -> 48.7 us
    ppermute x7, waiting for transfers between devices: 50.7 us -> 44.7 us  [line(): return lax.ppermute(array, 'zl', pairs)]
    ppermute x1, waiting for transfers between devices: 0.01 us -> 3.94 us  [neighbour_in_group(): return lax.ppermute(array, ('blk', 'zl'), pairs)]
where the time goes in v6:
time: 88.6 us; the launch traced here: 88.2 us
  waiting for transfers between devices  48.7 us (55%)
  starting transfers between devices  35.1 us (40%)
  between operations  2.17 us (2%)
  other arithmetic  1.97 us (2%)
    ppermute x7, waiting for transfers between devices, line(): return lax.ppermute(array, 'zl', pairs)  44.7 us
    ppermute x7, starting transfers between devices, line(): return lax.ppermute(array, 'zl', pairs)  22.9 us
    ppermute x1, starting transfers between devices, neighbour_in_group(): return lax.ppermute(array, ('blk', 'zl'), pairs)  7.29 us
    ppermute x1, waiting for transfers between devices, neighbour_in_group(): return lax.ppermute(array, ('blk', 'zl'), pairs)  3.94 us
    ppermute x3, starting transfers between devices, swapped(): return lax.ppermute(array, ('zl', 'core'), pairs)  2.12 us
  transfers between devices with their start and end apart: 15, of which 4 were waited for; matrix products, arithmetic and copies ran while one was open for 0% of the time, Pallas kernels for 0%

profile of v6, /device:TPU:1, one launch (start us, length us, event | category | flops | bytes accessed | tf_op | source)
XLA Modules:
  0.0 88.2 jit_solution(12732033133219697621)
XLA Ops:
  0.6 1.1 %broadcast_select_fusion.2 = (bf16[128,1024]{1,0:T(8,128)(2,1)S(1)}, bf16[128,1024]{1,0:T(8,128)(2,1)S(1)}, bf16[128,1024]{1,0:T(8,128)(2,1)S(1)}) fusion(pred[]{:T(512)S(6)} %or.3, bf16[128,1024]{1,0:T(8,128)(2,1)} %param.4, bf16[128,1024]{1,0:T(8,128)(2,1)} %param.5, pred[]{:T(512)S(6)} %lt.3), kind=kLoop, calls=%fused_computation.3 | loop fusion | flops 393216 | bytes 1310722 | tf_op jit(solution)/shard_map/jit(_where)/select_n | solution.py:206
  1.8 4.9 %collective-permute-start = (bf16[256,1024]{1,0:T(8,128)(2,1)S(1)}, bf16[256,1024]{1,0:T(8,128)(2,1)S(1)}, u32[]{:S(2)}, u32[]{:S(2)}) collective-permute-start(bf16[256,1024]{1,0:T(8,128)(2,1)S(1)} %pad_maximum_fusion), channel_id=1, source_target_pairs={{0,2},{6,4},{1,3},{7,5},{8,10},{14,12},{9,11},{15,13},{16,18},{22,... | collective-permute-start | bytes 1572872 | tf_op jit(solution)/shard_map/ppermute | solution.py:144
  6.6 0.7 collective-permute-start.1
  7.3 4.3 %collective-permute-start.2 = (bf16[128,1024]{1,0:T(8,128)(2,1)S(1)}, bf16[128,1024]{1,0:T(8,128)(2,1)S(1)}, u32[]{:S(2)}, u32[]{:S(2)}) collective-permute-start(bf16[128,1024]{1,0:T(8,128)(2,1)S(1)} %get-tuple-element.57.own), channel_id=1, source_target_pairs={{0,4},{6,2},{1,5},{7,3},{8,12},{14,10},{9,13},{15,11},{16,20},{22,... | collective-permute-start | bytes 786440 | tf_op jit(solution)/shard_map/ppermute | solution.py:144
  11.7 7.3 %collective-permute-start.4 = (bf16[128,1024]{1,0:T(8,128)(2,1)S(1)}, bf16[128,1024]{1,0:T(8,128)(2,1)S(1)}, u32[]{:S(2)}, u32[]{:S(2)}) collective-permute-start(bf16[128,1024]{1,0:T(8,128)(2,1)S(1)} %get-tuple-element.56), channel_id=1, source_target_pairs={{8,0},{250,2},{12,4},{254,6},{16,8},{2,10},{20,12},{6,14},{24,16},... | collective-permute-start | bytes 786440 | tf_op jit(solution)/shard_map/ppermute | solution.py:182
  19.0 0.7 collective-permute-start.3
  19.6 0.0 collective-permute-done.2.af
  19.7 3.9 %collective-permute-done.4.y0 = bf16[128,1024]{1,0:T(8,128)(2,1)S(1)} collective-permute-done((bf16[128,1024]{1,0:T(8,128)(2,1)S(1)}, bf16[128,1024]{1,0:T(8,128)(2,1)S(1)}, u32[]{:S(2)}, u32[]{:S(2)}) %collective-permute-start.4) | collective-permute-done | bytes 262176 | tf_op jit(solution)/shard_map/ppermute | solution.py:182
  23.6 0.0 collective-permute-done.xe
  23.6 0.0 collective-permute-done.1.xo
  23.6 0.1 shard_map.59
  23.7 0.0 collective-permute-done.3.own_far
  23.7 0.7 collective-permute-start.5
  24.4 0.7 collective-permute-start.6
  25.1 9.8 %collective-permute-start.7 = (bf16[256,1024]{1,0:T(8,128)(2,1)S(1)}, bf16[256,1024]{1,0:T(8,128)(2,1)S(1)}, u32[]{:S(2)}, u32[]{:S(2)}) collective-permute-start(bf16[256,1024]{1,0:T(8,128)(2,1)S(1)} %get-tuple-element.36), channel_id=1, source_target_pairs={{0,4},{6,2},{1,5},{7,3},{8,12},{14,10},{9,13},{15,11},{16,20},{22,... | collective-permute-start | bytes 1572872 | tf_op jit(solution)/shard_map/ppermute | solution.py:144
  34.9 0.7 collective-permute-start.10
  35.6 0.7 collective-permute-start.8
  36.3 0.0 collective-permute-done.5.w1_far
  36.3 0.7 collective-permute-start.9
  38.3 0.0 collective-permute-done.8.kb
  38.3 0.0 collective-permute-done.9.ka
  38.4 0.0 collective-permute-done.6.y1
  38.4 7.9 %collective-permute-done.7.last = bf16[256,1024]{1,0:T(8,128)(2,1)S(1)} collective-permute-done((bf16[256,1024]{1,0:T(8,128)(2,1)S(1)}, bf16[256,1024]{1,0:T(8,128)(2,1)S(1)}, u32[]{:S(2)}, u32[]{:S(2)}) %collective-permute-start.7) | collective-permute-done | bytes 524320 | tf_op jit(solution)/shard_map/ppermute | solution.py:144
  46.2 0.0 collective-permute-done.10.y2
  46.2 0.1 shard_map.61.w2
  46.3 0.7 collective-permute-start.11
  47.1 1.3 %collective-permute-start.13 = (bf16[128,1024]{1,0:T(8,128)(2,1)S(1)}, bf16[128,1024]{1,0:T(8,128)(2,1)S(1)}, u32[]{:S(2)}, u32[]{:S(2)}) collective-permute-start(bf16[128,1024]{1,0:T(8,128)(2,1)S(1)} %shard_map.63), channel_id=1, source_target_pairs={{2,6},{4,0},{3,7},{5,1},{10,14},{12,8},{11,15},{13,9},{18,22},{20,... | collective-permute-start | bytes 786440 | tf_op jit(solution)/shard_map/ppermute | solution.py:144
  48.4 1.3 %collective-permute-start.12 = (bf16[128,1024]{1,0:T(8,128)(2,1)S(1)}, bf16[128,1024]{1,0:T(8,128)(2,1)S(1)}, u32[]{:S(2)}, u32[]{:S(2)}) collective-permute-start(bf16[128,1024]{1,0:T(8,128)(2,1)S(1)} %get-tuple-element.50), channel_id=1, source_target_pairs={{2,0},{4,6},{3,1},{5,7},{10,8},{12,14},{11,9},{13,15},{18,16},{20,... | collective-permute-start | bytes 786440 | tf_op jit(solution)/shard_map/ppermute | solution.py:144
  49.7 0.7 collective-permute-start.14
  50.4 30.9 %collective-permute-done.13 = bf16[128,1024]{1,0:T(8,128)(2,1)S(1)} collective-permute-done((bf16[128,1024]{1,0:T(8,128)(2,1)S(1)}, bf16[128,1024]{1,0:T(8,128)(2,1)S(1)}, u32[]{:S(2)}, u32[]{:S(2)}) %collective-permute-start.13) | collective-permute-done | bytes 262176 | tf_op jit(solution)/shard_map/ppermute | solution.py:144
  81.3 6.0 %collective-permute-done.12 = bf16[128,1024]{1,0:T(8,128)(2,1)S(1)} collective-permute-done((bf16[128,1024]{1,0:T(8,128)(2,1)S(1)}, bf16[128,1024]{1,0:T(8,128)(2,1)S(1)}, u32[]{:S(2)}, u32[]{:S(2)}) %collective-permute-start.12) | collective-permute-done | bytes 262176 | tf_op jit(solution)/shard_map/ppermute | solution.py:144
  87.3 0.8 broadcast_select_fusion.3
  (7 shorter events, 0.1 us)
Async XLA Ops:
  1.8 21.8 %collective-permute-start = (bf16[256,1024]{1,0:T(8,128)(2,1)S(1)}, bf16[256,1024]{1,0:T(8,128)(2,1)S(1)}, u32[]{:S(2)}, u32[]{:S(2)}) collective-permute-start(bf16[256,1024]{1,0:T(8,128)(2,1)S(1)} %pad_maximum_fusion), channel_id=1, source_target_pairs={{0,2},{6,4},{1,3},{7,5},{8,10},{14,12},{9,11},{15,13},{16,18},{22,... | collective-permute-start | bytes 1572872 | tf_op jit(solution)/shard_map/ppermute | solution.py:144
  6.6 17.0 %collective-permute-start.1 = (bf16[256,1024]{1,0:T(8,128)(2,1)S(1)}, bf16[256,1024]{1,0:T(8,128)(2,1)S(1)}, u32[]{:S(2)}, u32[]{:S(2)}) collective-permute-start(bf16[256,1024]{1,0:T(8,128)(2,1)S(1)} %pad_maximum_fusion), channel_id=1, source_target_pairs={{2,4},{4,2},{3,5},{5,3},{10,12},{12,10},{11,13},{13,11},{18,20},{2... | collective-permute-start | bytes 1572872 | tf_op jit(solution)/shard_map/ppermute | solution.py:144
  7.3 12.3 %collective-permute-start.2 = (bf16[128,1024]{1,0:T(8,128)(2,1)S(1)}, bf16[128,1024]{1,0:T(8,128)(2,1)S(1)}, u32[]{:S(2)}, u32[]{:S(2)}) collective-permute-start(bf16[128,1024]{1,0:T(8,128)(2,1)S(1)} %get-tuple-element.57.own), channel_id=1, source_target_pairs={{0,4},{6,2},{1,5},{7,3},{8,12},{14,10},{9,13},{15,11},{16,20},{22,... | collective-permute-start | bytes 786440 | tf_op jit(solution)/shard_map/ppermute | solution.py:144
  11.7 11.9 %collective-permute-start.4 = (bf16[128,1024]{1,0:T(8,128)(2,1)S(1)}, bf16[128,1024]{1,0:T(8,128)(2,1)S(1)}, u32[]{:S(2)}, u32[]{:S(2)}) collective-permute-start(bf16[128,1024]{1,0:T(8,128)(2,1)S(1)} %get-tuple-element.56), channel_id=1, source_target_pairs={{8,0},{250,2},{12,4},{254,6},{16,8},{2,10},{20,12},{6,14},{24,16},... | collective-permute-start | bytes 786440 | tf_op jit(solution)/shard_map/ppermute | solution.py:182
  19.0 4.8 %collective-permute-start.3 = (bf16[128,1024]{1,0:T(8,128)(2,1)S(1)}, bf16[128,1024]{1,0:T(8,128)(2,1)S(1)}, u32[]{:S(2)}, u32[]{:S(2)}) collective-permute-start(bf16[128,1024]{1,0:T(8,128)(2,1)S(1)} %get-tuple-element.57.own), channel_id=1, source_target_pairs={{2,3},{3,2},{4,5},{5,4},{10,11},{11,10},{12,13},{13,12},{18,19},{1... | collective-permute-start | bytes 786440 | tf_op jit(solution)/shard_map/ppermute | solution.py:149
  23.7 12.6 %collective-permute-start.5 = (bf16[256,1024]{1,0:T(8,128)(2,1)S(1)}, bf16[256,1024]{1,0:T(8,128)(2,1)S(1)}, u32[]{:S(2)}, u32[]{:S(2)}) collective-permute-start(bf16[256,1024]{1,0:T(8,128)(2,1)S(1)} %get-tuple-element.34.w1), channel_id=1, source_target_pairs={{2,3},{3,2},{4,5},{5,4},{10,11},{11,10},{12,13},{13,12},{18,19},{1... | collective-permute-start | bytes 1572872 | tf_op jit(solution)/shard_map/ppermute | solution.py:149
  24.4 13.9 %collective-permute-start.6 = (bf16[256,1024]{1,0:T(8,128)(2,1)S(1)}, bf16[256,1024]{1,0:T(8,128)(2,1)S(1)}, u32[]{:S(2)}, u32[]{:S(2)}) collective-permute-start(bf16[256,1024]{1,0:T(8,128)(2,1)S(1)} %get-tuple-element.34.w1), channel_id=1, source_target_pairs={{12,4},{20,12},{2,10},{28,20},{10,18},{36,28},{18,26},{44,36},{26,... | collective-permute-start | bytes 1572872 | tf_op jit(solution)/shard_map/ppermute | solution.py:165
  25.1 21.1 %collective-permute-start.7 = (bf16[256,1024]{1,0:T(8,128)(2,1)S(1)}, bf16[256,1024]{1,0:T(8,128)(2,1)S(1)}, u32[]{:S(2)}, u32[]{:S(2)}) collective-permute-start(bf16[256,1024]{1,0:T(8,128)(2,1)S(1)} %get-tuple-element.36), channel_id=1, source_target_pairs={{0,4},{6,2},{1,5},{7,3},{8,12},{14,10},{9,13},{15,11},{16,20},{22,... | collective-permute-start | bytes 1572872 | tf_op jit(solution)/shard_map/ppermute | solution.py:144
  34.9 11.3 %collective-permute-start.10 = (bf16[256,1024]{1,0:T(8,128)(2,1)S(1)}, bf16[256,1024]{1,0:T(8,128)(2,1)S(1)}, u32[]{:S(2)}, u32[]{:S(2)}) collective-permute-start(bf16[256,1024]{1,0:T(8,128)(2,1)S(1)} %get-tuple-element.44), channel_id=1, source_target_pairs={{258,252},{250,258},{514,508},{506,514},{4,764},{764,2},{259,253},... | collective-permute-start | bytes 1572872 | tf_op jit(solution)/shard_map/ppermute | solution.py:173
  35.6 2.7 %collective-permute-start.8 = (bf16[128,1024]{1,0:T(8,128)(2,1)S(1)}, bf16[128,1024]{1,0:T(8,128)(2,1)S(1)}, u32[]{:S(2)}, u32[]{:S(2)}) collective-permute-start(bf16[128,1024]{1,0:T(8,128)(2,1)S(1)} %collective-permute-done.4.y0), channel_id=1, source_target_pairs={{504,252},{518,2},{760,508},{6,258},{248,764},{262,514},{505,253},... | collective-permute-start | bytes 786440 | tf_op jit(solution)/shard_map/ppermute | solution.py:190
  36.3 2.0 %collective-permute-start.9 = (bf16[128,1024]{1,0:T(8,128)(2,1)S(1)}, bf16[128,1024]{1,0:T(8,128)(2,1)S(1)}, u32[]{:S(2)}, u32[]{:S(2)}) collective-permute-start(bf16[128,1024]{1,0:T(8,128)(2,1)S(1)} %collective-permute-done.4.y0), channel_id=1, source_target_pairs={{508,252},{514,2},{764,508},{2,258},{252,764},{258,514},{509,253},... | collective-permute-start | bytes 786440 | tf_op jit(solution)/shard_map/ppermute | solution.py:190
  46.3 0.8 collective-permute-start.11
  47.1 34.2 %collective-permute-start.13 = (bf16[128,1024]{1,0:T(8,128)(2,1)S(1)}, bf16[128,1024]{1,0:T(8,128)(2,1)S(1)}, u32[]{:S(2)}, u32[]{:S(2)}) collective-permute-start(bf16[128,1024]{1,0:T(8,128)(2,1)S(1)} %shard_map.63), channel_id=1, source_target_pairs={{2,6},{4,0},{3,7},{5,1},{10,14},{12,8},{11,15},{13,9},{18,22},{20,... | collective-permute-start | bytes 786440 | tf_op jit(solution)/shard_map/ppermute | solution.py:144
  48.4 38.9 %collective-permute-start.12 = (bf16[128,1024]{1,0:T(8,128)(2,1)S(1)}, bf16[128,1024]{1,0:T(8,128)(2,1)S(1)}, u32[]{:S(2)}, u32[]{:S(2)}) collective-permute-start(bf16[128,1024]{1,0:T(8,128)(2,1)S(1)} %get-tuple-element.50), channel_id=1, source_target_pairs={{2,0},{4,6},{3,1},{5,7},{10,8},{12,14},{11,9},{13,15},{18,16},{20,... | collective-permute-start | bytes 786440 | tf_op jit(solution)/shard_map/ppermute | solution.py:144
  49.7 37.6 %collective-permute-start.14 = (bf16[128,1024]{1,0:T(8,128)(2,1)S(1)}, bf16[128,1024]{1,0:T(8,128)(2,1)S(1)}, u32[]{:S(2)}, u32[]{:S(2)}) collective-permute-start(bf16[128,1024]{1,0:T(8,128)(2,1)S(1)} %get-tuple-element.52), channel_id=1, source_target_pairs={{2,4},{4,2},{3,5},{5,3},{10,12},{12,10},{11,13},{13,11},{18,20},{2... | collective-permute-start | bytes 786440 | tf_op jit(solution)/shard_map/ppermute | solution.py:144

commit v7 on v6

--- a/solution.py
+++ b/solution.py
@@ -85,17 +85,17 @@
 
 
 def accumulated(left, columns, total, scale, bias, matches=()):
-    rows = left.shape[0]
     wide = 256
-    for j in range(columns.shape[0] // wide):
-        chunk = columns[j * wide : (j + 1) * wide, :]
+    for start in range(0, columns.shape[0], wide):
+        chunk = columns[start : min(start + wide, columns.shape[0]), :]
         scores = across(left, chunk)
         diagonal = None
-        starts = [row for row, number in matches if number == j]
-        if starts:
-            row = lax.broadcasted_iota(jnp.int32, scores.shape, 0)
-            column = lax.broadcasted_iota(jnp.int32, scores.shape, 1)
-            diagonal = jnp.logical_and(column == row - starts[0], column < wide // 2)
+        for first_row, first_column in matches:
+            if start <= first_column < start + wide:
+                row = lax.broadcasted_iota(jnp.int32, scores.shape, 0) - first_row
+                column = lax.broadcasted_iota(jnp.int32, scores.shape, 1) - (first_column - start)
+                inside = jnp.logical_and(column >= 0, column < wide // 2)
+                diagonal = jnp.logical_and(column == row, inside)
         term = jnp.dot(slopes_of(scores, scale, bias, diagonal), chunk, preferred_element_type=jnp.float32)
         total = term if total is None else total + term
     return total
@@ -107,7 +107,7 @@
         rows = am.shape[0]
         gathered(left, [(am, 0, rows), (xe, 1, rows), (xo, 0, rows), (af, 0, rows)])
         gathered(columns, pairs_of(rows, (own, own_far, 0), (w1, w1_far, 0), (w1, w1_far, 1)))
-        acc[...] = accumulated(left[...], columns, None, scale[0], bias[0], [(i * rows, i) for i in range(3)])
+        acc[...] = accumulated(left[...], columns, None, scale[0], bias[0], [(i * rows, 2 * i * rows) for i in range(3)])
 
 
 def second_pack_kernel(group, y1, y2, last, y0, ka, kb, w2):
@@ -120,15 +120,19 @@
         gathered(w2.at[3 * rows :, :], [(kb, 0, rows), (ka, 0, rows)])
 
 
-def late_kernel(start, scale, bias, left, acc, w2, w2_far, *outs_and_columns):
+def near_kernel(scale, bias, left, acc, w2, out):
     @pl.when(at_inner())
     def _():
-        *outs, columns = outs_and_columns
+        rows = left.shape[0] // CHIPS
+        out[...] = accumulated(left[...], w2, acc[...], scale[0], bias[0], [(3 * rows, 2 * rows)])
+
+
+def late_kernel(start, scale, bias, left, acc, w2_far, *outs):
+    @pl.when(at_inner())
+    def _():
         rows = outs[0].shape[0]
-        gathered(columns, pairs_of(rows, *((w2, w2_far, i) for i in range(5))))
         here = slice(start * rows, (start + len(outs)) * rows)
-        matches = [(0, 2)] if start == CHIPS - 1 else []
-        total = scale[0] * accumulated(left[here, :], columns, acc[here, :], scale[0], bias[0], matches)
+        total = scale[0] * accumulated(left[here, :], w2_far, acc[here, :], scale[0], bias[0])
         for i, out in enumerate(outs):
             out[...] = total[i * rows : (i + 1) * rows, :].astype(out.dtype)
 
@@ -229,17 +233,20 @@
         functools.partial(second_pack_kernel, group), [b16((5 * rows, width))], y1, y2, last, y0, ka, kb
     )
     w2_far = swapped(w2)
+    (acc,) = in_vmem(
+        near_kernel, [f32((4 * rows, width))], scale, bias, left, acc, w2, flops=20 * unit, scalars=2
+    )
     (of,) = in_vmem(
-        functools.partial(late_kernel, 3), [b16((rows, width))] * 1, scale, bias, left, acc, w2, w2_far,
-        flops=10 * unit, scalars=2, scratch=[b16((10 * rows, width))],
+        functools.partial(late_kernel, 3), [b16((rows, width))] * 1, scale, bias, left, acc, w2_far,
+        flops=5 * unit, scalars=2,
     )
     oe, oo = in_vmem(
-        functools.partial(late_kernel, 1), [b16((rows, width))] * 2, scale, bias, left, acc, w2, w2_far,
-        flops=20 * unit, scalars=2, scratch=[b16((10 * rows, width))],
+        functools.partial(late_kernel, 1), [b16((rows, width))] * 2, scale, bias, left, acc, w2_far,
+        flops=10 * unit, scalars=2,
     )
     (om,) = in_vmem(
-        functools.partial(late_kernel, 0), [b16((rows, width))] * 1, scale, bias, left, acc, w2, w2_far,
-        flops=10 * unit, scalars=2, scratch=[b16((10 * rows, width))],
+        functools.partial(late_kernel, 0), [b16((rows, width))] * 1, scale, bias, left, acc, w2_far,
+        flops=5 * unit, scalars=2,
     )
 
     to_far_end = line(of, [(1, 3), (2, 0)])

time: 88.6 us -> 88.3 us (level)
  no operation moved by 1% of the time
where the time goes in v7:
time: 88.3 us; the launch traced here: 87.8 us
  waiting for transfers between devices  48.3 us (55%)
  starting transfers between devices  35.1 us (40%)
  between operations  2.17 us (2%)
  other arithmetic  1.97 us (2%)
    ppermute x7, waiting for transfers between devices, line(): return lax.ppermute(array, 'zl', pairs)  44.4 us
    ppermute x7, starting transfers between devices, line(): return lax.ppermute(array, 'zl', pairs)  22.9 us
    ppermute x1, starting transfers between devices, neighbour_in_group(): return lax.ppermute(array, ('blk', 'zl'), pairs)  7.29 us
    ppermute x1, waiting for transfers between devices, neighbour_in_group(): return lax.ppermute(array, ('blk', 'zl'), pairs)  3.94 us
    ppermute x3, starting transfers between devices, swapped(): return lax.ppermute(array, ('zl', 'core'), pairs)  2.12 us
  transfers between devices with their start and end apart: 15, of which 4 were waited for; matrix products, arithmetic and copies ran while one was open for 0% of the time, Pallas kernels for 0%

profile of v7, /device:TPU:1, one launch (start us, length us, event | category | flops | bytes accessed | tf_op | source)
XLA Modules:
  0.0 87.8 jit_solution(12603736876168579620)
XLA Ops:
  0.6 1.1 %broadcast_select_fusion.2 = (bf16[128,1024]{1,0:T(8,128)(2,1)S(1)}, bf16[128,1024]{1,0:T(8,128)(2,1)S(1)}, bf16[128,1024]{1,0:T(8,128)(2,1)S(1)}) fusion(pred[]{:T(512)S(6)} %or.3, bf16[128,1024]{1,0:T(8,128)(2,1)} %param.4, bf16[128,1024]{1,0:T(8,128)(2,1)} %param.5, pred[]{:T(512)S(6)} %lt.3), kind=kLoop, calls=%fused_computation.3 | loop fusion | flops 393216 | bytes 1310722 | tf_op jit(solution)/shard_map/jit(_where)/select_n | solution.py:210
  1.8 4.9 %collective-permute-start = (bf16[256,1024]{1,0:T(8,128)(2,1)S(1)}, bf16[256,1024]{1,0:T(8,128)(2,1)S(1)}, u32[]{:S(2)}, u32[]{:S(2)}) collective-permute-start(bf16[256,1024]{1,0:T(8,128)(2,1)S(1)} %pad_maximum_fusion), channel_id=1, source_target_pairs={{0,2},{6,4},{1,3},{7,5},{8,10},{14,12},{9,11},{15,13},{16,18},{22,... | collective-permute-start | bytes 1572872 | tf_op jit(solution)/shard_map/ppermute | solution.py:148
  6.6 0.7 collective-permute-start.1
  7.3 4.3 %collective-permute-start.2 = (bf16[128,1024]{1,0:T(8,128)(2,1)S(1)}, bf16[128,1024]{1,0:T(8,128)(2,1)S(1)}, u32[]{:S(2)}, u32[]{:S(2)}) collective-permute-start(bf16[128,1024]{1,0:T(8,128)(2,1)S(1)} %get-tuple-element.57.own), channel_id=1, source_target_pairs={{0,4},{6,2},{1,5},{7,3},{8,12},{14,10},{9,13},{15,11},{16,20},{22,... | collective-permute-start | bytes 786440 | tf_op jit(solution)/shard_map/ppermute | solution.py:148
  11.7 7.3 %collective-permute-start.4 = (bf16[128,1024]{1,0:T(8,128)(2,1)S(1)}, bf16[128,1024]{1,0:T(8,128)(2,1)S(1)}, u32[]{:S(2)}, u32[]{:S(2)}) collective-permute-start(bf16[128,1024]{1,0:T(8,128)(2,1)S(1)} %get-tuple-element.56), channel_id=1, source_target_pairs={{8,0},{250,2},{12,4},{254,6},{16,8},{2,10},{20,12},{6,14},{24,16},... | collective-permute-start | bytes 786440 | tf_op jit(solution)/shard_map/ppermute | solution.py:186
  19.0 0.7 collective-permute-start.3
  19.6 0.0 collective-permute-done.2.af
  19.7 3.9 %collective-permute-done.4.y0 = bf16[128,1024]{1,0:T(8,128)(2,1)S(1)} collective-permute-done((bf16[128,1024]{1,0:T(8,128)(2,1)S(1)}, bf16[128,1024]{1,0:T(8,128)(2,1)S(1)}, u32[]{:S(2)}, u32[]{:S(2)}) %collective-permute-start.4) | collective-permute-done | bytes 262176 | tf_op jit(solution)/shard_map/ppermute | solution.py:186
  23.6 0.0 collective-permute-done.xe
  23.6 0.0 collective-permute-done.1.xo
  23.6 0.1 shard_map.59
  23.7 0.0 collective-permute-done.3.own_far
  23.7 0.7 collective-permute-start.5
  24.4 0.7 collective-permute-start.6
  25.1 9.8 %collective-permute-start.7 = (bf16[256,1024]{1,0:T(8,128)(2,1)S(1)}, bf16[256,1024]{1,0:T(8,128)(2,1)S(1)}, u32[]{:S(2)}, u32[]{:S(2)}) collective-permute-start(bf16[256,1024]{1,0:T(8,128)(2,1)S(1)} %get-tuple-element.36), channel_id=1, source_target_pairs={{0,4},{6,2},{1,5},{7,3},{8,12},{14,10},{9,13},{15,11},{16,20},{22,... | collective-permute-start | bytes 1572872 | tf_op jit(solution)/shard_map/ppermute | solution.py:148
  34.9 0.7 collective-permute-start.10
  35.6 0.7 collective-permute-start.8
  36.3 0.0 collective-permute-done.5.w1_far
  36.3 0.7 collective-permute-start.9
  38.3 0.0 collective-permute-done.8.kb
  38.3 0.0 collective-permute-done.9.ka
  38.4 7.9 %collective-permute-done.7.last = bf16[256,1024]{1,0:T(8,128)(2,1)S(1)} collective-permute-done((bf16[256,1024]{1,0:T(8,128)(2,1)S(1)}, bf16[256,1024]{1,0:T(8,128)(2,1)S(1)}, u32[]{:S(2)}, u32[]{:S(2)}) %collective-permute-start.7) | collective-permute-done | bytes 524320 | tf_op jit(solution)/shard_map/ppermute | solution.py:148
  46.2 0.0 collective-permute-done.10.y2
  46.2 0.1 shard_map.61.w2
  46.3 0.7 collective-permute-start.11
  47.1 0.0 collective-permute-done.11.w2_far
  47.1 1.3 %collective-permute-start.13 = (bf16[128,1024]{1,0:T(8,128)(2,1)S(1)}, bf16[128,1024]{1,0:T(8,128)(2,1)S(1)}, u32[]{:S(2)}, u32[]{:S(2)}) collective-permute-start(bf16[128,1024]{1,0:T(8,128)(2,1)S(1)} %shard_map.64), channel_id=1, source_target_pairs={{2,6},{4,0},{3,7},{5,1},{10,14},{12,8},{11,15},{13,9},{18,22},{20,... | collective-permute-start | bytes 786440 | tf_op jit(solution)/shard_map/ppermute | solution.py:148
  48.5 1.3 %collective-permute-start.12 = (bf16[128,1024]{1,0:T(8,128)(2,1)S(1)}, bf16[128,1024]{1,0:T(8,128)(2,1)S(1)}, u32[]{:S(2)}, u32[]{:S(2)}) collective-permute-start(bf16[128,1024]{1,0:T(8,128)(2,1)S(1)} %get-tuple-element.50), channel_id=1, source_target_pairs={{2,0},{4,6},{3,1},{5,7},{10,8},{12,14},{11,9},{13,15},{18,16},{20,... | collective-permute-start | bytes 786440 | tf_op jit(solution)/shard_map/ppermute | solution.py:148
  49.8 0.7 collective-permute-start.14
  50.5 30.5 %collective-permute-done.13 = bf16[128,1024]{1,0:T(8,128)(2,1)S(1)} collective-permute-done((bf16[128,1024]{1,0:T(8,128)(2,1)S(1)}, bf16[128,1024]{1,0:T(8,128)(2,1)S(1)}, u32[]{:S(2)}, u32[]{:S(2)}) %collective-permute-start.13) | collective-permute-done | bytes 262176 | tf_op jit(solution)/shard_map/ppermute | solution.py:148
  81.0 6.0 %collective-permute-done.12 = bf16[128,1024]{1,0:T(8,128)(2,1)S(1)} collective-permute-done((bf16[128,1024]{1,0:T(8,128)(2,1)S(1)}, bf16[128,1024]{1,0:T(8,128)(2,1)S(1)}, u32[]{:S(2)}, u32[]{:S(2)}) %collective-permute-start.12) | collective-permute-done | bytes 262176 | tf_op jit(solution)/shard_map/ppermute | solution.py:148
  87.0 0.8 broadcast_select_fusion.3
  (8 shorter events, 0.1 us)
Async XLA Ops:
  1.8 21.8 %collective-permute-start = (bf16[256,1024]{1,0:T(8,128)(2,1)S(1)}, bf16[256,1024]{1,0:T(8,128)(2,1)S(1)}, u32[]{:S(2)}, u32[]{:S(2)}) collective-permute-start(bf16[256,1024]{1,0:T(8,128)(2,1)S(1)} %pad_maximum_fusion), channel_id=1, source_target_pairs={{0,2},{6,4},{1,3},{7,5},{8,10},{14,12},{9,11},{15,13},{16,18},{22,... | collective-permute-start | bytes 1572872 | tf_op jit(solution)/shard_map/ppermute | solution.py:148
  6.6 17.0 %collective-permute-start.1 = (bf16[256,1024]{1,0:T(8,128)(2,1)S(1)}, bf16[256,1024]{1,0:T(8,128)(2,1)S(1)}, u32[]{:S(2)}, u32[]{:S(2)}) collective-permute-start(bf16[256,1024]{1,0:T(8,128)(2,1)S(1)} %pad_maximum_fusion), channel_id=1, source_target_pairs={{2,4},{4,2},{3,5},{5,3},{10,12},{12,10},{11,13},{13,11},{18,20},{2... | collective-permute-start | bytes 1572872 | tf_op jit(solution)/shard_map/ppermute | solution.py:148
  7.3 12.3 %collective-permute-start.2 = (bf16[128,1024]{1,0:T(8,128)(2,1)S(1)}, bf16[128,1024]{1,0:T(8,128)(2,1)S(1)}, u32[]{:S(2)}, u32[]{:S(2)}) collective-permute-start(bf16[128,1024]{1,0:T(8,128)(2,1)S(1)} %get-tuple-element.57.own), channel_id=1, source_target_pairs={{0,4},{6,2},{1,5},{7,3},{8,12},{14,10},{9,13},{15,11},{16,20},{22,... | collective-permute-start | bytes 786440 | tf_op jit(solution)/shard_map/ppermute | solution.py:148
  11.7 11.9 %collective-permute-start.4 = (bf16[128,1024]{1,0:T(8,128)(2,1)S(1)}, bf16[128,1024]{1,0:T(8,128)(2,1)S(1)}, u32[]{:S(2)}, u32[]{:S(2)}) collective-permute-start(bf16[128,1024]{1,0:T(8,128)(2,1)S(1)} %get-tuple-element.56), channel_id=1, source_target_pairs={{8,0},{250,2},{12,4},{254,6},{16,8},{2,10},{20,12},{6,14},{24,16},... | collective-permute-start | bytes 786440 | tf_op jit(solution)/shard_map/ppermute | solution.py:186
  19.0 4.8 %collective-permute-start.3 = (bf16[128,1024]{1,0:T(8,128)(2,1)S(1)}, bf16[128,1024]{1,0:T(8,128)(2,1)S(1)}, u32[]{:S(2)}, u32[]{:S(2)}) collective-permute-start(bf16[128,1024]{1,0:T(8,128)(2,1)S(1)} %get-tuple-element.57.own), channel_id=1, source_target_pairs={{2,3},{3,2},{4,5},{5,4},{10,11},{11,10},{12,13},{13,12},{18,19},{1... | collective-permute-start | bytes 786440 | tf_op jit(solution)/shard_map/ppermute | solution.py:153
  23.7 12.6 %collective-permute-start.5 = (bf16[256,1024]{1,0:T(8,128)(2,1)S(1)}, bf16[256,1024]{1,0:T(8,128)(2,1)S(1)}, u32[]{:S(2)}, u32[]{:S(2)}) collective-permute-start(bf16[256,1024]{1,0:T(8,128)(2,1)S(1)} %get-tuple-element.34.w1), channel_id=1, source_target_pairs={{2,3},{3,2},{4,5},{5,4},{10,11},{11,10},{12,13},{13,12},{18,19},{1... | collective-permute-start | bytes 1572872 | tf_op jit(solution)/shard_map/ppermute | solution.py:153
  24.4 13.9 %collective-permute-start.6 = (bf16[256,1024]{1,0:T(8,128)(2,1)S(1)}, bf16[256,1024]{1,0:T(8,128)(2,1)S(1)}, u32[]{:S(2)}, u32[]{:S(2)}) collective-permute-start(bf16[256,1024]{1,0:T(8,128)(2,1)S(1)} %get-tuple-element.34.w1), channel_id=1, source_target_pairs={{12,4},{20,12},{2,10},{28,20},{10,18},{36,28},{18,26},{44,36},{26,... | collective-permute-start | bytes 1572872 | tf_op jit(solution)/shard_map/ppermute | solution.py:169
  25.1 21.1 %collective-permute-start.7 = (bf16[256,1024]{1,0:T(8,128)(2,1)S(1)}, bf16[256,1024]{1,0:T(8,128)(2,1)S(1)}, u32[]{:S(2)}, u32[]{:S(2)}) collective-permute-start(bf16[256,1024]{1,0:T(8,128)(2,1)S(1)} %get-tuple-element.36), channel_id=1, source_target_pairs={{0,4},{6,2},{1,5},{7,3},{8,12},{14,10},{9,13},{15,11},{16,20},{22,... | collective-permute-start | bytes 1572872 | tf_op jit(solution)/shard_map/ppermute | solution.py:148
  34.9 11.3 %collective-permute-start.10 = (bf16[256,1024]{1,0:T(8,128)(2,1)S(1)}, bf16[256,1024]{1,0:T(8,128)(2,1)S(1)}, u32[]{:S(2)}, u32[]{:S(2)}) collective-permute-start(bf16[256,1024]{1,0:T(8,128)(2,1)S(1)} %get-tuple-element.44), channel_id=1, source_target_pairs={{258,252},{250,258},{514,508},{506,514},{4,764},{764,2},{259,253},... | collective-permute-start | bytes 1572872 | tf_op jit(solution)/shard_map/ppermute | solution.py:177
  35.6 2.7 %collective-permute-start.8 = (bf16[128,1024]{1,0:T(8,128)(2,1)S(1)}, bf16[128,1024]{1,0:T(8,128)(2,1)S(1)}, u32[]{:S(2)}, u32[]{:S(2)}) collective-permute-start(bf16[128,1024]{1,0:T(8,128)(2,1)S(1)} %collective-permute-done.4.y0), channel_id=1, source_target_pairs={{504,252},{518,2},{760,508},{6,258},{248,764},{262,514},{505,253},... | collective-permute-start | bytes 786440 | tf_op jit(solution)/shard_map/ppermute | solution.py:194
  36.3 2.0 %collective-permute-start.9 = (bf16[128,1024]{1,0:T(8,128)(2,1)S(1)}, bf16[128,1024]{1,0:T(8,128)(2,1)S(1)}, u32[]{:S(2)}, u32[]{:S(2)}) collective-permute-start(bf16[128,1024]{1,0:T(8,128)(2,1)S(1)} %collective-permute-done.4.y0), channel_id=1, source_target_pairs={{508,252},{514,2},{764,508},{2,258},{252,764},{258,514},{509,253},... | collective-permute-start | bytes 786440 | tf_op jit(solution)/shard_map/ppermute | solution.py:194
  46.3 0.8 collective-permute-start.11
  47.1 33.9 %collective-permute-start.13 = (bf16[128,1024]{1,0:T(8,128)(2,1)S(1)}, bf16[128,1024]{1,0:T(8,128)(2,1)S(1)}, u32[]{:S(2)}, u32[]{:S(2)}) collective-permute-start(bf16[128,1024]{1,0:T(8,128)(2,1)S(1)} %shard_map.64), channel_id=1, source_target_pairs={{2,6},{4,0},{3,7},{5,1},{10,14},{12,8},{11,15},{13,9},{18,22},{20,... | collective-permute-start | bytes 786440 | tf_op jit(solution)/shard_map/ppermute | solution.py:148
  48.5 38.5 %collective-permute-start.12 = (bf16[128,1024]{1,0:T(8,128)(2,1)S(1)}, bf16[128,1024]{1,0:T(8,128)(2,1)S(1)}, u32[]{:S(2)}, u32[]{:S(2)}) collective-permute-start(bf16[128,1024]{1,0:T(8,128)(2,1)S(1)} %get-tuple-element.50), channel_id=1, source_target_pairs={{2,0},{4,6},{3,1},{5,7},{10,8},{12,14},{11,9},{13,15},{18,16},{20,... | collective-permute-start | bytes 786440 | tf_op jit(solution)/shard_map/ppermute | solution.py:148
  49.8 37.2 %collective-permute-start.14 = (bf16[128,1024]{1,0:T(8,128)(2,1)S(1)}, bf16[128,1024]{1,0:T(8,128)(2,1)S(1)}, u32[]{:S(2)}, u32[]{:S(2)}) collective-permute-start(bf16[128,1024]{1,0:T(8,128)(2,1)S(1)} %get-tuple-element.52), channel_id=1, source_target_pairs={{2,4},{4,2},{3,5},{5,3},{10,12},{12,10},{11,13},{13,11},{18,20},{2... | collective-permute-start | bytes 786440 | tf_op jit(solution)/shard_map/ppermute | solution.py:148

commit v8 on v7

--- a/solution.py
+++ b/solution.py
@@ -216,19 +216,19 @@
     af, own_far, y0, to_near, to_last, to_group = lax.optimization_barrier(
         (af, own_far, y0, to_near, to_last, to_group)
     )
-    y1 = neighbour(to_near)
     last = line(to_last, to_far)
     kb = across_groups(y0, 0, 3)
     ka = across_groups(y0, 2, 1)
     y2 = between_groups(to_group)
     w1_far = swapped(to_near)
+    w1_far, inside = lax.optimization_barrier((w1_far, to_near))
+    y1 = neighbour(inside)
     left, acc = in_vmem(
         early_kernel, [b16((4 * rows, width)), f32((4 * rows, width))],
         scale, bias, other, xe, xo, af, own, own_far, to_near, w1_far,
         flops=24 * unit, scalars=2, scratch=[b16((6 * rows, width))],
     )
-    y1, last, kb, ka, acc = lax.optimization_barrier((y1, last, kb, ka, acc))
-    y1, last, kb, ka, y2 = lax.optimization_barrier((y1, last, kb, ka, y2))
+    last, y2, kb, ka, y1, acc = lax.optimization_barrier((last, y2, kb, ka, y1, acc))
     (w2,) = in_vmem(
         functools.partial(second_pack_kernel, group), [b16((5 * rows, width))], y1, y2, last, y0, ka, kb
     )
@@ -236,13 +236,17 @@
     (acc,) = in_vmem(
         near_kernel, [f32((4 * rows, width))], scale, bias, left, acc, w2, flops=20 * unit, scalars=2
     )
+    (oe,) = in_vmem(
+        functools.partial(late_kernel, 1), [b16((rows, width))] * 1, scale, bias, left, acc, w2_far,
+        flops=5 * unit, scalars=2,
+    )
     (of,) = in_vmem(
         functools.partial(late_kernel, 3), [b16((rows, width))] * 1, scale, bias, left, acc, w2_far,
         flops=5 * unit, scalars=2,
     )
-    oe, oo = in_vmem(
-        functools.partial(late_kernel, 1), [b16((rows, width))] * 2, scale, bias, left, acc, w2_far,
-        flops=10 * unit, scalars=2,
+    (oo,) = in_vmem(
+        functools.partial(late_kernel, 2), [b16((rows, width))] * 1, scale, bias, left, acc, w2_far,
+        flops=5 * unit, scalars=2,
     )
     (om,) = in_vmem(
         functools.partial(late_kernel, 0), [b16((rows, width))] * 1, scale, bias, left, acc, w2_far,
@@ -252,8 +256,6 @@
     to_far_end = line(of, [(1, 3), (2, 0)])
     to_end = line(oe, [(1, 0), (2, 3)])
     to_other = line(oo, between)
-    to_end, to_far_end = lax.optimization_barrier((to_end, to_far_end))
-    to_end, to_other = lax.optimization_barrier((to_end, to_other))
     own_result = jnp.where(inner, om, to_end)
     other_result = jnp.where(inner, to_other, to_far_end)
     return (jnp.where(low, other_result, own_result), jnp.where(low, own_result, other_result))

time: 88.3 us -> 87.5 us (level)
  the two profiles are of different devices: /device:TPU:1 before, /device:TPU:64 now
where the time goes in v8:
time: 87.5 us; the launch traced here: 87 us
  starting transfers between devices  43.2 us (49%)
  waiting for transfers between devices  29.5 us (34%)
  Pallas kernels  10.2 us (12%)
  between operations  2.17 us (2%)
  other arithmetic  1.97 us (2%)
    ppermute x7, waiting for transfers between devices, line(): return lax.ppermute(array, 'zl', pairs)  18.7 us
    ppermute x7, starting transfers between devices, line(): return lax.ppermute(array, 'zl', pairs)  16.2 us
    ppermute x2, starting transfers between devices, across_groups(): return lax.ppermute(array, ('blk', 'zl'), pairs)  13.5 us
    ppermute x2, waiting for transfers between devices, across_groups(): return lax.ppermute(array, ('blk', 'zl'), pairs)  10.5 us
    pallas_call x8, Pallas kernels, in_vmem(): pl.pallas_call(kernel, out_shape=shapes, in_specs=[pl.BlockSpec(memory_sp...  10.2 us
    ppermute x3, starting transfers between devices, swapped(): return lax.ppermute(array, ('zl', 'core'), pairs)  5.82 us
    ppermute x1, starting transfers between devices, neighbour_in_group(): return lax.ppermute(array, ('blk', 'zl'), pairs)  3.48 us
    ppermute x1, starting transfers between devices, neighbour(): return lax.ppermute(array, ('blk', 'zl'), pairs)  2.92 us
  transfers between devices with their start and end apart: 15, of which 5 were waited for; matrix products, arithmetic and copies ran while one was open for 0% of the time, Pallas kernels for 10%

profile of v8, /device:TPU:64, one launch (start us, length us, event | category | flops | bytes accessed | tf_op | source)
XLA Modules:
  0.0 87.0 jit_solution(16132005170681908757)
XLA Ops:
  0.6 1.1 %broadcast_select_fusion.2 = (bf16[128,1024]{1,0:T(8,128)(2,1)S(1)}, bf16[128,1024]{1,0:T(8,128)(2,1)S(1)}, bf16[128,1024]{1,0:T(8,128)(2,1)S(1)}) fusion(pred[]{:T(512)S(6)} %or.3, bf16[128,1024]{1,0:T(8,128)(2,1)} %param.4, bf16[128,1024]{1,0:T(8,128)(2,1)} %param.5, pred[]{:T(512)S(6)} %lt.3), kind=kLoop, calls=%fused_computation.3 | loop fusion | flops 393216 | bytes 1310722 | tf_op jit(solution)/shard_map/jit(_where)/select_n | solution.py:210
  1.8 1.3 %collective-permute-start = (bf16[256,1024]{1,0:T(8,128)(2,1)S(1)}, bf16[256,1024]{1,0:T(8,128)(2,1)S(1)}, u32[]{:S(2)}, u32[]{:S(2)}) collective-permute-start(bf16[256,1024]{1,0:T(8,128)(2,1)S(1)} %pad_maximum_fusion), channel_id=1, source_target_pairs={{0,2},{6,4},{1,3},{7,5},{8,10},{14,12},{9,11},{15,13},{16,18},{22,... | collective-permute-start | bytes 1572872 | tf_op jit(solution)/shard_map/ppermute | solution.py:148
  3.1 4.3 %collective-permute-start.1 = (bf16[256,1024]{1,0:T(8,128)(2,1)S(1)}, bf16[256,1024]{1,0:T(8,128)(2,1)S(1)}, u32[]{:S(2)}, u32[]{:S(2)}) collective-permute-start(bf16[256,1024]{1,0:T(8,128)(2,1)S(1)} %pad_maximum_fusion), channel_id=1, source_target_pairs={{2,4},{4,2},{3,5},{5,3},{10,12},{12,10},{11,13},{13,11},{18,20},{2... | collective-permute-start | bytes 1572872 | tf_op jit(solution)/shard_map/ppermute | solution.py:148
  7.4 1.3 %collective-permute-start.2 = (bf16[128,1024]{1,0:T(8,128)(2,1)S(1)}, bf16[128,1024]{1,0:T(8,128)(2,1)S(1)}, u32[]{:S(2)}, u32[]{:S(2)}) collective-permute-start(bf16[128,1024]{1,0:T(8,128)(2,1)S(1)} %get-tuple-element.41.own), channel_id=1, source_target_pairs={{0,4},{6,2},{1,5},{7,3},{8,12},{14,10},{9,13},{15,11},{16,20},{22,... | collective-permute-start | bytes 786440 | tf_op jit(solution)/shard_map/ppermute | solution.py:148
  8.7 3.5 %collective-permute-start.4 = (bf16[128,1024]{1,0:T(8,128)(2,1)S(1)}, bf16[128,1024]{1,0:T(8,128)(2,1)S(1)}, u32[]{:S(2)}, u32[]{:S(2)}) collective-permute-start(bf16[128,1024]{1,0:T(8,128)(2,1)S(1)} %get-tuple-element.40), channel_id=1, source_target_pairs={{8,0},{250,2},{12,4},{254,6},{16,8},{2,10},{20,12},{6,14},{24,16},... | collective-permute-start | bytes 786440 | tf_op jit(solution)/shard_map/ppermute | solution.py:186
  12.2 1.9 %collective-permute-start.3 = (bf16[128,1024]{1,0:T(8,128)(2,1)S(1)}, bf16[128,1024]{1,0:T(8,128)(2,1)S(1)}, u32[]{:S(2)}, u32[]{:S(2)}) collective-permute-start(bf16[128,1024]{1,0:T(8,128)(2,1)S(1)} %get-tuple-element.41.own), channel_id=1, source_target_pairs={{2,3},{3,2},{4,5},{5,4},{10,11},{11,10},{12,13},{13,12},{18,19},{1... | collective-permute-start | bytes 786440 | tf_op jit(solution)/shard_map/ppermute | solution.py:153
  14.1 10.8 %collective-permute-done.2.af = bf16[128,1024]{1,0:T(8,128)(2,1)S(1)} collective-permute-done((bf16[128,1024]{1,0:T(8,128)(2,1)S(1)}, bf16[128,1024]{1,0:T(8,128)(2,1)S(1)}, u32[]{:S(2)}, u32[]{:S(2)}) %collective-permute-start.2) | collective-permute-done | bytes 262176 | tf_op jit(solution)/shard_map/ppermute | solution.py:148
  24.9 0.0 collective-permute-done.4.y0
  24.9 0.0 collective-permute-done.xe
  24.9 0.1 shard_map.59
  25.0 1.9 %collective-permute-start.5 = (bf16[256,1024]{1,0:T(8,128)(2,1)S(1)}, bf16[256,1024]{1,0:T(8,128)(2,1)S(1)}, u32[]{:S(2)}, u32[]{:S(2)}) collective-permute-start(bf16[256,1024]{1,0:T(8,128)(2,1)S(1)} %get-tuple-element.32.w1), channel_id=1, source_target_pairs={{2,3},{3,2},{4,5},{5,4},{10,11},{11,10},{12,13},{13,12},{18,19},{1... | collective-permute-start | bytes 1572872 | tf_op jit(solution)/shard_map/ppermute | solution.py:153
  26.9 1.3 %collective-permute-start.6 = (bf16[256,1024]{1,0:T(8,128)(2,1)S(1)}, bf16[256,1024]{1,0:T(8,128)(2,1)S(1)}, u32[]{:S(2)}, u32[]{:S(2)}) collective-permute-start(bf16[256,1024]{1,0:T(8,128)(2,1)S(1)} %get-tuple-element.29), channel_id=1, source_target_pairs={{0,4},{6,2},{1,5},{7,3},{8,12},{14,10},{9,13},{15,11},{16,20},{22,... | collective-permute-start | bytes 1572872 | tf_op jit(solution)/shard_map/ppermute | solution.py:148
  28.2 1.3 %collective-permute-start.7 = (bf16[256,1024]{1,0:T(8,128)(2,1)S(1)}, bf16[256,1024]{1,0:T(8,128)(2,1)S(1)}, u32[]{:S(2)}, u32[]{:S(2)}) collective-permute-start(bf16[256,1024]{1,0:T(8,128)(2,1)S(1)} %get-tuple-element.30), channel_id=1, source_target_pairs={{258,252},{250,258},{514,508},{506,514},{4,764},{764,2},{259,253},... | collective-permute-start | bytes 1572872 | tf_op jit(solution)/shard_map/ppermute | solution.py:177
  29.6 2.9 %collective-permute-start.10 = (bf16[256,1024]{1,0:T(8,128)(2,1)S(1)}, bf16[256,1024]{1,0:T(8,128)(2,1)S(1)}, u32[]{:S(2)}, u32[]{:S(2)}) collective-permute-start(bf16[256,1024]{1,0:T(8,128)(2,1)S(1)} %get-tuple-element.32.w1), channel_id=1, source_target_pairs={{12,4},{20,12},{2,10},{28,20},{10,18},{36,28},{18,26},{44,36},{26,... | collective-permute-start | bytes 1572872 | tf_op jit(solution)/shard_map/ppermute | solution.py:169
  32.5 1.3 %collective-permute-start.8 = (bf16[128,1024]{1,0:T(8,128)(2,1)S(1)}, bf16[128,1024]{1,0:T(8,128)(2,1)S(1)}, u32[]{:S(2)}, u32[]{:S(2)}) collective-permute-start(bf16[128,1024]{1,0:T(8,128)(2,1)S(1)} %collective-permute-done.4.y0), channel_id=1, source_target_pairs={{504,252},{518,2},{760,508},{6,258},{248,764},{262,514},{505,253},... | collective-permute-start | bytes 786440 | tf_op jit(solution)/shard_map/ppermute | solution.py:194
  33.8 12.2 %collective-permute-start.9 = (bf16[128,1024]{1,0:T(8,128)(2,1)S(1)}, bf16[128,1024]{1,0:T(8,128)(2,1)S(1)}, u32[]{:S(2)}, u32[]{:S(2)}) collective-permute-start(bf16[128,1024]{1,0:T(8,128)(2,1)S(1)} %collective-permute-done.4.y0), channel_id=1, source_target_pairs={{508,252},{514,2},{764,508},{2,258},{252,764},{258,514},{509,253},... | collective-permute-start | bytes 786440 | tf_op jit(solution)/shard_map/ppermute | solution.py:194
  47.3 2.5 %shard_map.60 = (bf16[512,1024]{1,0:T(8,128)(2,1)S(1)}, f32[512,1024]{1,0:T(8,128)S(1)}) custom-call(f32[1]{0:T(128)S(6)} %copy.6.scale, f32[1]{0:T(128)S(6)} %copy.7.bias, bf16[128,1024]{1,0:T(8,128)(2,1)S(1)} %get-tuple-element.42.other.am, bf16[256,1024]{1,0:T(8,128)(2,1)S(1)} %collective-permute-done.xe, ...), custom_call_target="tpu_custom_call" | custom-call | flops 1610612736 | bytes 3145728 | tf_op jit(solution)/shard_map/pallas_call | solution.py:19
  49.8 0.2 collective-permute-done.8.kb
  50.0 10.3 %collective-permute-done.9.ka = bf16[128,1024]{1,0:T(8,128)(2,1)S(1)} collective-permute-done((bf16[128,1024]{1,0:T(8,128)(2,1)S(1)}, bf16[128,1024]{1,0:T(8,128)(2,1)S(1)}, u32[]{:S(2)}, u32[]{:S(2)}) %collective-permute-start.9) | collective-permute-done | bytes 262176 | tf_op jit(solution)/shard_map/ppermute | solution.py:194
  60.2 0.2 shard_map.61.w2
  60.4 2.0 %collective-permute-start.11 = (bf16[640,1024]{1,0:T(8,128)(2,1)S(1)}, bf16[640,1024]{1,0:T(8,128)(2,1)S(1)}, u32[]{:S(2)}, u32[]{:S(2)}) collective-permute-start(bf16[640,1024]{1,0:T(8,128)(2,1)S(1)} %shard_map.61.w2), channel_id=1, source_target_pairs={{2,3},{3,2},{4,5},{5,4},{10,11},{11,10},{12,13},{13,12},{18,19},{1... | collective-permute-start | bytes 3932168 | tf_op jit(solution)/shard_map/ppermute | solution.py:153
  62.4 2.6 %shard_map.62.acc = f32[512,1024]{1,0:T(8,128)S(1)} custom-call(f32[1]{0:T(128)S(6)} %copy.6.scale, f32[1]{0:T(128)S(6)} %copy.7.bias, bf16[512,1024]{1,0:T(8,128)(2,1)S(1)} %get-tuple-element.28.left, f32[512,1024]{1,0:T(8,128)S(1)} %get-tuple-element.34.acc, bf16[640,1024]{1,0:T(8,128)(2,1)S(1)} %shard_map.61.w2), custom_call_target="tpu_custom_call" | custom-call | flops 1342177280 | bytes 2097152 | tf_op jit(solution)/shard_map/pallas_call | solution.py:19
  65.0 0.3 collective-permute-done.11.w2_far
  65.3 1.2 %shard_map.66 = bf16[128,1024]{1,0:T(8,128)(2,1)S(1)} custom-call(f32[1]{0:T(128)S(6)} %copy.6.scale, f32[1]{0:T(128)S(6)} %copy.7.bias, bf16[512,1024]{1,0:T(8,128)(2,1)S(1)} %get-tuple-element.28.left, f32[512,1024]{1,0:T(8,128)S(1)} %shard_map.62.acc, bf16[640,1024]{1,0:T(8,128)(2,1)S(1)} %collective-permute-done.11.w2_far), custom_call_target="tpu_custom_call" | custom-call | flops 335544320 | bytes 262144 | tf_op jit(solution)/shard_map/pallas_call | solution.py:19
  66.5 1.3 %collective-permute-start.14 = (bf16[128,1024]{1,0:T(8,128)(2,1)S(1)}, bf16[128,1024]{1,0:T(8,128)(2,1)S(1)}, u32[]{:S(2)}, u32[]{:S(2)}) collective-permute-start(bf16[128,1024]{1,0:T(8,128)(2,1)S(1)} %shard_map.66), channel_id=1, source_target_pairs={{2,0},{4,6},{3,1},{5,7},{10,8},{12,14},{11,9},{13,15},{18,16},{20,... | collective-permute-start | bytes 786440 | tf_op jit(solution)/shard_map/ppermute | solution.py:148
  67.9 1.2 %shard_map.64 = bf16[128,1024]{1,0:T(8,128)(2,1)S(1)} custom-call(f32[1]{0:T(128)S(6)} %copy.6.scale, f32[1]{0:T(128)S(6)} %copy.7.bias, bf16[512,1024]{1,0:T(8,128)(2,1)S(1)} %get-tuple-element.28.left, f32[512,1024]{1,0:T(8,128)S(1)} %shard_map.62.acc, bf16[640,1024]{1,0:T(8,128)(2,1)S(1)} %collective-permute-done.11.w2_far), custom_call_target="tpu_custom_call" | custom-call | flops 335544320 | bytes 262144 | tf_op jit(solution)/shard_map/pallas_call | solution.py:19
  69.1 1.3 %collective-permute-start.13 = (bf16[128,1024]{1,0:T(8,128)(2,1)S(1)}, bf16[128,1024]{1,0:T(8,128)(2,1)S(1)}, u32[]{:S(2)}, u32[]{:S(2)}) collective-permute-start(bf16[128,1024]{1,0:T(8,128)(2,1)S(1)} %shard_map.64), channel_id=1, source_target_pairs={{2,6},{4,0},{3,7},{5,1},{10,14},{12,8},{11,15},{13,9},{18,22},{20,... | collective-permute-start | bytes 786440 | tf_op jit(solution)/shard_map/ppermute | solution.py:148
  70.4 1.2 %shard_map.63 = bf16[128,1024]{1,0:T(8,128)(2,1)S(1)} custom-call(f32[1]{0:T(128)S(6)} %copy.6.scale, f32[1]{0:T(128)S(6)} %copy.7.bias, bf16[512,1024]{1,0:T(8,128)(2,1)S(1)} %get-tuple-element.28.left, f32[512,1024]{1,0:T(8,128)S(1)} %shard_map.62.acc, bf16[640,1024]{1,0:T(8,128)(2,1)S(1)} %collective-permute-done.11.w2_far), custom_call_target="tpu_custom_call" | custom-call | flops 335544320 | bytes 262144 | tf_op jit(solution)/shard_map/pallas_call | solution.py:19
  71.6 5.4 %collective-permute-start.12 = (bf16[128,1024]{1,0:T(8,128)(2,1)S(1)}, bf16[128,1024]{1,0:T(8,128)(2,1)S(1)}, u32[]{:S(2)}, u32[]{:S(2)}) collective-permute-start(bf16[128,1024]{1,0:T(8,128)(2,1)S(1)} %shard_map.63), channel_id=1, source_target_pairs={{2,4},{4,2},{3,5},{5,3},{10,12},{12,10},{11,13},{13,11},{18,20},{2... | collective-permute-start | bytes 786440 | tf_op jit(solution)/shard_map/ppermute | solution.py:148
  77.1 1.2 %shard_map.65 = bf16[128,1024]{1,0:T(8,128)(2,1)S(1)} custom-call(f32[1]{0:T(128)S(6)} %copy.6.scale, f32[1]{0:T(128)S(6)} %copy.7.bias, bf16[512,1024]{1,0:T(8,128)(2,1)S(1)} %get-tuple-element.28.left, f32[512,1024]{1,0:T(8,128)S(1)} %shard_map.62.acc, bf16[640,1024]{1,0:T(8,128)(2,1)S(1)} %collective-permute-done.11.w2_far), custom_call_target="tpu_custom_call" | custom-call | flops 335544320 | bytes 262144 | tf_op jit(solution)/shard_map/pallas_call | solution.py:19
  78.3 7.9 %collective-permute-done.12 = bf16[128,1024]{1,0:T(8,128)(2,1)S(1)} collective-permute-done((bf16[128,1024]{1,0:T(8,128)(2,1)S(1)}, bf16[128,1024]{1,0:T(8,128)(2,1)S(1)}, u32[]{:S(2)}, u32[]{:S(2)}) %collective-permute-start.12) | collective-permute-done | bytes 262176 | tf_op jit(solution)/shard_map/ppermute | solution.py:148
  86.2 0.8 broadcast_select_fusion.3
  (9 shorter events, 0.1 us)
Async XLA Ops:
  1.8 23.1 %collective-permute-start = (bf16[256,1024]{1,0:T(8,128)(2,1)S(1)}, bf16[256,1024]{1,0:T(8,128)(2,1)S(1)}, u32[]{:S(2)}, u32[]{:S(2)}) collective-permute-start(bf16[256,1024]{1,0:T(8,128)(2,1)S(1)} %pad_maximum_fusion), channel_id=1, source_target_pairs={{0,2},{6,4},{1,3},{7,5},{8,10},{14,12},{9,11},{15,13},{16,18},{22,... | collective-permute-start | bytes 1572872 | tf_op jit(solution)/shard_map/ppermute | solution.py:148
  3.1 21.8 %collective-permute-start.1 = (bf16[256,1024]{1,0:T(8,128)(2,1)S(1)}, bf16[256,1024]{1,0:T(8,128)(2,1)S(1)}, u32[]{:S(2)}, u32[]{:S(2)}) collective-permute-start(bf16[256,1024]{1,0:T(8,128)(2,1)S(1)} %pad_maximum_fusion), channel_id=1, source_target_pairs={{2,4},{4,2},{3,5},{5,3},{10,12},{12,10},{11,13},{13,11},{18,20},{2... | collective-permute-start | bytes 1572872 | tf_op jit(solution)/shard_map/ppermute | solution.py:148
  7.4 17.5 %collective-permute-start.2 = (bf16[128,1024]{1,0:T(8,128)(2,1)S(1)}, bf16[128,1024]{1,0:T(8,128)(2,1)S(1)}, u32[]{:S(2)}, u32[]{:S(2)}) collective-permute-start(bf16[128,1024]{1,0:T(8,128)(2,1)S(1)} %get-tuple-element.41.own), channel_id=1, source_target_pairs={{0,4},{6,2},{1,5},{7,3},{8,12},{14,10},{9,13},{15,11},{16,20},{22,... | collective-permute-start | bytes 786440 | tf_op jit(solution)/shard_map/ppermute | solution.py:148
  8.7 16.2 %collective-permute-start.4 = (bf16[128,1024]{1,0:T(8,128)(2,1)S(1)}, bf16[128,1024]{1,0:T(8,128)(2,1)S(1)}, u32[]{:S(2)}, u32[]{:S(2)}) collective-permute-start(bf16[128,1024]{1,0:T(8,128)(2,1)S(1)} %get-tuple-element.40), channel_id=1, source_target_pairs={{8,0},{250,2},{12,4},{254,6},{16,8},{2,10},{20,12},{6,14},{24,16},... | collective-permute-start | bytes 786440 | tf_op jit(solution)/shard_map/ppermute | solution.py:186
  12.2 12.9 %collective-permute-start.3 = (bf16[128,1024]{1,0:T(8,128)(2,1)S(1)}, bf16[128,1024]{1,0:T(8,128)(2,1)S(1)}, u32[]{:S(2)}, u32[]{:S(2)}) collective-permute-start(bf16[128,1024]{1,0:T(8,128)(2,1)S(1)} %get-tuple-element.41.own), channel_id=1, source_target_pairs={{2,3},{3,2},{4,5},{5,4},{10,11},{11,10},{12,13},{13,12},{18,19},{1... | collective-permute-start | bytes 786440 | tf_op jit(solution)/shard_map/ppermute | solution.py:153
  25.0 4.5 %collective-permute-start.5 = (bf16[256,1024]{1,0:T(8,128)(2,1)S(1)}, bf16[256,1024]{1,0:T(8,128)(2,1)S(1)}, u32[]{:S(2)}, u32[]{:S(2)}) collective-permute-start(bf16[256,1024]{1,0:T(8,128)(2,1)S(1)} %get-tuple-element.32.w1), channel_id=1, source_target_pairs={{2,3},{3,2},{4,5},{5,4},{10,11},{11,10},{12,13},{13,12},{18,19},{1... | collective-permute-start | bytes 1572872 | tf_op jit(solution)/shard_map/ppermute | solution.py:153
  26.9 33.3 %collective-permute-start.6 = (bf16[256,1024]{1,0:T(8,128)(2,1)S(1)}, bf16[256,1024]{1,0:T(8,128)(2,1)S(1)}, u32[]{:S(2)}, u32[]{:S(2)}) collective-permute-start(bf16[256,1024]{1,0:T(8,128)(2,1)S(1)} %get-tuple-element.29), channel_id=1, source_target_pairs={{0,4},{6,2},{1,5},{7,3},{8,12},{14,10},{9,13},{15,11},{16,20},{22,... | collective-permute-start | bytes 1572872 | tf_op jit(solution)/shard_map/ppermute | solution.py:148
  28.2 32.0 %collective-permute-start.7 = (bf16[256,1024]{1,0:T(8,128)(2,1)S(1)}, bf16[256,1024]{1,0:T(8,128)(2,1)S(1)}, u32[]{:S(2)}, u32[]{:S(2)}) collective-permute-start(bf16[256,1024]{1,0:T(8,128)(2,1)S(1)} %get-tuple-element.30), channel_id=1, source_target_pairs={{258,252},{250,258},{514,508},{506,514},{4,764},{764,2},{259,253},... | collective-permute-start | bytes 1572872 | tf_op jit(solution)/shard_map/ppermute | solution.py:177
  29.6 30.7 %collective-permute-start.10 = (bf16[256,1024]{1,0:T(8,128)(2,1)S(1)}, bf16[256,1024]{1,0:T(8,128)(2,1)S(1)}, u32[]{:S(2)}, u32[]{:S(2)}) collective-permute-start(bf16[256,1024]{1,0:T(8,128)(2,1)S(1)} %get-tuple-element.32.w1), channel_id=1, source_target_pairs={{12,4},{20,12},{2,10},{28,20},{10,18},{36,28},{18,26},{44,36},{26,... | collective-permute-start | bytes 1572872 | tf_op jit(solution)/shard_map/ppermute | solution.py:169
  32.5 17.5 %collective-permute-start.8 = (bf16[128,1024]{1,0:T(8,128)(2,1)S(1)}, bf16[128,1024]{1,0:T(8,128)(2,1)S(1)}, u32[]{:S(2)}, u32[]{:S(2)}) collective-permute-start(bf16[128,1024]{1,0:T(8,128)(2,1)S(1)} %collective-permute-done.4.y0), channel_id=1, source_target_pairs={{504,252},{518,2},{760,508},{6,258},{248,764},{262,514},{505,253},... | collective-permute-start | bytes 786440 | tf_op jit(solution)/shard_map/ppermute | solution.py:194
  33.8 26.4 %collective-permute-start.9 = (bf16[128,1024]{1,0:T(8,128)(2,1)S(1)}, bf16[128,1024]{1,0:T(8,128)(2,1)S(1)}, u32[]{:S(2)}, u32[]{:S(2)}) collective-permute-start(bf16[128,1024]{1,0:T(8,128)(2,1)S(1)} %collective-permute-done.4.y0), channel_id=1, source_target_pairs={{508,252},{514,2},{764,508},{2,258},{252,764},{258,514},{509,253},... | collective-permute-start | bytes 786440 | tf_op jit(solution)/shard_map/ppermute | solution.py:194
  60.4 4.9 %collective-permute-start.11 = (bf16[640,1024]{1,0:T(8,128)(2,1)S(1)}, bf16[640,1024]{1,0:T(8,128)(2,1)S(1)}, u32[]{:S(2)}, u32[]{:S(2)}) collective-permute-start(bf16[640,1024]{1,0:T(8,128)(2,1)S(1)} %shard_map.61.w2), channel_id=1, source_target_pairs={{2,3},{3,2},{4,5},{5,4},{10,11},{11,10},{12,13},{13,12},{18,19},{1... | collective-permute-start | bytes 3932168 | tf_op jit(solution)/shard_map/ppermute | solution.py:153
  66.5 11.7 %collective-permute-start.14 = (bf16[128,1024]{1,0:T(8,128)(2,1)S(1)}, bf16[128,1024]{1,0:T(8,128)(2,1)S(1)}, u32[]{:S(2)}, u32[]{:S(2)}) collective-permute-start(bf16[128,1024]{1,0:T(8,128)(2,1)S(1)} %shard_map.66), channel_id=1, source_target_pairs={{2,0},{4,6},{3,1},{5,7},{10,8},{12,14},{11,9},{13,15},{18,16},{20,... | collective-permute-start | bytes 786440 | tf_op jit(solution)/shard_map/ppermute | solution.py:148
  69.1 9.2 %collective-permute-start.13 = (bf16[128,1024]{1,0:T(8,128)(2,1)S(1)}, bf16[128,1024]{1,0:T(8,128)(2,1)S(1)}, u32[]{:S(2)}, u32[]{:S(2)}) collective-permute-start(bf16[128,1024]{1,0:T(8,128)(2,1)S(1)} %shard_map.64), channel_id=1, source_target_pairs={{2,6},{4,0},{3,7},{5,1},{10,14},{12,8},{11,15},{13,9},{18,22},{20,... | collective-permute-start | bytes 786440 | tf_op jit(solution)/shard_map/ppermute | solution.py:148
  71.6 14.6 %collective-permute-start.12 = (bf16[128,1024]{1,0:T(8,128)(2,1)S(1)}, bf16[128,1024]{1,0:T(8,128)(2,1)S(1)}, u32[]{:S(2)}, u32[]{:S(2)}) collective-permute-start(bf16[128,1024]{1,0:T(8,128)(2,1)S(1)} %shard_map.63), channel_id=1, source_target_pairs={{2,4},{4,2},{3,5},{5,3},{10,12},{12,10},{11,13},{13,11},{18,20},{2... | collective-permute-start | bytes 786440 | tf_op jit(solution)/shard_map/ppermute | solution.py:148

commit v9 on v8

--- a/solution.py
+++ b/solution.py
@@ -110,13 +110,22 @@
         acc[...] = accumulated(left[...], columns, None, scale[0], bias[0], [(i * rows, 2 * i * rows) for i in range(3)])
 
 
+def sends_up(group):
+    chip, block, blocks = lax.axis_index("zl"), lax.axis_index("blk"), lax.axis_size("blk")
+    upper = jnp.logical_and(lax.rem(block, group) == group - 1, block < blocks - 1)
+    return jnp.logical_or(jnp.logical_and(block == 0, chip == 2), jnp.logical_and(upper, chip == 1))
+
+
 def second_pack_kernel(group, y1, y2, last, y0, ka, kb, w2):
     rows = y0.shape[0]
     gathered(w2, [(y1, 0, 2 * rows), (last, 0, 2 * rows), (y0, 0, rows)])
 
+    @pl.when(jnp.logical_or(at_border(group), sends_up(group)))
+    def _():
+        gathered(w2, [(y2, 0, 2 * rows)])
+
     @pl.when(at_border(group))
     def _():
-        gathered(w2, [(y2, 0, 2 * rows)])
         gathered(w2.at[3 * rows :, :], [(kb, 0, rows), (ka, 0, rows)])
 
 
@@ -162,9 +171,9 @@
     def neighbour(array):
         pairs = []
         for p in range(blocks):
-            if (p + 1) % group:
+            if (p + 1) % group and p > 0:
                 pairs.append(((p + 1) * CHIPS + 2, p * CHIPS + 2))
-            if p % group:
+            if p % group and ((p + 1) % group or p == blocks - 1):
                 pairs.append(((p - 1) * CHIPS + 1, p * CHIPS + 1))
         return lax.ppermute(array, ("blk", "zl"), pairs)
 
@@ -174,6 +183,7 @@
             q = (p + 1) % blocks
             pairs.append((q * CHIPS + (1 if q else 2), p * CHIPS + 2))
             pairs.append((p * CHIPS + (1 if q else 2), q * CHIPS + 1))
+            pairs.append(((p - 1) * CHIPS + 1, p * CHIPS + 1) if q else (CHIPS + 2, 2))
         return lax.ppermute(array, ("blk", "zl"), pairs)
 
     def neighbour_in_group(array):

time: 87.5 us -> 84.8 us (0.969)
  the two profiles are of different devices: /device:TPU:64 before, /device:TPU:1 now
where the time goes in v9:
time: 84.8 us; the launch traced here: 84 us
  waiting for transfers between devices  45 us (53%)
  starting transfers between devices  34.5 us (41%)
  between operations  2.18 us (3%)
  other arithmetic  1.97 us (2%)
    ppermute x7, waiting for transfers between devices, line(): return lax.ppermute(array, 'zl', pairs)  41.1 us
    ppermute x7, starting transfers between devices, line(): return lax.ppermute(array, 'zl', pairs)  22.3 us
    ppermute x1, starting transfers between devices, neighbour_in_group(): return lax.ppermute(array, ('blk', 'zl'), pairs)  7.29 us
    ppermute x1, waiting for transfers between devices, neighbour_in_group(): return lax.ppermute(array, ('blk', 'zl'), pairs)  3.94 us
    ppermute x3, starting transfers between devices, swapped(): return lax.ppermute(array, ('zl', 'core'), pairs)  2.12 us
  transfers between devices with their start and end apart: 15, of which 3 were waited for; matrix products, arithmetic and copies ran while one was open for 0% of the time, Pallas kernels for 0%

profile of v9, /device:TPU:1, one launch (start us, length us, event | category | flops | bytes accessed | tf_op | source)
XLA Modules:
  0.0 84.0 jit_solution(4123888140501837341)
XLA Ops:
  0.6 1.1 %broadcast_select_fusion.2 = (bf16[128,1024]{1,0:T(8,128)(2,1)S(1)}, bf16[128,1024]{1,0:T(8,128)(2,1)S(1)}, bf16[128,1024]{1,0:T(8,128)(2,1)S(1)}) fusion(pred[]{:T(512)S(6)} %or.3, bf16[128,1024]{1,0:T(8,128)(2,1)} %param.4, bf16[128,1024]{1,0:T(8,128)(2,1)} %param.5, pred[]{:T(512)S(6)} %lt.3), kind=kLoop, calls=%fused_computation.3 | loop fusion | flops 393216 | bytes 1310722 | tf_op jit(solution)/shard_map/jit(_where)/select_n | solution.py:220
  1.8 4.9 %collective-permute-start = (bf16[256,1024]{1,0:T(8,128)(2,1)S(1)}, bf16[256,1024]{1,0:T(8,128)(2,1)S(1)}, u32[]{:S(2)}, u32[]{:S(2)}) collective-permute-start(bf16[256,1024]{1,0:T(8,128)(2,1)S(1)} %pad_maximum_fusion), channel_id=1, source_target_pairs={{0,2},{6,4},{1,3},{7,5},{8,10},{14,12},{9,11},{15,13},{16,18},{22,... | collective-permute-start | bytes 1572872 | tf_op jit(solution)/shard_map/ppermute | solution.py:157
  6.6 0.7 collective-permute-start.1
  7.3 4.3 %collective-permute-start.2 = (bf16[128,1024]{1,0:T(8,128)(2,1)S(1)}, bf16[128,1024]{1,0:T(8,128)(2,1)S(1)}, u32[]{:S(2)}, u32[]{:S(2)}) collective-permute-start(bf16[128,1024]{1,0:T(8,128)(2,1)S(1)} %get-tuple-element.41.own), channel_id=1, source_target_pairs={{0,4},{6,2},{1,5},{7,3},{8,12},{14,10},{9,13},{15,11},{16,20},{22,... | collective-permute-start | bytes 786440 | tf_op jit(solution)/shard_map/ppermute | solution.py:157
  11.7 7.3 %collective-permute-start.4 = (bf16[128,1024]{1,0:T(8,128)(2,1)S(1)}, bf16[128,1024]{1,0:T(8,128)(2,1)S(1)}, u32[]{:S(2)}, u32[]{:S(2)}) collective-permute-start(bf16[128,1024]{1,0:T(8,128)(2,1)S(1)} %get-tuple-element.40), channel_id=1, source_target_pairs={{8,0},{250,2},{12,4},{254,6},{16,8},{2,10},{20,12},{6,14},{24,16},... | collective-permute-start | bytes 786440 | tf_op jit(solution)/shard_map/ppermute | solution.py:196
  19.0 0.7 collective-permute-start.3
  19.6 0.0 collective-permute-done.2.af
  19.7 3.9 %collective-permute-done.4.y0 = bf16[128,1024]{1,0:T(8,128)(2,1)S(1)} collective-permute-done((bf16[128,1024]{1,0:T(8,128)(2,1)S(1)}, bf16[128,1024]{1,0:T(8,128)(2,1)S(1)}, u32[]{:S(2)}, u32[]{:S(2)}) %collective-permute-start.4) | collective-permute-done | bytes 262176 | tf_op jit(solution)/shard_map/ppermute | solution.py:196
  23.6 0.0 collective-permute-done.xe
  23.6 0.0 collective-permute-done.1.xo
  23.6 0.1 shard_map.59
  23.7 0.0 collective-permute-done.3.own_far
  23.7 0.7 collective-permute-start.5
  24.4 9.2 %collective-permute-start.6 = (bf16[256,1024]{1,0:T(8,128)(2,1)S(1)}, bf16[256,1024]{1,0:T(8,128)(2,1)S(1)}, u32[]{:S(2)}, u32[]{:S(2)}) collective-permute-start(bf16[256,1024]{1,0:T(8,128)(2,1)S(1)} %get-tuple-element.29), channel_id=1, source_target_pairs={{0,4},{6,2},{1,5},{7,3},{8,12},{14,10},{9,13},{15,11},{16,20},{22,... | collective-permute-start | bytes 1572872 | tf_op jit(solution)/shard_map/ppermute | solution.py:157
  33.6 0.7 collective-permute-start.7
  34.3 0.0 collective-permute-done.5.w1_far
  34.3 0.7 collective-permute-start.10
  35.0 0.7 collective-permute-start.8
  35.7 0.7 collective-permute-start.9
  37.7 0.0 collective-permute-done.8.kb
  37.8 0.0 collective-permute-done.9.ka
  37.8 7.2 %collective-permute-done.6.last = bf16[256,1024]{1,0:T(8,128)(2,1)S(1)} collective-permute-done((bf16[256,1024]{1,0:T(8,128)(2,1)S(1)}, bf16[256,1024]{1,0:T(8,128)(2,1)S(1)}, u32[]{:S(2)}, u32[]{:S(2)}) %collective-permute-start.6) | collective-permute-done | bytes 524320 | tf_op jit(solution)/shard_map/ppermute | solution.py:157
  44.9 0.0 collective-permute-done.7.y2
  44.9 0.1 shard_map.61.w2
  45.0 0.7 collective-permute-start.11
  45.8 1.3 %collective-permute-start.14 = (bf16[128,1024]{1,0:T(8,128)(2,1)S(1)}, bf16[128,1024]{1,0:T(8,128)(2,1)S(1)}, u32[]{:S(2)}, u32[]{:S(2)}) collective-permute-start(bf16[128,1024]{1,0:T(8,128)(2,1)S(1)} %shard_map.66), channel_id=1, source_target_pairs={{2,0},{4,6},{3,1},{5,7},{10,8},{12,14},{11,9},{13,15},{18,16},{20,... | collective-permute-start | bytes 786440 | tf_op jit(solution)/shard_map/ppermute | solution.py:157
  47.2 1.3 %collective-permute-start.13 = (bf16[128,1024]{1,0:T(8,128)(2,1)S(1)}, bf16[128,1024]{1,0:T(8,128)(2,1)S(1)}, u32[]{:S(2)}, u32[]{:S(2)}) collective-permute-start(bf16[128,1024]{1,0:T(8,128)(2,1)S(1)} %shard_map.64), channel_id=1, source_target_pairs={{2,6},{4,0},{3,7},{5,1},{10,14},{12,8},{11,15},{13,9},{18,22},{20,... | collective-permute-start | bytes 786440 | tf_op jit(solution)/shard_map/ppermute | solution.py:157
  48.5 0.7 collective-permute-start.12
  49.2 33.9 %collective-permute-done.14 = bf16[128,1024]{1,0:T(8,128)(2,1)S(1)} collective-permute-done((bf16[128,1024]{1,0:T(8,128)(2,1)S(1)}, bf16[128,1024]{1,0:T(8,128)(2,1)S(1)}, u32[]{:S(2)}, u32[]{:S(2)}) %collective-permute-start.14) | collective-permute-done | bytes 262176 | tf_op jit(solution)/shard_map/ppermute | solution.py:157
  83.1 0.0 collective-permute-done.13
  83.1 0.0 collective-permute-done.12
  83.1 0.8 %broadcast_select_fusion.3 = (bf16[128,1024]{1,0:T(8,128)(2,1)}, bf16[128,1024]{1,0:T(8,128)(2,1)}) fusion(pred[]{:T(512)S(6)} %lt.3, bf16[128,1024]{1,0:T(8,128)(2,1)S(1)} %collective-permute-done.12, bf16[128,1024]{1,0:T(8,128)(2,1)S(1)} %collective-permute-done.13, pred[]{:T(512)S(6)} %or.3, bf16[128,1024]{1,0:T(8,128)(2,1)S(1)} %shard_map.65, ...), kind=kLoop, calls=%fused_computation.4 | loop fusion | flops 524288 | bytes 1572866 | tf_op jit(solution)/shard_map/jit(_where)/select_n | solution.py:271
  (9 shorter events, 0.2 us)
Async XLA Ops:
  1.8 21.8 %collective-permute-start = (bf16[256,1024]{1,0:T(8,128)(2,1)S(1)}, bf16[256,1024]{1,0:T(8,128)(2,1)S(1)}, u32[]{:S(2)}, u32[]{:S(2)}) collective-permute-start(bf16[256,1024]{1,0:T(8,128)(2,1)S(1)} %pad_maximum_fusion), channel_id=1, source_target_pairs={{0,2},{6,4},{1,3},{7,5},{8,10},{14,12},{9,11},{15,13},{16,18},{22,... | collective-permute-start | bytes 1572872 | tf_op jit(solution)/shard_map/ppermute | solution.py:157
  6.6 17.0 %collective-permute-start.1 = (bf16[256,1024]{1,0:T(8,128)(2,1)S(1)}, bf16[256,1024]{1,0:T(8,128)(2,1)S(1)}, u32[]{:S(2)}, u32[]{:S(2)}) collective-permute-start(bf16[256,1024]{1,0:T(8,128)(2,1)S(1)} %pad_maximum_fusion), channel_id=1, source_target_pairs={{2,4},{4,2},{3,5},{5,3},{10,12},{12,10},{11,13},{13,11},{18,20},{2... | collective-permute-start | bytes 1572872 | tf_op jit(solution)/shard_map/ppermute | solution.py:157
  7.3 12.3 %collective-permute-start.2 = (bf16[128,1024]{1,0:T(8,128)(2,1)S(1)}, bf16[128,1024]{1,0:T(8,128)(2,1)S(1)}, u32[]{:S(2)}, u32[]{:S(2)}) collective-permute-start(bf16[128,1024]{1,0:T(8,128)(2,1)S(1)} %get-tuple-element.41.own), channel_id=1, source_target_pairs={{0,4},{6,2},{1,5},{7,3},{8,12},{14,10},{9,13},{15,11},{16,20},{22,... | collective-permute-start | bytes 786440 | tf_op jit(solution)/shard_map/ppermute | solution.py:157
  11.7 11.9 %collective-permute-start.4 = (bf16[128,1024]{1,0:T(8,128)(2,1)S(1)}, bf16[128,1024]{1,0:T(8,128)(2,1)S(1)}, u32[]{:S(2)}, u32[]{:S(2)}) collective-permute-start(bf16[128,1024]{1,0:T(8,128)(2,1)S(1)} %get-tuple-element.40), channel_id=1, source_target_pairs={{8,0},{250,2},{12,4},{254,6},{16,8},{2,10},{20,12},{6,14},{24,16},... | collective-permute-start | bytes 786440 | tf_op jit(solution)/shard_map/ppermute | solution.py:196
  19.0 4.8 %collective-permute-start.3 = (bf16[128,1024]{1,0:T(8,128)(2,1)S(1)}, bf16[128,1024]{1,0:T(8,128)(2,1)S(1)}, u32[]{:S(2)}, u32[]{:S(2)}) collective-permute-start(bf16[128,1024]{1,0:T(8,128)(2,1)S(1)} %get-tuple-element.41.own), channel_id=1, source_target_pairs={{2,3},{3,2},{4,5},{5,4},{10,11},{11,10},{12,13},{13,12},{18,19},{1... | collective-permute-start | bytes 786440 | tf_op jit(solution)/shard_map/ppermute | solution.py:162
  23.7 10.6 %collective-permute-start.5 = (bf16[256,1024]{1,0:T(8,128)(2,1)S(1)}, bf16[256,1024]{1,0:T(8,128)(2,1)S(1)}, u32[]{:S(2)}, u32[]{:S(2)}) collective-permute-start(bf16[256,1024]{1,0:T(8,128)(2,1)S(1)} %get-tuple-element.32.w1), channel_id=1, source_target_pairs={{2,3},{3,2},{4,5},{5,4},{10,11},{11,10},{12,13},{13,12},{18,19},{1... | collective-permute-start | bytes 1572872 | tf_op jit(solution)/shard_map/ppermute | solution.py:162
  24.4 20.5 %collective-permute-start.6 = (bf16[256,1024]{1,0:T(8,128)(2,1)S(1)}, bf16[256,1024]{1,0:T(8,128)(2,1)S(1)}, u32[]{:S(2)}, u32[]{:S(2)}) collective-permute-start(bf16[256,1024]{1,0:T(8,128)(2,1)S(1)} %get-tuple-element.29), channel_id=1, source_target_pairs={{0,4},{6,2},{1,5},{7,3},{8,12},{14,10},{9,13},{15,11},{16,20},{22,... | collective-permute-start | bytes 1572872 | tf_op jit(solution)/shard_map/ppermute | solution.py:157
  33.6 11.3 %collective-permute-start.7 = (bf16[256,1024]{1,0:T(8,128)(2,1)S(1)}, bf16[256,1024]{1,0:T(8,128)(2,1)S(1)}, u32[]{:S(2)}, u32[]{:S(2)}) collective-permute-start(bf16[256,1024]{1,0:T(8,128)(2,1)S(1)} %get-tuple-element.30), channel_id=1, source_target_pairs={{258,252},{250,258},{242,250},{514,508},{506,514},{498,506},{4,764... | collective-permute-start | bytes 1572872 | tf_op jit(solution)/shard_map/ppermute | solution.py:187
  34.3 10.6 %collective-permute-start.10 = (bf16[256,1024]{1,0:T(8,128)(2,1)S(1)}, bf16[256,1024]{1,0:T(8,128)(2,1)S(1)}, u32[]{:S(2)}, u32[]{:S(2)}) collective-permute-start(bf16[256,1024]{1,0:T(8,128)(2,1)S(1)} %get-tuple-element.32.w1), channel_id=1, source_target_pairs={{20,12},{2,10},{28,20},{10,18},{36,28},{18,26},{44,36},{26,34},{52... | collective-permute-start | bytes 1572872 | tf_op jit(solution)/shard_map/ppermute | solution.py:178
  35.0 2.7 %collective-permute-start.8 = (bf16[128,1024]{1,0:T(8,128)(2,1)S(1)}, bf16[128,1024]{1,0:T(8,128)(2,1)S(1)}, u32[]{:S(2)}, u32[]{:S(2)}) collective-permute-start(bf16[128,1024]{1,0:T(8,128)(2,1)S(1)} %collective-permute-done.4.y0), channel_id=1, source_target_pairs={{504,252},{518,2},{760,508},{6,258},{248,764},{262,514},{505,253},... | collective-permute-start | bytes 786440 | tf_op jit(solution)/shard_map/ppermute | solution.py:204
  35.7 2.0 %collective-permute-start.9 = (bf16[128,1024]{1,0:T(8,128)(2,1)S(1)}, bf16[128,1024]{1,0:T(8,128)(2,1)S(1)}, u32[]{:S(2)}, u32[]{:S(2)}) collective-permute-start(bf16[128,1024]{1,0:T(8,128)(2,1)S(1)} %collective-permute-done.4.y0), channel_id=1, source_target_pairs={{508,252},{514,2},{764,508},{2,258},{252,764},{258,514},{509,253},... | collective-permute-start | bytes 786440 | tf_op jit(solution)/shard_map/ppermute | solution.py:204
  45.0 0.8 collective-permute-start.11
  45.8 37.3 %collective-permute-start.14 = (bf16[128,1024]{1,0:T(8,128)(2,1)S(1)}, bf16[128,1024]{1,0:T(8,128)(2,1)S(1)}, u32[]{:S(2)}, u32[]{:S(2)}) collective-permute-start(bf16[128,1024]{1,0:T(8,128)(2,1)S(1)} %shard_map.66), channel_id=1, source_target_pairs={{2,0},{4,6},{3,1},{5,7},{10,8},{12,14},{11,9},{13,15},{18,16},{20,... | collective-permute-start | bytes 786440 | tf_op jit(solution)/shard_map/ppermute | solution.py:157
  47.2 35.9 %collective-permute-start.13 = (bf16[128,1024]{1,0:T(8,128)(2,1)S(1)}, bf16[128,1024]{1,0:T(8,128)(2,1)S(1)}, u32[]{:S(2)}, u32[]{:S(2)}) collective-permute-start(bf16[128,1024]{1,0:T(8,128)(2,1)S(1)} %shard_map.64), channel_id=1, source_target_pairs={{2,6},{4,0},{3,7},{5,1},{10,14},{12,8},{11,15},{13,9},{18,22},{20,... | collective-permute-start | bytes 786440 | tf_op jit(solution)/shard_map/ppermute | solution.py:157
  48.5 34.6 %collective-permute-start.12 = (bf16[128,1024]{1,0:T(8,128)(2,1)S(1)}, bf16[128,1024]{1,0:T(8,128)(2,1)S(1)}, u32[]{:S(2)}, u32[]{:S(2)}) collective-permute-start(bf16[128,1024]{1,0:T(8,128)(2,1)S(1)} %shard_map.63), channel_id=1, source_target_pairs={{2,4},{4,2},{3,5},{5,3},{10,12},{12,10},{11,13},{13,11},{18,20},{2... | collective-permute-start | bytes 786440 | tf_op jit(solution)/shard_map/ppermute | solution.py:157

commit v10 on v9

--- a/solution.py
+++ b/solution.py
@@ -227,16 +227,16 @@
         (af, own_far, y0, to_near, to_last, to_group)
     )
     last = line(to_last, to_far)
-    kb = across_groups(y0, 0, 3)
-    ka = across_groups(y0, 2, 1)
     y2 = between_groups(to_group)
     w1_far = swapped(to_near)
-    w1_far, inside = lax.optimization_barrier((w1_far, to_near))
+    w1_far, inside, y0_late = lax.optimization_barrier((w1_far, to_near, y0))
     y1 = neighbour(inside)
+    kb = across_groups(y0_late, 0, 3)
+    ka = across_groups(y0_late, 2, 1)
     left, acc = in_vmem(
         early_kernel, [b16((4 * rows, width)), f32((4 * rows, width))],
         scale, bias, other, xe, xo, af, own, own_far, to_near, w1_far,
-        flops=24 * unit, scalars=2, scratch=[b16((6 * rows, width))],
+        flops=400 * unit, scalars=2, scratch=[b16((6 * rows, width))],
     )
     last, y2, kb, ka, y1, acc = lax.optimization_barrier((last, y2, kb, ka, y1, acc))
     (w2,) = in_vmem(

time: 84.8 us -> 86.2 us (1.017); the launches traced: 84 us -> 84.5 us
  no operation moved by 1% of the time
where the time goes in v10:
time: 86.2 us; the launch traced here: 84.5 us
  waiting for transfers between devices  45.5 us (53%)
  starting transfers between devices  34.5 us (40%)
  between operations  2.17 us (3%)
  other arithmetic  1.97 us (2%)
    ppermute x7, waiting for transfers between devices, line(): return lax.ppermute(array, 'zl', pairs)  41.6 us
    ppermute x7, starting transfers between devices, line(): return lax.ppermute(array, 'zl', pairs)  22.3 us
    ppermute x1, starting transfers between devices, neighbour_in_group(): return lax.ppermute(array, ('blk', 'zl'), pairs)  7.29 us
    ppermute x1, waiting for transfers between devices, neighbour_in_group(): return lax.ppermute(array, ('blk', 'zl'), pairs)  3.94 us
    ppermute x3, starting transfers between devices, swapped(): return lax.ppermute(array, ('zl', 'core'), pairs)  2.12 us
  transfers between devices with their start and end apart: 15, of which 3 were waited for; matrix products, arithmetic and copies ran while one was open for 0% of the time, Pallas kernels for 0%

profile of v10, /device:TPU:1, one launch (start us, length us, event | category | flops | bytes accessed | tf_op | source)
XLA Modules:
  0.0 84.5 jit_solution(17153931277026954199)
XLA Ops:
  0.6 1.1 %broadcast_select_fusion.2 = (bf16[128,1024]{1,0:T(8,128)(2,1)S(1)}, bf16[128,1024]{1,0:T(8,128)(2,1)S(1)}, bf16[128,1024]{1,0:T(8,128)(2,1)S(1)}) fusion(pred[]{:T(512)S(6)} %or.3, bf16[128,1024]{1,0:T(8,128)(2,1)} %param.4, bf16[128,1024]{1,0:T(8,128)(2,1)} %param.5, pred[]{:T(512)S(6)} %lt.3), kind=kLoop, calls=%fused_computation.3 | loop fusion | flops 393216 | bytes 1310722 | tf_op jit(solution)/shard_map/jit(_where)/select_n | solution.py:220
  1.8 4.9 %collective-permute-start = (bf16[256,1024]{1,0:T(8,128)(2,1)S(1)}, bf16[256,1024]{1,0:T(8,128)(2,1)S(1)}, u32[]{:S(2)}, u32[]{:S(2)}) collective-permute-start(bf16[256,1024]{1,0:T(8,128)(2,1)S(1)} %pad_maximum_fusion), channel_id=1, source_target_pairs={{0,2},{6,4},{1,3},{7,5},{8,10},{14,12},{9,11},{15,13},{16,18},{22,... | collective-permute-start | bytes 1572872 | tf_op jit(solution)/shard_map/ppermute | solution.py:157
  6.6 0.7 collective-permute-start.1
  7.3 4.3 %collective-permute-start.2 = (bf16[128,1024]{1,0:T(8,128)(2,1)S(1)}, bf16[128,1024]{1,0:T(8,128)(2,1)S(1)}, u32[]{:S(2)}, u32[]{:S(2)}) collective-permute-start(bf16[128,1024]{1,0:T(8,128)(2,1)S(1)} %get-tuple-element.43.own), channel_id=1, source_target_pairs={{0,4},{6,2},{1,5},{7,3},{8,12},{14,10},{9,13},{15,11},{16,20},{22,... | collective-permute-start | bytes 786440 | tf_op jit(solution)/shard_map/ppermute | solution.py:157
  11.7 7.3 %collective-permute-start.4 = (bf16[128,1024]{1,0:T(8,128)(2,1)S(1)}, bf16[128,1024]{1,0:T(8,128)(2,1)S(1)}, u32[]{:S(2)}, u32[]{:S(2)}) collective-permute-start(bf16[128,1024]{1,0:T(8,128)(2,1)S(1)} %get-tuple-element.42), channel_id=1, source_target_pairs={{8,0},{250,2},{12,4},{254,6},{16,8},{2,10},{20,12},{6,14},{24,16},... | collective-permute-start | bytes 786440 | tf_op jit(solution)/shard_map/ppermute | solution.py:196
  19.0 0.7 collective-permute-start.3
  19.7 3.9 %collective-permute-done.4.y0 = bf16[128,1024]{1,0:T(8,128)(2,1)S(1)} collective-permute-done((bf16[128,1024]{1,0:T(8,128)(2,1)S(1)}, bf16[128,1024]{1,0:T(8,128)(2,1)S(1)}, u32[]{:S(2)}, u32[]{:S(2)}) %collective-permute-start.4) | collective-permute-done | bytes 262176 | tf_op jit(solution)/shard_map/ppermute | solution.py:196
  23.6 0.0 collective-permute-done.xe
  23.6 0.0 collective-permute-done.1.xo
  23.6 0.1 shard_map.59
  23.7 0.0 collective-permute-done.3.own_far
  23.7 0.7 collective-permute-start.5
  25.7 9.2 %collective-permute-start.6 = (bf16[256,1024]{1,0:T(8,128)(2,1)S(1)}, bf16[256,1024]{1,0:T(8,128)(2,1)S(1)}, u32[]{:S(2)}, u32[]{:S(2)}) collective-permute-start(bf16[256,1024]{1,0:T(8,128)(2,1)S(1)} %get-tuple-element.31), channel_id=1, source_target_pairs={{0,4},{6,2},{1,5},{7,3},{8,12},{14,10},{9,13},{15,11},{16,20},{22,... | collective-permute-start | bytes 1572872 | tf_op jit(solution)/shard_map/ppermute | solution.py:157
  34.9 0.7 collective-permute-start.7
  35.6 0.0 collective-permute-done.5.w1_far
  35.6 0.7 collective-permute-start.8
  36.3 0.7 collective-permute-start.9
  37.0 0.7 collective-permute-start.10
  37.7 8.4 %collective-permute-done.6.last = bf16[256,1024]{1,0:T(8,128)(2,1)S(1)} collective-permute-done((bf16[256,1024]{1,0:T(8,128)(2,1)S(1)}, bf16[256,1024]{1,0:T(8,128)(2,1)S(1)}, u32[]{:S(2)}, u32[]{:S(2)}) %collective-permute-start.6) | collective-permute-done | bytes 524320 | tf_op jit(solution)/shard_map/ppermute | solution.py:157
  46.1 0.0 collective-permute-done.7.y2
  46.2 0.0 collective-permute-done.8.kb
  46.2 0.0 collective-permute-done.10.y1
  46.2 0.1 shard_map.61.w2
  46.3 0.7 collective-permute-start.11
  47.1 0.0 collective-permute-done.11.w2_far
  47.1 1.3 %collective-permute-start.14 = (bf16[128,1024]{1,0:T(8,128)(2,1)S(1)}, bf16[128,1024]{1,0:T(8,128)(2,1)S(1)}, u32[]{:S(2)}, u32[]{:S(2)}) collective-permute-start(bf16[128,1024]{1,0:T(8,128)(2,1)S(1)} %shard_map.66), channel_id=1, source_target_pairs={{2,0},{4,6},{3,1},{5,7},{10,8},{12,14},{11,9},{13,15},{18,16},{20,... | collective-permute-start | bytes 786440 | tf_op jit(solution)/shard_map/ppermute | solution.py:157
  48.4 1.3 %collective-permute-start.13 = (bf16[128,1024]{1,0:T(8,128)(2,1)S(1)}, bf16[128,1024]{1,0:T(8,128)(2,1)S(1)}, u32[]{:S(2)}, u32[]{:S(2)}) collective-permute-start(bf16[128,1024]{1,0:T(8,128)(2,1)S(1)} %shard_map.64), channel_id=1, source_target_pairs={{2,6},{4,0},{3,7},{5,1},{10,14},{12,8},{11,15},{13,9},{18,22},{20,... | collective-permute-start | bytes 786440 | tf_op jit(solution)/shard_map/ppermute | solution.py:157
  49.7 0.7 collective-permute-start.12
  50.5 33.2 %collective-permute-done.14 = bf16[128,1024]{1,0:T(8,128)(2,1)S(1)} collective-permute-done((bf16[128,1024]{1,0:T(8,128)(2,1)S(1)}, bf16[128,1024]{1,0:T(8,128)(2,1)S(1)}, u32[]{:S(2)}, u32[]{:S(2)}) %collective-permute-start.14) | collective-permute-done | bytes 262176 | tf_op jit(solution)/shard_map/ppermute | solution.py:157
  83.6 0.0 collective-permute-done.13
  83.6 0.0 collective-permute-done.12
  83.6 0.8 %broadcast_select_fusion.3 = (bf16[128,1024]{1,0:T(8,128)(2,1)}, bf16[128,1024]{1,0:T(8,128)(2,1)}) fusion(pred[]{:T(512)S(6)} %lt.3, bf16[128,1024]{1,0:T(8,128)(2,1)S(1)} %collective-permute-done.12, bf16[128,1024]{1,0:T(8,128)(2,1)S(1)} %collective-permute-done.13, pred[]{:T(512)S(6)} %or.3, bf16[128,1024]{1,0:T(8,128)(2,1)S(1)} %shard_map.65, ...), kind=kLoop, calls=%fused_computation.4 | loop fusion | flops 524288 | bytes 1572866 | tf_op jit(solution)/shard_map/jit(_where)/select_n | solution.py:271
  (9 shorter events, 0.2 us)
Async XLA Ops:
  1.8 21.8 %collective-permute-start = (bf16[256,1024]{1,0:T(8,128)(2,1)S(1)}, bf16[256,1024]{1,0:T(8,128)(2,1)S(1)}, u32[]{:S(2)}, u32[]{:S(2)}) collective-permute-start(bf16[256,1024]{1,0:T(8,128)(2,1)S(1)} %pad_maximum_fusion), channel_id=1, source_target_pairs={{0,2},{6,4},{1,3},{7,5},{8,10},{14,12},{9,11},{15,13},{16,18},{22,... | collective-permute-start | bytes 1572872 | tf_op jit(solution)/shard_map/ppermute | solution.py:157
  6.6 17.0 %collective-permute-start.1 = (bf16[256,1024]{1,0:T(8,128)(2,1)S(1)}, bf16[256,1024]{1,0:T(8,128)(2,1)S(1)}, u32[]{:S(2)}, u32[]{:S(2)}) collective-permute-start(bf16[256,1024]{1,0:T(8,128)(2,1)S(1)} %pad_maximum_fusion), channel_id=1, source_target_pairs={{2,4},{4,2},{3,5},{5,3},{10,12},{12,10},{11,13},{13,11},{18,20},{2... | collective-permute-start | bytes 1572872 | tf_op jit(solution)/shard_map/ppermute | solution.py:157
  7.3 12.3 %collective-permute-start.2 = (bf16[128,1024]{1,0:T(8,128)(2,1)S(1)}, bf16[128,1024]{1,0:T(8,128)(2,1)S(1)}, u32[]{:S(2)}, u32[]{:S(2)}) collective-permute-start(bf16[128,1024]{1,0:T(8,128)(2,1)S(1)} %get-tuple-element.43.own), channel_id=1, source_target_pairs={{0,4},{6,2},{1,5},{7,3},{8,12},{14,10},{9,13},{15,11},{16,20},{22,... | collective-permute-start | bytes 786440 | tf_op jit(solution)/shard_map/ppermute | solution.py:157
  11.7 11.9 %collective-permute-start.4 = (bf16[128,1024]{1,0:T(8,128)(2,1)S(1)}, bf16[128,1024]{1,0:T(8,128)(2,1)S(1)}, u32[]{:S(2)}, u32[]{:S(2)}) collective-permute-start(bf16[128,1024]{1,0:T(8,128)(2,1)S(1)} %get-tuple-element.42), channel_id=1, source_target_pairs={{8,0},{250,2},{12,4},{254,6},{16,8},{2,10},{20,12},{6,14},{24,16},... | collective-permute-start | bytes 786440 | tf_op jit(solution)/shard_map/ppermute | solution.py:196
  19.0 4.8 %collective-permute-start.3 = (bf16[128,1024]{1,0:T(8,128)(2,1)S(1)}, bf16[128,1024]{1,0:T(8,128)(2,1)S(1)}, u32[]{:S(2)}, u32[]{:S(2)}) collective-permute-start(bf16[128,1024]{1,0:T(8,128)(2,1)S(1)} %get-tuple-element.43.own), channel_id=1, source_target_pairs={{2,3},{3,2},{4,5},{5,4},{10,11},{11,10},{12,13},{13,12},{18,19},{1... | collective-permute-start | bytes 786440 | tf_op jit(solution)/shard_map/ppermute | solution.py:162
  23.7 11.9 %collective-permute-start.5 = (bf16[256,1024]{1,0:T(8,128)(2,1)S(1)}, bf16[256,1024]{1,0:T(8,128)(2,1)S(1)}, u32[]{:S(2)}, u32[]{:S(2)}) collective-permute-start(bf16[256,1024]{1,0:T(8,128)(2,1)S(1)} %get-tuple-element.34.w1), channel_id=1, source_target_pairs={{2,3},{3,2},{4,5},{5,4},{10,11},{11,10},{12,13},{13,12},{18,19},{1... | collective-permute-start | bytes 1572872 | tf_op jit(solution)/shard_map/ppermute | solution.py:162
  25.7 20.4 %collective-permute-start.6 = (bf16[256,1024]{1,0:T(8,128)(2,1)S(1)}, bf16[256,1024]{1,0:T(8,128)(2,1)S(1)}, u32[]{:S(2)}, u32[]{:S(2)}) collective-permute-start(bf16[256,1024]{1,0:T(8,128)(2,1)S(1)} %get-tuple-element.31), channel_id=1, source_target_pairs={{0,4},{6,2},{1,5},{7,3},{8,12},{14,10},{9,13},{15,11},{16,20},{22,... | collective-permute-start | bytes 1572872 | tf_op jit(solution)/shard_map/ppermute | solution.py:157
  34.9 11.2 %collective-permute-start.7 = (bf16[256,1024]{1,0:T(8,128)(2,1)S(1)}, bf16[256,1024]{1,0:T(8,128)(2,1)S(1)}, u32[]{:S(2)}, u32[]{:S(2)}) collective-permute-start(bf16[256,1024]{1,0:T(8,128)(2,1)S(1)} %get-tuple-element.32), channel_id=1, source_target_pairs={{258,252},{250,258},{242,250},{514,508},{506,514},{498,506},{4,764... | collective-permute-start | bytes 1572872 | tf_op jit(solution)/shard_map/ppermute | solution.py:187
  35.6 10.5 %collective-permute-start.8 = (bf16[128,1024]{1,0:T(8,128)(2,1)S(1)}, bf16[128,1024]{1,0:T(8,128)(2,1)S(1)}, u32[]{:S(2)}, u32[]{:S(2)}) collective-permute-start(bf16[128,1024]{1,0:T(8,128)(2,1)S(1)} %collective-permute-done.4.y0), channel_id=1, source_target_pairs={{504,252},{518,2},{760,508},{6,258},{248,764},{262,514},{505,253},... | collective-permute-start | bytes 786440 | tf_op jit(solution)/shard_map/ppermute | solution.py:204
  36.3 9.8 %collective-permute-start.9 = (bf16[128,1024]{1,0:T(8,128)(2,1)S(1)}, bf16[128,1024]{1,0:T(8,128)(2,1)S(1)}, u32[]{:S(2)}, u32[]{:S(2)}) collective-permute-start(bf16[128,1024]{1,0:T(8,128)(2,1)S(1)} %collective-permute-done.4.y0), channel_id=1, source_target_pairs={{508,252},{514,2},{764,508},{2,258},{252,764},{258,514},{509,253},... | collective-permute-start | bytes 786440 | tf_op jit(solution)/shard_map/ppermute | solution.py:204
  37.0 9.2 %collective-permute-start.10 = (bf16[256,1024]{1,0:T(8,128)(2,1)S(1)}, bf16[256,1024]{1,0:T(8,128)(2,1)S(1)}, u32[]{:S(2)}, u32[]{:S(2)}) collective-permute-start(bf16[256,1024]{1,0:T(8,128)(2,1)S(1)} %get-tuple-element.34.w1), channel_id=1, source_target_pairs={{20,12},{2,10},{28,20},{10,18},{36,28},{18,26},{44,36},{26,34},{52... | collective-permute-start | bytes 1572872 | tf_op jit(solution)/shard_map/ppermute | solution.py:178
  46.3 0.8 collective-permute-start.11
  47.1 36.5 %collective-permute-start.14 = (bf16[128,1024]{1,0:T(8,128)(2,1)S(1)}, bf16[128,1024]{1,0:T(8,128)(2,1)S(1)}, u32[]{:S(2)}, u32[]{:S(2)}) collective-permute-start(bf16[128,1024]{1,0:T(8,128)(2,1)S(1)} %shard_map.66), channel_id=1, source_target_pairs={{2,0},{4,6},{3,1},{5,7},{10,8},{12,14},{11,9},{13,15},{18,16},{20,... | collective-permute-start | bytes 786440 | tf_op jit(solution)/shard_map/ppermute | solution.py:157
  48.4 35.2 %collective-permute-start.13 = (bf16[128,1024]{1,0:T(8,128)(2,1)S(1)}, bf16[128,1024]{1,0:T(8,128)(2,1)S(1)}, u32[]{:S(2)}, u32[]{:S(2)}) collective-permute-start(bf16[128,1024]{1,0:T(8,128)(2,1)S(1)} %shard_map.64), channel_id=1, source_target_pairs={{2,6},{4,0},{3,7},{5,1},{10,14},{12,8},{11,15},{13,9},{18,22},{20,... | collective-permute-start | bytes 786440 | tf_op jit(solution)/shard_map/ppermute | solution.py:157
  49.7 33.9 %collective-permute-start.12 = (bf16[128,1024]{1,0:T(8,128)(2,1)S(1)}, bf16[128,1024]{1,0:T(8,128)(2,1)S(1)}, u32[]{:S(2)}, u32[]{:S(2)}) collective-permute-start(bf16[128,1024]{1,0:T(8,128)(2,1)S(1)} %shard_map.63), channel_id=1, source_target_pairs={{2,4},{4,2},{3,5},{5,3},{10,12},{12,10},{11,13},{13,11},{18,20},{2... | collective-permute-start | bytes 786440 | tf_op jit(solution)/shard_map/ppermute | solution.py:157

commit v11 on v9

--- a/solution.py
+++ b/solution.py
@@ -266,6 +266,8 @@
     to_far_end = line(of, [(1, 3), (2, 0)])
     to_end = line(oe, [(1, 0), (2, 3)])
     to_other = line(oo, between)
+    to_end, to_far_end = lax.optimization_barrier((to_end, to_far_end))
+    to_far_end, to_other = lax.optimization_barrier((to_far_end, to_other))
     own_result = jnp.where(inner, om, to_end)
     other_result = jnp.where(inner, to_other, to_far_end)
     return (jnp.where(low, other_result, own_result), jnp.where(low, own_result, other_result))

time: 84.8 us -> 85.1 us (level)
  transfers between devices with their start and end apart: 15 -> 15, of which waited for: 3 -> 4; matrix products, arithmetic and copies ran while one was open for 0% -> 0% of each run, Pallas kernels for 0% -> 0%
where the time goes in v11:
time: 85.1 us; the launch traced here: 84.7 us
  waiting for transfers between devices  45.8 us (54%)
  starting transfers between devices  34.5 us (41%)
  between operations  2.18 us (3%)
  other arithmetic  1.97 us (2%)
    ppermute x7, waiting for transfers between devices, line(): return lax.ppermute(array, 'zl', pairs)  41.8 us
    ppermute x7, starting transfers between devices, line(): return lax.ppermute(array, 'zl', pairs)  22.3 us
    ppermute x1, starting transfers between devices, neighbour_in_group(): return lax.ppermute(array, ('blk', 'zl'), pairs)  7.29 us
    ppermute x1, waiting for transfers between devices, neighbour_in_group(): return lax.ppermute(array, ('blk', 'zl'), pairs)  3.94 us
    ppermute x3, starting transfers between devices, swapped(): return lax.ppermute(array, ('zl', 'core'), pairs)  2.12 us
  transfers between devices with their start and end apart: 15, of which 4 were waited for; matrix products, arithmetic and copies ran while one was open for 0% of the time, Pallas kernels for 0%

profile of v11, /device:TPU:1, one launch (start us, length us, event | category | flops | bytes accessed | tf_op | source)
XLA Modules:
  0.0 84.7 jit_solution(5123372593882650791)
XLA Ops:
  0.6 1.1 %broadcast_select_fusion.2 = (bf16[128,1024]{1,0:T(8,128)(2,1)S(1)}, bf16[128,1024]{1,0:T(8,128)(2,1)S(1)}, bf16[128,1024]{1,0:T(8,128)(2,1)S(1)}) fusion(pred[]{:T(512)S(6)} %or.3, bf16[128,1024]{1,0:T(8,128)(2,1)} %param.4, bf16[128,1024]{1,0:T(8,128)(2,1)} %param.5, pred[]{:T(512)S(6)} %lt.3), kind=kLoop, calls=%fused_computation.3 | loop fusion | flops 393216 | bytes 1310722 | tf_op jit(solution)/shard_map/jit(_where)/select_n | solution.py:220
  1.8 4.9 %collective-permute-start = (bf16[256,1024]{1,0:T(8,128)(2,1)S(1)}, bf16[256,1024]{1,0:T(8,128)(2,1)S(1)}, u32[]{:S(2)}, u32[]{:S(2)}) collective-permute-start(bf16[256,1024]{1,0:T(8,128)(2,1)S(1)} %pad_maximum_fusion), channel_id=1, source_target_pairs={{0,2},{6,4},{1,3},{7,5},{8,10},{14,12},{9,11},{15,13},{16,18},{22,... | collective-permute-start | bytes 1572872 | tf_op jit(solution)/shard_map/ppermute | solution.py:157
  6.6 0.7 collective-permute-start.1
  7.3 4.3 %collective-permute-start.2 = (bf16[128,1024]{1,0:T(8,128)(2,1)S(1)}, bf16[128,1024]{1,0:T(8,128)(2,1)S(1)}, u32[]{:S(2)}, u32[]{:S(2)}) collective-permute-start(bf16[128,1024]{1,0:T(8,128)(2,1)S(1)} %get-tuple-element.49.own), channel_id=1, source_target_pairs={{0,4},{6,2},{1,5},{7,3},{8,12},{14,10},{9,13},{15,11},{16,20},{22,... | collective-permute-start | bytes 786440 | tf_op jit(solution)/shard_map/ppermute | solution.py:157
  11.7 7.3 %collective-permute-start.4 = (bf16[128,1024]{1,0:T(8,128)(2,1)S(1)}, bf16[128,1024]{1,0:T(8,128)(2,1)S(1)}, u32[]{:S(2)}, u32[]{:S(2)}) collective-permute-start(bf16[128,1024]{1,0:T(8,128)(2,1)S(1)} %get-tuple-element.48), channel_id=1, source_target_pairs={{8,0},{250,2},{12,4},{254,6},{16,8},{2,10},{20,12},{6,14},{24,16},... | collective-permute-start | bytes 786440 | tf_op jit(solution)/shard_map/ppermute | solution.py:196
  19.0 0.7 collective-permute-start.3
  19.7 3.9 %collective-permute-done.4.y0 = bf16[128,1024]{1,0:T(8,128)(2,1)S(1)} collective-permute-done((bf16[128,1024]{1,0:T(8,128)(2,1)S(1)}, bf16[128,1024]{1,0:T(8,128)(2,1)S(1)}, u32[]{:S(2)}, u32[]{:S(2)}) %collective-permute-start.4) | collective-permute-done | bytes 262176 | tf_op jit(solution)/shard_map/ppermute | solution.py:196
  23.6 0.0 collective-permute-done.xe
  23.6 0.0 collective-permute-done.1.xo
  23.6 0.1 shard_map.59
  23.7 0.0 collective-permute-done.3.own_far
  23.7 0.7 collective-permute-start.5
  24.4 9.2 %collective-permute-start.6 = (bf16[256,1024]{1,0:T(8,128)(2,1)S(1)}, bf16[256,1024]{1,0:T(8,128)(2,1)S(1)}, u32[]{:S(2)}, u32[]{:S(2)}) collective-permute-start(bf16[256,1024]{1,0:T(8,128)(2,1)S(1)} %get-tuple-element.33), channel_id=1, source_target_pairs={{0,4},{6,2},{1,5},{7,3},{8,12},{14,10},{9,13},{15,11},{16,20},{22,... | collective-permute-start | bytes 1572872 | tf_op jit(solution)/shard_map/ppermute | solution.py:157
  33.6 0.7 collective-permute-start.7
  34.3 0.7 collective-permute-start.10
  35.0 0.7 collective-permute-start.8
  35.7 0.7 collective-permute-start.9
  37.7 0.0 collective-permute-done.8.kb
  37.8 0.0 collective-permute-done.9.ka
  37.8 7.2 %collective-permute-done.6.last = bf16[256,1024]{1,0:T(8,128)(2,1)S(1)} collective-permute-done((bf16[256,1024]{1,0:T(8,128)(2,1)S(1)}, bf16[256,1024]{1,0:T(8,128)(2,1)S(1)}, u32[]{:S(2)}, u32[]{:S(2)}) %collective-permute-start.6) | collective-permute-done | bytes 524320 | tf_op jit(solution)/shard_map/ppermute | solution.py:157
  44.9 0.0 collective-permute-done.7.y2
  44.9 0.0 collective-permute-done.10.y1
  44.9 0.1 shard_map.61.w2
  45.0 0.7 collective-permute-start.11
  45.8 0.0 collective-permute-done.11.w2_far
  45.8 1.3 %collective-permute-start.13 = (bf16[128,1024]{1,0:T(8,128)(2,1)S(1)}, bf16[128,1024]{1,0:T(8,128)(2,1)S(1)}, u32[]{:S(2)}, u32[]{:S(2)}) collective-permute-start(bf16[128,1024]{1,0:T(8,128)(2,1)S(1)} %shard_map.64), channel_id=1, source_target_pairs={{2,6},{4,0},{3,7},{5,1},{10,14},{12,8},{11,15},{13,9},{18,22},{20,... | collective-permute-start | bytes 786440 | tf_op jit(solution)/shard_map/ppermute | solution.py:157
  47.2 1.3 %collective-permute-start.12 = (bf16[128,1024]{1,0:T(8,128)(2,1)S(1)}, bf16[128,1024]{1,0:T(8,128)(2,1)S(1)}, u32[]{:S(2)}, u32[]{:S(2)}) collective-permute-start(bf16[128,1024]{1,0:T(8,128)(2,1)S(1)} %shard_map.63), channel_id=1, source_target_pairs={{2,0},{4,6},{3,1},{5,7},{10,8},{12,14},{11,9},{13,15},{18,16},{20,... | collective-permute-start | bytes 786440 | tf_op jit(solution)/shard_map/ppermute | solution.py:157
  48.5 0.7 collective-permute-start.14
  49.2 28.7 %collective-permute-done.13 = bf16[128,1024]{1,0:T(8,128)(2,1)S(1)} collective-permute-done((bf16[128,1024]{1,0:T(8,128)(2,1)S(1)}, bf16[128,1024]{1,0:T(8,128)(2,1)S(1)}, u32[]{:S(2)}, u32[]{:S(2)}) %collective-permute-start.13) | collective-permute-done | bytes 262176 | tf_op jit(solution)/shard_map/ppermute | solution.py:157
  77.9 6.0 %collective-permute-done.12 = bf16[128,1024]{1,0:T(8,128)(2,1)S(1)} collective-permute-done((bf16[128,1024]{1,0:T(8,128)(2,1)S(1)}, bf16[128,1024]{1,0:T(8,128)(2,1)S(1)}, u32[]{:S(2)}, u32[]{:S(2)}) %collective-permute-start.12) | collective-permute-done | bytes 262176 | tf_op jit(solution)/shard_map/ppermute | solution.py:157
  83.8 0.0 collective-permute-done.14
  83.8 0.8 %broadcast_select_fusion.3 = (bf16[128,1024]{1,0:T(8,128)(2,1)}, bf16[128,1024]{1,0:T(8,128)(2,1)}) fusion(pred[]{:T(512)S(6)} %lt.3, bf16[128,1024]{1,0:T(8,128)(2,1)S(1)} %collective-permute-done.14, bf16[128,1024]{1,0:T(8,128)(2,1)S(1)} %collective-permute-done.13, pred[]{:T(512)S(6)} %or.3, bf16[128,1024]{1,0:T(8,128)(2,1)S(1)} %shard_map.66, ...), kind=kLoop, calls=%fused_computation.4 | loop fusion | flops 524288 | bytes 1572866 | tf_op jit(solution)/shard_map/jit(_where)/select_n | solution.py:273
  (9 shorter events, 0.2 us)
Async XLA Ops:
  1.8 21.8 %collective-permute-start = (bf16[256,1024]{1,0:T(8,128)(2,1)S(1)}, bf16[256,1024]{1,0:T(8,128)(2,1)S(1)}, u32[]{:S(2)}, u32[]{:S(2)}) collective-permute-start(bf16[256,1024]{1,0:T(8,128)(2,1)S(1)} %pad_maximum_fusion), channel_id=1, source_target_pairs={{0,2},{6,4},{1,3},{7,5},{8,10},{14,12},{9,11},{15,13},{16,18},{22,... | collective-permute-start | bytes 1572872 | tf_op jit(solution)/shard_map/ppermute | solution.py:157
  6.6 17.0 %collective-permute-start.1 = (bf16[256,1024]{1,0:T(8,128)(2,1)S(1)}, bf16[256,1024]{1,0:T(8,128)(2,1)S(1)}, u32[]{:S(2)}, u32[]{:S(2)}) collective-permute-start(bf16[256,1024]{1,0:T(8,128)(2,1)S(1)} %pad_maximum_fusion), channel_id=1, source_target_pairs={{2,4},{4,2},{3,5},{5,3},{10,12},{12,10},{11,13},{13,11},{18,20},{2... | collective-permute-start | bytes 1572872 | tf_op jit(solution)/shard_map/ppermute | solution.py:157
  7.3 12.3 %collective-permute-start.2 = (bf16[128,1024]{1,0:T(8,128)(2,1)S(1)}, bf16[128,1024]{1,0:T(8,128)(2,1)S(1)}, u32[]{:S(2)}, u32[]{:S(2)}) collective-permute-start(bf16[128,1024]{1,0:T(8,128)(2,1)S(1)} %get-tuple-element.49.own), channel_id=1, source_target_pairs={{0,4},{6,2},{1,5},{7,3},{8,12},{14,10},{9,13},{15,11},{16,20},{22,... | collective-permute-start | bytes 786440 | tf_op jit(solution)/shard_map/ppermute | solution.py:157
  11.7 11.9 %collective-permute-start.4 = (bf16[128,1024]{1,0:T(8,128)(2,1)S(1)}, bf16[128,1024]{1,0:T(8,128)(2,1)S(1)}, u32[]{:S(2)}, u32[]{:S(2)}) collective-permute-start(bf16[128,1024]{1,0:T(8,128)(2,1)S(1)} %get-tuple-element.48), channel_id=1, source_target_pairs={{8,0},{250,2},{12,4},{254,6},{16,8},{2,10},{20,12},{6,14},{24,16},... | collective-permute-start | bytes 786440 | tf_op jit(solution)/shard_map/ppermute | solution.py:196
  19.0 4.8 %collective-permute-start.3 = (bf16[128,1024]{1,0:T(8,128)(2,1)S(1)}, bf16[128,1024]{1,0:T(8,128)(2,1)S(1)}, u32[]{:S(2)}, u32[]{:S(2)}) collective-permute-start(bf16[128,1024]{1,0:T(8,128)(2,1)S(1)} %get-tuple-element.49.own), channel_id=1, source_target_pairs={{2,3},{3,2},{4,5},{5,4},{10,11},{11,10},{12,13},{13,12},{18,19},{1... | collective-permute-start | bytes 786440 | tf_op jit(solution)/shard_map/ppermute | solution.py:162
  23.7 10.6 %collective-permute-start.5 = (bf16[256,1024]{1,0:T(8,128)(2,1)S(1)}, bf16[256,1024]{1,0:T(8,128)(2,1)S(1)}, u32[]{:S(2)}, u32[]{:S(2)}) collective-permute-start(bf16[256,1024]{1,0:T(8,128)(2,1)S(1)} %get-tuple-element.36.w1), channel_id=1, source_target_pairs={{2,3},{3,2},{4,5},{5,4},{10,11},{11,10},{12,13},{13,12},{18,19},{1... | collective-permute-start | bytes 1572872 | tf_op jit(solution)/shard_map/ppermute | solution.py:162
  24.4 20.5 %collective-permute-start.6 = (bf16[256,1024]{1,0:T(8,128)(2,1)S(1)}, bf16[256,1024]{1,0:T(8,128)(2,1)S(1)}, u32[]{:S(2)}, u32[]{:S(2)}) collective-permute-start(bf16[256,1024]{1,0:T(8,128)(2,1)S(1)} %get-tuple-element.33), channel_id=1, source_target_pairs={{0,4},{6,2},{1,5},{7,3},{8,12},{14,10},{9,13},{15,11},{16,20},{22,... | collective-permute-start | bytes 1572872 | tf_op jit(solution)/shard_map/ppermute | solution.py:157
  33.6 11.3 %collective-permute-start.7 = (bf16[256,1024]{1,0:T(8,128)(2,1)S(1)}, bf16[256,1024]{1,0:T(8,128)(2,1)S(1)}, u32[]{:S(2)}, u32[]{:S(2)}) collective-permute-start(bf16[256,1024]{1,0:T(8,128)(2,1)S(1)} %get-tuple-element.34), channel_id=1, source_target_pairs={{258,252},{250,258},{242,250},{514,508},{506,514},{498,506},{4,764... | collective-permute-start | bytes 1572872 | tf_op jit(solution)/shard_map/ppermute | solution.py:187
  34.3 10.6 %collective-permute-start.10 = (bf16[256,1024]{1,0:T(8,128)(2,1)S(1)}, bf16[256,1024]{1,0:T(8,128)(2,1)S(1)}, u32[]{:S(2)}, u32[]{:S(2)}) collective-permute-start(bf16[256,1024]{1,0:T(8,128)(2,1)S(1)} %get-tuple-element.36.w1), channel_id=1, source_target_pairs={{20,12},{2,10},{28,20},{10,18},{36,28},{18,26},{44,36},{26,34},{52... | collective-permute-start | bytes 1572872 | tf_op jit(solution)/shard_map/ppermute | solution.py:178
  35.0 2.7 %collective-permute-start.8 = (bf16[128,1024]{1,0:T(8,128)(2,1)S(1)}, bf16[128,1024]{1,0:T(8,128)(2,1)S(1)}, u32[]{:S(2)}, u32[]{:S(2)}) collective-permute-start(bf16[128,1024]{1,0:T(8,128)(2,1)S(1)} %collective-permute-done.4.y0), channel_id=1, source_target_pairs={{504,252},{518,2},{760,508},{6,258},{248,764},{262,514},{505,253},... | collective-permute-start | bytes 786440 | tf_op jit(solution)/shard_map/ppermute | solution.py:204
  35.7 2.0 %collective-permute-start.9 = (bf16[128,1024]{1,0:T(8,128)(2,1)S(1)}, bf16[128,1024]{1,0:T(8,128)(2,1)S(1)}, u32[]{:S(2)}, u32[]{:S(2)}) collective-permute-start(bf16[128,1024]{1,0:T(8,128)(2,1)S(1)} %collective-permute-done.4.y0), channel_id=1, source_target_pairs={{508,252},{514,2},{764,508},{2,258},{252,764},{258,514},{509,253},... | collective-permute-start | bytes 786440 | tf_op jit(solution)/shard_map/ppermute | solution.py:204
  45.0 0.8 collective-permute-start.11
  45.8 32.0 %collective-permute-start.13 = (bf16[128,1024]{1,0:T(8,128)(2,1)S(1)}, bf16[128,1024]{1,0:T(8,128)(2,1)S(1)}, u32[]{:S(2)}, u32[]{:S(2)}) collective-permute-start(bf16[128,1024]{1,0:T(8,128)(2,1)S(1)} %shard_map.64), channel_id=1, source_target_pairs={{2,6},{4,0},{3,7},{5,1},{10,14},{12,8},{11,15},{13,9},{18,22},{20,... | collective-permute-start | bytes 786440 | tf_op jit(solution)/shard_map/ppermute | solution.py:157
  47.2 36.7 %collective-permute-start.12 = (bf16[128,1024]{1,0:T(8,128)(2,1)S(1)}, bf16[128,1024]{1,0:T(8,128)(2,1)S(1)}, u32[]{:S(2)}, u32[]{:S(2)}) collective-permute-start(bf16[128,1024]{1,0:T(8,128)(2,1)S(1)} %shard_map.63), channel_id=1, source_target_pairs={{2,0},{4,6},{3,1},{5,7},{10,8},{12,14},{11,9},{13,15},{18,16},{20,... | collective-permute-start | bytes 786440 | tf_op jit(solution)/shard_map/ppermute | solution.py:157
  48.5 35.3 %collective-permute-start.14 = (bf16[128,1024]{1,0:T(8,128)(2,1)S(1)}, bf16[128,1024]{1,0:T(8,128)(2,1)S(1)}, u32[]{:S(2)}, u32[]{:S(2)}) collective-permute-start(bf16[128,1024]{1,0:T(8,128)(2,1)S(1)} %shard_map.65), channel_id=1, source_target_pairs={{2,4},{4,2},{3,5},{5,3},{10,12},{12,10},{11,13},{13,11},{18,20},{2... | collective-permute-start | bytes 786440 | tf_op jit(solution)/shard_map/ppermute | solution.py:157
